TPU v7x, 128 devices: a whole 4x4x4 slice. The times are simulated.
128 devices in a mesh: sec: 32 (over x, y_lo, z), ax: 4 (over y_hi, core).
Axes of the slice: x: 4, y: 4 (y_hi: 2, y_lo: 2; y = y_hi * 2 + y_lo), z: 4, core: 2. Of those that a mesh axis runs over, the one named last changes fastest.
Arguments:
- material_labels: int32 [256, 512, 256], P('ax', 'sec'), may hold values from 0 to 3
- excitation_amplitudes: float32 [2, 256, 512, 256], P(None, 'ax', 'sec'), may hold values from -6 to 6
- opening_magnetic_gauge: float32 [256, 512, 256], P('ax', 'sec'), may hold values from -6 to 6
- prior_warming_excess: float32 [256, 256, 512], P('ax', 'sec'), may hold values from -6 to 6
Outputs:
- closing_magnetic_gauge: float32 [256, 512, 256], P('ax', 'sec')
- dissipation_accumulated: float32 [256, 512, 256], P('ax', 'sec')
- temperature: float32 [256, 256, 512], P('ax', 'sec')
Inputs may be any that keep to these rules, and one draw needn't show every extreme that they name: `material_labels`: 0 iron, 1 copper, 2 air, 3 magnet.
All inputs are finite; a program needn't handle non-finite values.
Results may differ from a plain program's by a relative error of at most 0.00002.
Values sent between devices are 32-bit elements; how exact they have to be, the bound alone decides.
No kernel may reach another device: no remote copies, remote signals or barrier semaphores. Data moves between devices by JAX's collectives and lax.ppermute only.
A program may use at most 128 MiB of HBM per device.

v0:
```python
import jax
import jax.numpy as jnp
from jax import lax
from jax.sharding import PartitionSpec as P

SAMPLES = 16
SWEEPS = 2


electrical_period = 32.0
reluct_table = (0.05, 0.24, 0.24, 0.2)
sigma_table = (0.3, 1.0, 0.0, 0.6)
kappa_table = (1.0, 1.5, 0.1, 0.4)
capacity_table = (3.0, 3.5, 0.5, 3.0)
drive_table = (0.0, 1.0, 0.0, 1.0)


def with_halo(cells, sides, width, closed):
    for axis, dim in sides:
        count = lax.axis_size(axis)
        ends = count if closed else count - 1
        head = lax.slice_in_dim(cells, 0, width, axis=dim)
        tail = lax.slice_in_dim(cells, cells.shape[dim] - width, cells.shape[dim], axis=dim)
        cells = jnp.concatenate(
            [
                lax.ppermute(tail, axis, [(i, (i + 1) % count) for i in range(ends)]),
                cells,
                lax.ppermute(head, axis, [((i + 1) % count, i) for i in range(ends)]),
            ],
            axis=dim,
        )
    return cells


def lookup(material_labels, table):
    result = jnp.zeros(material_labels.shape, jnp.float32)
    for index, value in enumerate(table):
        result = result + jnp.where(material_labels == index, jnp.float32(value), jnp.float32(0.0))
    return result


def advance(
    potential,
    induced_dissipation,
    azimuth_sum,
    reluct,
    sigma,
    driven,
    cosine_part,
    sine_part,
    sample,
):
    padded = jnp.pad(potential, ((0, 0), (0, 0), (1, 1)))
    radial_sum = padded[:, :, 2:] + padded[:, :, :-2]
    phase = 2.0 * jnp.pi / electrical_period * sample.astype(jnp.float32)
    source = driven * (jnp.cos(phase) * cosine_part + jnp.sin(phase) * sine_part)
    fresh = potential + reluct * (azimuth_sum + radial_sum - 4.0 * potential) + source
    change = fresh - potential
    return (fresh, induced_dissipation + sigma * change * change)


def damping_weight(
    warmth_distribution,
    conduction_coupling,
    earlier_iterate,
    specific_warmth_store,
    induced_dissipation,
    adjacent_couples,
):
    energy_stream = jnp.zeros_like(warmth_distribution)
    main_entries = specific_warmth_store
    for adjacent_warmth, other_cond in adjacent_couples:
        boundary_surface = 0.5 * (conduction_coupling + other_cond)
        energy_stream = energy_stream + boundary_surface * (adjacent_warmth - warmth_distribution)
        main_entries = main_entries + boundary_surface
    mismatch_amount = (
        specific_warmth_store * (warmth_distribution - earlier_iterate)
        - energy_stream
        - induced_dissipation
    )
    return warmth_distribution - mismatch_amount / main_entries


def shifted_couples(warmth_distribution, conduction_coupling, dimension_label):
    return [
        (
            jnp.roll(warmth_distribution, 1, dimension_label),
            jnp.roll(conduction_coupling, 1, dimension_label),
        ),
        (
            jnp.roll(warmth_distribution, -1, dimension_label),
            jnp.roll(conduction_coupling, -1, dimension_label),
        ),
    ]


def shards(material_labels, excitation_amplitudes, opening_magnetic_gauge, prior_warming_excess):
    reluct = lookup(material_labels, reluct_table)
    sigma = lookup(material_labels, sigma_table)
    driven = lookup(material_labels, drive_table)
    start_losses = jnp.zeros_like(opening_magnetic_gauge)

    def turn(sample, carry):
        potential, induced_dissipation = carry
        padded = with_halo(potential, (("sec", 1),), 1, True)
        azimuth_sum = padded[:, 2:, :] + padded[:, :-2, :]
        return advance(
            potential,
            induced_dissipation,
            azimuth_sum,
            reluct,
            sigma,
            driven,
            excitation_amplitudes[0],
            excitation_amplitudes[1],
            sample,
        )

    closing_magnetic_gauge, dissipation_accumulated = lax.fori_loop(
        0, SAMPLES, turn, (opening_magnetic_gauge, start_losses)
    )
    conductivity_coefficient = lookup(material_labels, kappa_table)
    specific_warmth_store = lookup(material_labels, capacity_table)
    fields = jnp.stack([dissipation_accumulated, conductivity_coefficient, specific_warmth_store])
    moved = jnp.swapaxes(
        lax.all_to_all(fields, "sec", split_axis=3, concat_axis=2, tiled=True), 2, 3
    )
    induced_dissipation, conductivity_patch, heat_capacity_block = (moved[0], moved[1], moved[2])
    warmth_distribution = prior_warming_excess
    for sweep_index in range(SWEEPS):
        conduction_coupling = conductivity_patch * (1.0 + 0.5 * jnp.tanh(warmth_distribution))
        gathered_arrays = jnp.stack([warmth_distribution, conduction_coupling])
        padded = with_halo(gathered_arrays, (("sec", 2), ("ax", 1)), 1, False)
        below = padded[:, :-2, 1:-1, :]
        above = padded[:, 2:, 1:-1, :]
        inward = padded[:, 1:-1, :-2, :]
        outward = padded[:, 1:-1, 2:, :]
        adjacent_couples = [
            (below[0], below[1]),
            (above[0], above[1]),
            (inward[0], inward[1]),
            (outward[0], outward[1]),
        ]
        adjacent_couples = adjacent_couples + shifted_couples(
            warmth_distribution, conduction_coupling, 2
        )
        warmth_distribution = damping_weight(
            warmth_distribution,
            conduction_coupling,
            prior_warming_excess,
            heat_capacity_block,
            induced_dissipation,
            adjacent_couples,
        )
    return (closing_magnetic_gauge, dissipation_accumulated, warmth_distribution)


def solution(mesh):
    return jax.shard_map(
        shards,
        mesh=mesh,
        in_specs=(
            P("ax", "sec", None),
            P(None, "ax", "sec", None),
            P("ax", "sec", None),
            P("ax", "sec", None),
        ),
        out_specs=(P("ax", "sec", None), P("ax", "sec", None), P("ax", "sec", None)),
        check_vma=False,
    )
```

profile of v0, /device:TPU:3, one launch (start us, length us, event | category | flops | bytes accessed | tf_op | source)
XLA Modules:
  0.0 491.7 jit_solution(17269066476829884182)
XLA Ops:
  7.5 4.8 add_bitcast_fusion
  22.0 196.9 %while.18 = (s32[]{:T(128)}, f32[64,16,256]{2,1,0:T(8,128)}, f32[64,16,256]{2,1,0:T(8,128)}, f32[64,16,256]{2,1,0:T(8,128)S(1)}, f32[2,64,16,256]{3,2,1,0:T(8,12...) while((s32[]{:T(128)}, f32[64,16,256]{2,1,0:T(8,128)}, ...), condition=%wide.region_1.2_spmd.clone, body=%wide.region_0.1_spmd.clone.sunk | while | flops 4980741 | bytes 12452083 | solution.py:119
  41.7 4.7 fusion.102
  54.0 4.7 fusion.102
  66.2 4.7 fusion.102
  90.8 4.7 fusion.102
  115.3 4.7 fusion.102
  127.6 4.7 fusion.102
  223.0 5.3 %fusion.98 = f32[256,3,16,64]{3,2,1,0:T(8,128)} fusion(f32[1,64,16,256]{1,2,0,3:T(8,128)} %get-tuple-element.285, f32[1,64,16,256]{1,2,0,3:T(8,128)S(1)} %copy-done.4, f32[1,64,16,256]{1,2,0,3:T(8,128)} %bitcast.253), kind=kLoop, calls=%fused_computation.163 | loop fusion | flops 1572864 | bytes 6291456
  228.3 7.4 %reshape.11 = f32[32,1,24576]{2,1,0:T(1,128)} reshape(f32[256,3,16,64]{3,2,1,0:T(8,128)} %fusion.98) | data formatting | bytes 6291456
  235.7 28.5 %all-to-all-start = ((f32[32,1,24576]{2,1,0:T(1,128)}), f32[32,1,24576]{2,1,0:T(1,128)}, u32[]{:S(2)}, u32[]{:S(2)}) async-start(f32[32,1,24576]{2,1,0:T(1,128)} %reshape.11), calls=%async_computation | async-start | bytes 6291456 | tf_op jit(solution)/shard_map/all_to_all | solution.py:126
  267.6 19.0 %all-to-all-done = f32[32,1,24576]{2,1,0:T(1,128)} async-done(((f32[32,1,24576]{2,1,0:T(1,128)}), f32[32,1,24576]{2,1,0:T(1,128)}, u32[]{:S(2)}, u32[]{:S(2)}) %all-to-all-start) | async-done | bytes 3145760 | tf_op jit(solution)/shard_map/all_to_all | solution.py:126
  287.1 12.0 %reduce = f32[32,24576]{1,0:T(8,128)} reduce(f32[32,1,24576]{2,1,0:T(1,128)} %all-to-all-done, f32[]{:T(128)} %broadcast.64), dimensions={1}, to_apply=%all_to_all.13.reduce_sub_computation | reduce | bytes 6291460 | tf_op jit(solution)/shard_map/all_to_all | solution.py:126
  299.1 6.6 %reshape.12 = f32[256,3,16,64]{3,2,1,0:T(8,128)} reshape(f32[32,24576]{1,0:T(8,128)} %reduce) | data formatting | bytes 6291456
  305.7 5.8 %copy.110 = f32[3,64,32,16,8]{1,4,3,2,0:T(8,128)S(1)} copy(f32[3,64,32,16,8]{1,3,0,4,2:T(8,128)} %bitcast.252) | data formatting | bytes 6291456 | tf_op jit(solution)/shard_map/all_to_all | solution.py:126
  314.8 5.9 %collective-permute-start.3 = (f32[2,64,1,512]{1,2,3,0:T(1,128)S(1)}, f32[2,64,1,512]{1,2,3,0:T(1,128)S(1)}, u32[]{:S(2)}, u32[]{:S(2)}) collective-permute-start(f32[2,64,1,512]{1,2,3,0:T(1,128)S(1)} %get-tuple-element.268), channel_id=1, source_target_pairs={{4,0},{8,4},{12,8},{16,12},{20,16},{24,20},{28,24},{32,28},{36,32}... | collective-permute-start | bytes 786440 | tf_op jit(solution)/shard_map/ppermute | solution.py:28
  326.9 6.8 %collective-permute-done.2 = f32[2,64,1,512]{1,2,3,0:T(1,128)S(1)} collective-permute-done((f32[2,64,1,512]{1,2,3,0:T(1,128)S(1)}, f32[2,64,1,512]{1,2,3,0:T(1,128)S(1)}, u32[]{:S(2)}, u32[]{:S(2)}) %collective-permute-start.2) | collective-permute-done | bytes 262176 | tf_op jit(solution)/shard_map/ppermute | solution.py:26
  335.8 7.1 %fusion.89 = (f32[2,1,10,512]{1,2,3,0:T(8,128)}, f32[2,1,10,512]{1,2,3,0:T(8,128)}) fusion(f32[2,64,10,512]{1,2,3,0:T(8,128)S(1)} %pad_maximum_fusion.2), kind=kLoop, calls=%fused_computation.154 | loop fusion | bytes 163840 | tf_op jit(solution)/shard_map/slice | solution.py:23
  342.9 5.3 %copy.118 = f32[2,1,10,512]{3,0,2,1:T(2,128)S(1)} copy(f32[2,1,10,512]{1,2,3,0:T(8,128)} %get-tuple-element.264) | data formatting | bytes 81920 | tf_op jit(solution)/shard_map/slice | solution.py:22
  348.1 22.0 %collective-permute-start.5 = (f32[2,1,10,512]{3,0,2,1:T(2,128)S(1)}, f32[2,1,10,512]{3,0,2,1:T(2,128)S(1)}, u32[]{:S(2)}, u32[]{:S(2)}) collective-permute-start(f32[2,1,10,512]{3,0,2,1:T(2,128)S(1)} %copy.118), channel_id=1, source_target_pairs={{1,0},{2,1},{3,2},{5,4},{6,5},{7,6},{9,8},{10,9},{11,10},{13,12},{... | collective-permute-start | bytes 122888 | tf_op jit(solution)/shard_map/ppermute | solution.py:28
  370.1 5.3 %copy.115 = f32[2,1,10,512]{3,0,2,1:T(2,128)S(1)} copy(f32[2,1,10,512]{1,2,3,0:T(8,128)} %get-tuple-element.263) | data formatting | bytes 81920 | tf_op jit(solution)/shard_map/slice | solution.py:23
  380.0 5.3 %copy.119 = f32[2,1,10,512]{1,2,3,0:T(8,128)} copy(f32[2,1,10,512]{3,0,2,1:T(2,128)S(1)} %collective-permute-done.5) | data formatting | bytes 81920 | tf_op jit(solution)/shard_map/ppermute | solution.py:28
  385.2 5.1 %copy.116 = f32[2,1,10,512]{1,2,3,0:T(8,128)} copy(f32[2,1,10,512]{3,0,2,1:T(2,128)S(1)} %collective-permute-done.4) | data formatting | bytes 81920 | tf_op jit(solution)/shard_map/ppermute | solution.py:26
  390.3 17.8 %add_multiply_fusion = (f32[64,8,512]{0,1,2:T(8,128)S(1)}, f32[64,8,512]{0,1,2:T(8,128)S(1)}) fusion(f32[3,64,8,512]{1,2,3,0:T(8,128)} %bitcast.250, f32[64,8,512]{0,1,2:T(8,128)S(1)} %copy.129, f32[64,8,1]{0,1,2:T(8,128)S(1)} %get-tuple-element.282, f32[64,8,511]{0,1,2:T(8,128)} %get-tuple-element.284, f32[64,8,512]{0,1,2:T(8,128)} %copy-done, ...), kind=kLoop, calls=%fused_computation.139 | loop fusion | flops 18874368 | bytes 14237696 | tf_op jit(solution)/shard_map/mul | solution.py:131
  417.6 6.1 %collective-permute-done.7 = f32[2,64,1,512]{1,2,3,0:T(1,128)S(1)} collective-permute-done((f32[2,64,1,512]{1,2,3,0:T(1,128)S(1)}, f32[2,64,1,512]{1,2,3,0:T(1,128)S(1)}, u32[]{:S(2)}, u32[]{:S(2)}) %collective-permute-start.7) | collective-permute-done | bytes 262176 | tf_op jit(solution)/shard_map/ppermute | solution.py:28
  430.5 7.1 %fusion.88 = (f32[2,1,10,512]{1,2,3,0:T(8,128)}, f32[2,1,10,512]{1,2,3,0:T(8,128)}) fusion(f32[2,64,10,512]{1,2,3,0:T(8,128)S(1)} %pad_maximum_fusion.3), kind=kLoop, calls=%fused_computation.153 | loop fusion | bytes 163840 | tf_op jit(solution)/shard_map/slice | solution.py:23
  437.5 5.3 %copy.133 = f32[2,1,10,512]{3,0,2,1:T(2,128)S(1)} copy(f32[2,1,10,512]{1,2,3,0:T(8,128)} %get-tuple-element.262) | data formatting | bytes 81920 | tf_op jit(solution)/shard_map/slice | solution.py:22
  444.7 5.3 %copy.131 = f32[2,1,10,512]{3,0,2,1:T(2,128)S(1)} copy(f32[2,1,10,512]{1,2,3,0:T(8,128)} %get-tuple-element.261) | data formatting | bytes 81920 | tf_op jit(solution)/shard_map/slice | solution.py:23
  450.0 5.1 %collective-permute-start.8 = (f32[2,1,10,512]{3,0,2,1:T(2,128)S(1)}, f32[2,1,10,512]{3,0,2,1:T(2,128)S(1)}, u32[]{:S(2)}, u32[]{:S(2)}) collective-permute-start(f32[2,1,10,512]{3,0,2,1:T(2,128)S(1)} %copy.131), channel_id=1, source_target_pairs={{0,1},{1,2},{2,3},{4,5},{5,6},{6,7},{8,9},{9,10},{10,11},{12,13},{... | collective-permute-start | bytes 122888 | tf_op jit(solution)/shard_map/ppermute | solution.py:26
  455.8 5.3 %copy.134 = f32[2,1,10,512]{1,2,3,0:T(8,128)} copy(f32[2,1,10,512]{3,0,2,1:T(2,128)S(1)} %collective-permute-done.9) | data formatting | bytes 81920 | tf_op jit(solution)/shard_map/ppermute | solution.py:28
  461.2 5.1 %copy.132 = f32[2,1,10,512]{1,2,3,0:T(8,128)} copy(f32[2,1,10,512]{3,0,2,1:T(2,128)S(1)} %collective-permute-done.8) | data formatting | bytes 81920 | tf_op jit(solution)/shard_map/ppermute | solution.py:26
  466.2 21.8 %fusion.18 = f32[64,8,512]{0,1,2:T(8,128)} fusion(f32[64,8,512]{0,1,2:T(8,128)} %copy-done.2, f32[2,64,1,512]{1,2,3,0:T(1,128)S(1)} %collective-permute-done.7, f32[1,64,8,512]{1,2,3,0:T(8,128)} %bitcast.245, f32[1,64,8,512]{1,2,3,0:T(8,128)} %bitcast.248, f32[2,64,1,512]{1,2,3,0:T(1,128)S(1)} %collective-permute-done.6, f32[2,1,10,512]{1,2,3,0:T(8,128)} %copy.134, ...), kind=kLoop, calls=%fused_computation.30 | loop fusion | flops 18087936 | bytes 13189120 | tf_op jit(solution)/shard_map/sub | solution.py:81
  (153 shorter events, 228.9 us)
Async XLA Ops:
  23.3 6.5 %collective-permute-start = (f32[64,1,256]{2,1,0:T(1,128)S(1)}, f32[64,1,256]{2,1,0:T(1,128)S(1)}, u32[]{:S(2)}, u32[]{:S(2)}) collective-permute-start(f32[64,1,256]{2,1,0:T(1,128)S(1)} %get-tuple-element.340), channel_id=1, source_target_pairs={{0,4},{4,8},{8,12},{12,16},{16,20},{20,24},{24,28},{28,32},{32,36}... | collective-permute-start | bytes 196616 | tf_op jit(solution)/shard_map/while/body/eval_jaxpr/ppermute | solution.py:26
  35.4 6.3 %collective-permute-start = (f32[64,1,256]{2,1,0:T(1,128)S(1)}, f32[64,1,256]{2,1,0:T(1,128)S(1)}, u32[]{:S(2)}, u32[]{:S(2)}) collective-permute-start(f32[64,1,256]{2,1,0:T(1,128)S(1)} %get-tuple-element.340), channel_id=1, source_target_pairs={{0,4},{4,8},{8,12},{12,16},{16,20},{20,24},{24,28},{28,32},{32,36}... | collective-permute-start | bytes 196616 | tf_op jit(solution)/shard_map/while/body/eval_jaxpr/ppermute | solution.py:26
  35.5 6.2 %collective-permute-start.1 = (f32[64,1,256]{2,1,0:T(1,128)S(1)}, f32[64,1,256]{2,1,0:T(1,128)S(1)}, u32[]{:S(2)}, u32[]{:S(2)}) collective-permute-start(f32[64,1,256]{2,1,0:T(1,128)S(1)} %get-tuple-element.341), channel_id=1, source_target_pairs={{4,0},{8,4},{12,8},{16,12},{20,16},{24,20},{28,24},{32,28},{36,32}... | collective-permute-start | bytes 196616 | tf_op jit(solution)/shard_map/while/body/eval_jaxpr/ppermute | solution.py:28
  47.7 6.3 %collective-permute-start = (f32[64,1,256]{2,1,0:T(1,128)S(1)}, f32[64,1,256]{2,1,0:T(1,128)S(1)}, u32[]{:S(2)}, u32[]{:S(2)}) collective-permute-start(f32[64,1,256]{2,1,0:T(1,128)S(1)} %get-tuple-element.340), channel_id=1, source_target_pairs={{0,4},{4,8},{8,12},{12,16},{16,20},{20,24},{24,28},{28,32},{32,36}... | collective-permute-start | bytes 196616 | tf_op jit(solution)/shard_map/while/body/eval_jaxpr/ppermute | solution.py:26
  47.8 6.2 %collective-permute-start.1 = (f32[64,1,256]{2,1,0:T(1,128)S(1)}, f32[64,1,256]{2,1,0:T(1,128)S(1)}, u32[]{:S(2)}, u32[]{:S(2)}) collective-permute-start(f32[64,1,256]{2,1,0:T(1,128)S(1)} %get-tuple-element.341), channel_id=1, source_target_pairs={{4,0},{8,4},{12,8},{16,12},{20,16},{24,20},{28,24},{32,28},{36,32}... | collective-permute-start | bytes 196616 | tf_op jit(solution)/shard_map/while/body/eval_jaxpr/ppermute | solution.py:28
  60.0 6.3 %collective-permute-start = (f32[64,1,256]{2,1,0:T(1,128)S(1)}, f32[64,1,256]{2,1,0:T(1,128)S(1)}, u32[]{:S(2)}, u32[]{:S(2)}) collective-permute-start(f32[64,1,256]{2,1,0:T(1,128)S(1)} %get-tuple-element.340), channel_id=1, source_target_pairs={{0,4},{4,8},{8,12},{12,16},{16,20},{20,24},{24,28},{28,32},{32,36}... | collective-permute-start | bytes 196616 | tf_op jit(solution)/shard_map/while/body/eval_jaxpr/ppermute | solution.py:26
  60.0 6.2 %collective-permute-start.1 = (f32[64,1,256]{2,1,0:T(1,128)S(1)}, f32[64,1,256]{2,1,0:T(1,128)S(1)}, u32[]{:S(2)}, u32[]{:S(2)}) collective-permute-start(f32[64,1,256]{2,1,0:T(1,128)S(1)} %get-tuple-element.341), channel_id=1, source_target_pairs={{4,0},{8,4},{12,8},{16,12},{20,16},{24,20},{28,24},{32,28},{36,32}... | collective-permute-start | bytes 196616 | tf_op jit(solution)/shard_map/while/body/eval_jaxpr/ppermute | solution.py:28
  72.2 6.3 %collective-permute-start = (f32[64,1,256]{2,1,0:T(1,128)S(1)}, f32[64,1,256]{2,1,0:T(1,128)S(1)}, u32[]{:S(2)}, u32[]{:S(2)}) collective-permute-start(f32[64,1,256]{2,1,0:T(1,128)S(1)} %get-tuple-element.340), channel_id=1, source_target_pairs={{0,4},{4,8},{8,12},{12,16},{16,20},{20,24},{24,28},{28,32},{32,36}... | collective-permute-start | bytes 196616 | tf_op jit(solution)/shard_map/while/body/eval_jaxpr/ppermute | solution.py:26
  72.3 6.2 %collective-permute-start.1 = (f32[64,1,256]{2,1,0:T(1,128)S(1)}, f32[64,1,256]{2,1,0:T(1,128)S(1)}, u32[]{:S(2)}, u32[]{:S(2)}) collective-permute-start(f32[64,1,256]{2,1,0:T(1,128)S(1)} %get-tuple-element.341), channel_id=1, source_target_pairs={{4,0},{8,4},{12,8},{16,12},{20,16},{24,20},{28,24},{32,28},{36,32}... | collective-permute-start | bytes 196616 | tf_op jit(solution)/shard_map/while/body/eval_jaxpr/ppermute | solution.py:28
  84.5 6.3 %collective-permute-start = (f32[64,1,256]{2,1,0:T(1,128)S(1)}, f32[64,1,256]{2,1,0:T(1,128)S(1)}, u32[]{:S(2)}, u32[]{:S(2)}) collective-permute-start(f32[64,1,256]{2,1,0:T(1,128)S(1)} %get-tuple-element.340), channel_id=1, source_target_pairs={{0,4},{4,8},{8,12},{12,16},{16,20},{20,24},{24,28},{28,32},{32,36}... | collective-permute-start | bytes 196616 | tf_op jit(solution)/shard_map/while/body/eval_jaxpr/ppermute | solution.py:26
  84.6 6.2 %collective-permute-start.1 = (f32[64,1,256]{2,1,0:T(1,128)S(1)}, f32[64,1,256]{2,1,0:T(1,128)S(1)}, u32[]{:S(2)}, u32[]{:S(2)}) collective-permute-start(f32[64,1,256]{2,1,0:T(1,128)S(1)} %get-tuple-element.341), channel_id=1, source_target_pairs={{4,0},{8,4},{12,8},{16,12},{20,16},{24,20},{28,24},{32,28},{36,32}... | collective-permute-start | bytes 196616 | tf_op jit(solution)/shard_map/while/body/eval_jaxpr/ppermute | solution.py:28
  96.8 6.3 %collective-permute-start = (f32[64,1,256]{2,1,0:T(1,128)S(1)}, f32[64,1,256]{2,1,0:T(1,128)S(1)}, u32[]{:S(2)}, u32[]{:S(2)}) collective-permute-start(f32[64,1,256]{2,1,0:T(1,128)S(1)} %get-tuple-element.340), channel_id=1, source_target_pairs={{0,4},{4,8},{8,12},{12,16},{16,20},{20,24},{24,28},{28,32},{32,36}... | collective-permute-start | bytes 196616 | tf_op jit(solution)/shard_map/while/body/eval_jaxpr/ppermute | solution.py:26
  96.8 6.2 %collective-permute-start.1 = (f32[64,1,256]{2,1,0:T(1,128)S(1)}, f32[64,1,256]{2,1,0:T(1,128)S(1)}, u32[]{:S(2)}, u32[]{:S(2)}) collective-permute-start(f32[64,1,256]{2,1,0:T(1,128)S(1)} %get-tuple-element.341), channel_id=1, source_target_pairs={{4,0},{8,4},{12,8},{16,12},{20,16},{24,20},{28,24},{32,28},{36,32}... | collective-permute-start | bytes 196616 | tf_op jit(solution)/shard_map/while/body/eval_jaxpr/ppermute | solution.py:28
  109.0 6.3 %collective-permute-start = (f32[64,1,256]{2,1,0:T(1,128)S(1)}, f32[64,1,256]{2,1,0:T(1,128)S(1)}, u32[]{:S(2)}, u32[]{:S(2)}) collective-permute-start(f32[64,1,256]{2,1,0:T(1,128)S(1)} %get-tuple-element.340), channel_id=1, source_target_pairs={{0,4},{4,8},{8,12},{12,16},{16,20},{20,24},{24,28},{28,32},{32,36}... | collective-permute-start | bytes 196616 | tf_op jit(solution)/shard_map/while/body/eval_jaxpr/ppermute | solution.py:26
  121.3 6.3 %collective-permute-start = (f32[64,1,256]{2,1,0:T(1,128)S(1)}, f32[64,1,256]{2,1,0:T(1,128)S(1)}, u32[]{:S(2)}, u32[]{:S(2)}) collective-permute-start(f32[64,1,256]{2,1,0:T(1,128)S(1)} %get-tuple-element.340), channel_id=1, source_target_pairs={{0,4},{4,8},{8,12},{12,16},{16,20},{20,24},{24,28},{28,32},{32,36}... | collective-permute-start | bytes 196616 | tf_op jit(solution)/shard_map/while/body/eval_jaxpr/ppermute | solution.py:26
  133.6 6.3 %collective-permute-start = (f32[64,1,256]{2,1,0:T(1,128)S(1)}, f32[64,1,256]{2,1,0:T(1,128)S(1)}, u32[]{:S(2)}, u32[]{:S(2)}) collective-permute-start(f32[64,1,256]{2,1,0:T(1,128)S(1)} %get-tuple-element.340), channel_id=1, source_target_pairs={{0,4},{4,8},{8,12},{12,16},{16,20},{20,24},{24,28},{28,32},{32,36}... | collective-permute-start | bytes 196616 | tf_op jit(solution)/shard_map/while/body/eval_jaxpr/ppermute | solution.py:26
  145.8 6.3 %collective-permute-start = (f32[64,1,256]{2,1,0:T(1,128)S(1)}, f32[64,1,256]{2,1,0:T(1,128)S(1)}, u32[]{:S(2)}, u32[]{:S(2)}) collective-permute-start(f32[64,1,256]{2,1,0:T(1,128)S(1)} %get-tuple-element.340), channel_id=1, source_target_pairs={{0,4},{4,8},{8,12},{12,16},{16,20},{20,24},{24,28},{28,32},{32,36}... | collective-permute-start | bytes 196616 | tf_op jit(solution)/shard_map/while/body/eval_jaxpr/ppermute | solution.py:26
  158.1 7.2 %collective-permute-start = (f32[64,1,256]{2,1,0:T(1,128)S(1)}, f32[64,1,256]{2,1,0:T(1,128)S(1)}, u32[]{:S(2)}, u32[]{:S(2)}) collective-permute-start(f32[64,1,256]{2,1,0:T(1,128)S(1)} %get-tuple-element.340), channel_id=1, source_target_pairs={{0,4},{4,8},{8,12},{12,16},{16,20},{20,24},{24,28},{28,32},{32,36}... | collective-permute-start | bytes 196616 | tf_op jit(solution)/shard_map/while/body/eval_jaxpr/ppermute | solution.py:26
  158.2 7.1 %collective-permute-start.1 = (f32[64,1,256]{2,1,0:T(1,128)S(1)}, f32[64,1,256]{2,1,0:T(1,128)S(1)}, u32[]{:S(2)}, u32[]{:S(2)}) collective-permute-start(f32[64,1,256]{2,1,0:T(1,128)S(1)} %get-tuple-element.341), channel_id=1, source_target_pairs={{4,0},{8,4},{12,8},{16,12},{20,16},{24,20},{28,24},{32,28},{36,32}... | collective-permute-start | bytes 196616 | tf_op jit(solution)/shard_map/while/body/eval_jaxpr/ppermute | solution.py:28
  171.3 6.2 %collective-permute-start = (f32[64,1,256]{2,1,0:T(1,128)S(1)}, f32[64,1,256]{2,1,0:T(1,128)S(1)}, u32[]{:S(2)}, u32[]{:S(2)}) collective-permute-start(f32[64,1,256]{2,1,0:T(1,128)S(1)} %get-tuple-element.340), channel_id=1, source_target_pairs={{0,4},{4,8},{8,12},{12,16},{16,20},{20,24},{24,28},{28,32},{32,36}... | collective-permute-start | bytes 196616 | tf_op jit(solution)/shard_map/while/body/eval_jaxpr/ppermute | solution.py:26
  183.5 6.2 %collective-permute-start = (f32[64,1,256]{2,1,0:T(1,128)S(1)}, f32[64,1,256]{2,1,0:T(1,128)S(1)}, u32[]{:S(2)}, u32[]{:S(2)}) collective-permute-start(f32[64,1,256]{2,1,0:T(1,128)S(1)} %get-tuple-element.340), channel_id=1, source_target_pairs={{0,4},{4,8},{8,12},{12,16},{16,20},{20,24},{24,28},{28,32},{32,36}... | collective-permute-start | bytes 196616 | tf_op jit(solution)/shard_map/while/body/eval_jaxpr/ppermute | solution.py:26
  195.7 6.3 %collective-permute-start = (f32[64,1,256]{2,1,0:T(1,128)S(1)}, f32[64,1,256]{2,1,0:T(1,128)S(1)}, u32[]{:S(2)}, u32[]{:S(2)}) collective-permute-start(f32[64,1,256]{2,1,0:T(1,128)S(1)} %get-tuple-element.340), channel_id=1, source_target_pairs={{0,4},{4,8},{8,12},{12,16},{16,20},{20,24},{24,28},{28,32},{32,36}... | collective-permute-start | bytes 196616 | tf_op jit(solution)/shard_map/while/body/eval_jaxpr/ppermute | solution.py:26
  207.9 6.3 %collective-permute-start = (f32[64,1,256]{2,1,0:T(1,128)S(1)}, f32[64,1,256]{2,1,0:T(1,128)S(1)}, u32[]{:S(2)}, u32[]{:S(2)}) collective-permute-start(f32[64,1,256]{2,1,0:T(1,128)S(1)} %get-tuple-element.340), channel_id=1, source_target_pairs={{0,4},{4,8},{8,12},{12,16},{16,20},{20,24},{24,28},{28,32},{32,36}... | collective-permute-start | bytes 196616 | tf_op jit(solution)/shard_map/while/body/eval_jaxpr/ppermute | solution.py:26
  235.7 50.9 %all-to-all-start = ((f32[32,1,24576]{2,1,0:T(1,128)}), f32[32,1,24576]{2,1,0:T(1,128)}, u32[]{:S(2)}, u32[]{:S(2)}) async-start(f32[32,1,24576]{2,1,0:T(1,128)} %reshape.11), calls=%async_computation | async-start | bytes 6291456 | tf_op jit(solution)/shard_map/all_to_all | solution.py:126
  314.8 12.0 %collective-permute-start.3 = (f32[2,64,1,512]{1,2,3,0:T(1,128)S(1)}, f32[2,64,1,512]{1,2,3,0:T(1,128)S(1)}, u32[]{:S(2)}, u32[]{:S(2)}) collective-permute-start(f32[2,64,1,512]{1,2,3,0:T(1,128)S(1)} %get-tuple-element.268), channel_id=1, source_target_pairs={{4,0},{8,4},{12,8},{16,12},{20,16},{24,20},{28,24},{32,28},{36,32}... | collective-permute-start | bytes 786440 | tf_op jit(solution)/shard_map/ppermute | solution.py:28
  320.8 12.9 %collective-permute-start.2 = (f32[2,64,1,512]{1,2,3,0:T(1,128)S(1)}, f32[2,64,1,512]{1,2,3,0:T(1,128)S(1)}, u32[]{:S(2)}, u32[]{:S(2)}) collective-permute-start(f32[2,64,1,512]{1,2,3,0:T(1,128)S(1)} %get-tuple-element.267), channel_id=1, source_target_pairs={{0,4},{4,8},{8,12},{12,16},{16,20},{20,24},{24,28},{28,32},{32,36}... | collective-permute-start | bytes 786440 | tf_op jit(solution)/shard_map/ppermute | solution.py:26
  348.1 31.8 %collective-permute-start.5 = (f32[2,1,10,512]{3,0,2,1:T(2,128)S(1)}, f32[2,1,10,512]{3,0,2,1:T(2,128)S(1)}, u32[]{:S(2)}, u32[]{:S(2)}) collective-permute-start(f32[2,1,10,512]{3,0,2,1:T(2,128)S(1)} %copy.118), channel_id=1, source_target_pairs={{1,0},{2,1},{3,2},{5,4},{6,5},{7,6},{9,8},{10,9},{11,10},{13,12},{... | collective-permute-start | bytes 122888 | tf_op jit(solution)/shard_map/ppermute | solution.py:28
  375.4 9.9 %collective-permute-start.4 = (f32[2,1,10,512]{3,0,2,1:T(2,128)S(1)}, f32[2,1,10,512]{3,0,2,1:T(2,128)S(1)}, u32[]{:S(2)}, u32[]{:S(2)}) collective-permute-start(f32[2,1,10,512]{3,0,2,1:T(2,128)S(1)} %copy.115), channel_id=1, source_target_pairs={{0,1},{1,2},{2,3},{4,5},{5,6},{6,7},{8,9},{9,10},{10,11},{12,13},{... | collective-permute-start | bytes 122888 | tf_op jit(solution)/shard_map/ppermute | solution.py:26
  408.9 14.8 %collective-permute-start.7 = (f32[2,64,1,512]{1,2,3,0:T(1,128)S(1)}, f32[2,64,1,512]{1,2,3,0:T(1,128)S(1)}, u32[]{:S(2)}, u32[]{:S(2)}) collective-permute-start(f32[2,64,1,512]{1,2,3,0:T(1,128)S(1)} %get-tuple-element.266), channel_id=1, source_target_pairs={{4,0},{8,4},{12,8},{16,12},{20,16},{24,20},{28,24},{32,28},{36,32}... | collective-permute-start | bytes 786440 | tf_op jit(solution)/shard_map/ppermute | solution.py:28
  410.8 17.5 %collective-permute-start.6 = (f32[2,64,1,512]{1,2,3,0:T(1,128)S(1)}, f32[2,64,1,512]{1,2,3,0:T(1,128)S(1)}, u32[]{:S(2)}, u32[]{:S(2)}) collective-permute-start(f32[2,64,1,512]{1,2,3,0:T(1,128)S(1)} %get-tuple-element.265), channel_id=1, source_target_pairs={{0,4},{4,8},{8,12},{12,16},{16,20},{20,24},{24,28},{28,32},{32,36}... | collective-permute-start | bytes 786440 | tf_op jit(solution)/shard_map/ppermute | solution.py:26
  442.8 13.0 %collective-permute-start.9 = (f32[2,1,10,512]{3,0,2,1:T(2,128)S(1)}, f32[2,1,10,512]{3,0,2,1:T(2,128)S(1)}, u32[]{:S(2)}, u32[]{:S(2)}) collective-permute-start(f32[2,1,10,512]{3,0,2,1:T(2,128)S(1)} %copy.133), channel_id=1, source_target_pairs={{1,0},{2,1},{3,2},{5,4},{6,5},{7,6},{9,8},{10,9},{11,10},{13,12},{... | collective-permute-start | bytes 122888 | tf_op jit(solution)/shard_map/ppermute | solution.py:28
  450.0 11.2 %collective-permute-start.8 = (f32[2,1,10,512]{3,0,2,1:T(2,128)S(1)}, f32[2,1,10,512]{3,0,2,1:T(2,128)S(1)}, u32[]{:S(2)}, u32[]{:S(2)}) collective-permute-start(f32[2,1,10,512]{3,0,2,1:T(2,128)S(1)} %copy.131), channel_id=1, source_target_pairs={{0,1},{1,2},{2,3},{4,5},{5,6},{6,7},{8,9},{9,10},{10,11},{12,13},{... | collective-permute-start | bytes 122888 | tf_op jit(solution)/shard_map/ppermute | solution.py:26
  (16 other events, 151.7 us)
where the time goes:
time: 497 us; the launch traced here: 492 us
  starting transfers between devices  150 us (30%)
  other arithmetic  145 us (29%)
  local copies, waits for them, and re-layouts  131 us (26%)
  waiting for transfers between devices  62.2 us (13%)
    ppermute x20, starting transfers between devices, with_halo(): lax.ppermute(head, axis, [((i + 1) % count, i) for i in range(ends)])  104 us
    add x16, other arithmetic, advance(): return (fresh, induced_dissipation + sigma * change * change)  74.4 us
    ppermute x20, waiting for transfers between devices, with_halo(): lax.ppermute(tail, axis, [(i, (i + 1) % count) for i in range(ends)])  35.1 us
    unnamed x23, local copies, waits for them, and re-layouts  34.4 us
    all_to_all x1, starting transfers between devices, shards(): lax.all_to_all(fields, 'sec', split_axis=3, concat_axis=2, tiled=True)  28.5 us
    slice x4, local copies, waits for them, and re-layouts, with_halo(): lax.slice_in_dim(cells, cells.shape[dim] - width, cells.shape[dim], axis=...  24.7 us
    sub x1, other arithmetic, damping_weight(): return warmth_distribution - mismatch_amount / main_entries  21.8 us
    while x16, local copies, waits for them, and re-layouts  19.6 us
  transfers between devices with their start and end apart: 41, of which 21 were waited for; matrix products, arithmetic and copies ran while one was open for 6% of the time, Pallas kernels for 0%

commit v1 on v0

v1 whole, which is shorter than its diff:
```python
import functools
import math

import jax
import jax.numpy as jnp
from jax import lax
from jax.experimental import pallas as pl
from jax.experimental.pallas import tpu as pltpu
from jax.sharding import PartitionSpec as P

SAMPLES = 16
PERIOD = 32
WIDTHS = (4, 4, 4, 4)
KMAX = max(WIDTHS)
CH = KMAX - 1

F32 = jnp.float32
AX, AZ, RAD, ANG = 64, 16, 256, 512
SEC = 32
RL = RAD // SEC
G = 8
NG = AX // G
REGION = 16


def _params(mib=None):
    return pltpu.CompilerParams(vmem_limit_bytes=(mib or 24) * 2**20)


def _sds(*shape):
    return jax.ShapeDtypeStruct(shape, F32)


def _reluct(lab):
    return jnp.where(lab == 0, 0.05, jnp.where(lab == 3, 0.2, 0.24)).astype(F32)


def _sigma(lab):
    return jnp.where(lab == 0, 0.3, jnp.where(lab == 1, 1.0, jnp.where(lab == 2, 0.0, 0.6))).astype(F32)


def _driven(lab, x):
    return jnp.where((lab == 1) | (lab == 3), x, 0.0)


def _edges_kernel(lab_ref, exc_ref, a_ref, low_ref, high_ref):
    lab = jnp.swapaxes(lab_ref[...], 0, 1)
    c = jnp.swapaxes(exc_ref[0], 0, 1)
    s = jnp.swapaxes(exc_ref[1], 0, 1)
    a = jnp.swapaxes(a_ref[...], 0, 1)
    w = WIDTHS[0]
    for out, ra, rc in ((low_ref, 0, 0), (high_ref, AZ - w, AZ - CH)):
        out[0:w] = a[ra : ra + w]
        lb = lab[rc : rc + CH]
        out[w : w + CH] = _reluct(lb)
        out[w + CH : w + 2 * CH] = _driven(lb, c[rc : rc + CH])
        out[w + 2 * CH : w + 3 * CH] = _driven(lb, s[rc : rc + CH])


def _edges(labels, exc, a):
    n = WIDTHS[0] + 3 * CH
    nat = pl.BlockSpec((G, AZ, RAD), lambda i: (i, 0, 0))
    out = pl.BlockSpec((n, G, RAD), lambda i: (0, i, 0))
    return pl.pallas_call(
        _edges_kernel,
        grid=(NG,),
        in_specs=[nat, pl.BlockSpec((2, G, AZ, RAD), lambda i: (0, i, 0, 0)), nat],
        out_specs=[out, out],
        out_shape=[_sds(n, AX, RAD)] * 2,
        compiler_params=_params(),
        name="edge_layers",
    )(labels, exc, a)


def _prepare_kernel(lab_ref, exc_ref, a_ref, a_out, nu_out, oc_out, os_out, lt_out):
    lab = lab_ref[...]
    lt_out[...] = jnp.transpose(lab.astype(F32).reshape(G * AZ, RAD)).reshape(SEC, 1, RL, G * AZ)
    lab = jnp.swapaxes(lab, 0, 1)
    a_out[...] = jnp.swapaxes(a_ref[...], 0, 1)
    nu_out[...] = _reluct(lab)
    oc_out[...] = _driven(lab, jnp.swapaxes(exc_ref[0], 0, 1))
    os_out[...] = _driven(lab, jnp.swapaxes(exc_ref[1], 0, 1))


def _prepare(labels, exc, a):
    nat = pl.BlockSpec((G, AZ, RAD), lambda i: (i, 0, 0))
    tr = pl.BlockSpec((AZ, G, RAD), lambda i: (0, i, 0))
    return pl.pallas_call(
        _prepare_kernel,
        grid=(NG,),
        in_specs=[nat, pl.BlockSpec((2, G, AZ, RAD), lambda i: (0, i, 0, 0)), nat],
        out_specs=[tr] * 4 + [pl.BlockSpec((SEC, 1, RL, G * AZ), lambda i: (0, i, 0, 0))],
        out_shape=[_sds(AZ, AX, RAD)] * 4 + [_sds(SEC, NG, RL, G * AZ)],
        compiler_params=_params(),
        name="prepare",
    )(labels, exc, a)


def _advance(first, width, a_rows, nu_of, oc_of, os_of, q_ref, bufs, fresh_q):
    half = RAD // 2
    lane = lax.broadcasted_iota(jnp.int32, (G, half), 1)
    at_low, at_high = lane == 0, lane == half - 1

    def get(t, r):
        return a_rows(r) if t == 0 else bufs[(t - 1) % 2, r + KMAX]

    for t in range(width):
        phase = 2.0 * math.pi / PERIOD * (first + t)
        cc, ss = math.cos(phase), math.sin(phase)
        lo, hi = -width + 1 + t, AZ - 1 + width - 1 - t
        down, mid = get(t, lo - 1), get(t, lo)
        for r in range(lo, hi + 1):
            up = get(t, r + 1)
            m0, m1 = mid[:, :half], mid[:, half:]
            f0, f1 = pltpu.roll(m0, 1, 1), pltpu.roll(m1, 1, 1)
            b0, b1 = pltpu.roll(m0, half - 1, 1), pltpu.roll(m1, half - 1, 1)
            side0 = jnp.where(at_low, 0.0, f0) + jnp.where(at_high, b1, b0)
            side1 = jnp.where(at_low, f0, f1) + jnp.where(at_high, 0.0, b1)
            side = jnp.concatenate([side0, side1], axis=1)
            source = cc * oc_of(r) if ss == 0.0 else cc * oc_of(r) + ss * os_of(r)
            change = nu_of(r) * ((down + up) + side - 4.0 * mid) + source
            new = mid + change
            if 0 <= r < AZ:
                sq = change * change
                q_ref[r] = sq if (fresh_q and t == 0) else q_ref[r] + sq
            bufs[t % 2, r + KMAX] = new
            down, mid = mid, up


def _phase_kernel(first, width, nextw, last, *refs):
    refs = list(refs)
    a_ref, low_ref, high_ref, nu_ref, oc_ref, os_ref, clow_ref, chigh_ref = refs[:8]
    refs = refs[8:]
    fresh = first == 0
    q_in = None if fresh else refs.pop(0)
    if last:
        lab_ref, a_out, d_out, dt_out, bufs, q = refs
    else:
        a_out, q, e_low, e_high, bufs = refs
    if not fresh:
        q[...] = q_in[...]
    w0 = WIDTHS[0]

    def rows(r):
        if r < 0:
            return low_ref[width + r]
        if r >= AZ:
            return high_ref[r - AZ]
        return a_ref[r]

    def const(ref, k):
        def get(r):
            if r < 0:
                return clow_ref[w0 + k * CH + CH + r]
            if r >= AZ:
                return chigh_ref[w0 + k * CH + r - AZ]
            return ref[r]

        return get

    _advance(first, width, rows, const(nu_ref, 0), const(oc_ref, 1), const(os_ref, 2), q, bufs, fresh)
    end = (width - 1) % 2
    a = bufs[end, KMAX : KMAX + AZ]
    if last:
        a_out[...] = jnp.swapaxes(a, 0, 1)
        d = _sigma(lab_ref[...]) * jnp.swapaxes(q[...], 0, 1)
        d_out[...] = d
        dt_out[...] = jnp.transpose(d.reshape(G * AZ, RAD)).reshape(SEC, 1, RL, G * AZ)
    else:
        a_out[...] = a
        e_low[...] = a[0:nextw]
        e_high[...] = a[AZ - nextw :]


def _phase(index, a, low, high, nu, oc, os, clow, chigh, q, labels):
    first, width = sum(WIDTHS[:index]), WIDTHS[index]
    last = index == len(WIDTHS) - 1
    nextw = None if last else WIDTHS[index + 1]

    def tr(x):
        return pl.BlockSpec((x.shape[0], G, RAD), lambda i: (0, i, 0))

    ins = [a, low, high, nu, oc, os, clow, chigh] + ([] if index == 0 else [q])
    specs = [tr(x) for x in ins]
    nat = pl.BlockSpec((G, AZ, RAD), lambda i: (i, 0, 0))
    scratch = [pltpu.VMEM((2, AZ + 2 * KMAX, G, RAD), F32)]
    if last:
        ins.append(labels)
        specs.append(nat)
        outs = [_sds(AX, AZ, RAD), _sds(AX, AZ, RAD), _sds(SEC, NG, RL, G * AZ)]
        out_specs = [nat, nat, pl.BlockSpec((SEC, 1, RL, G * AZ), lambda i: (0, i, 0, 0))]
        scratch.append(pltpu.VMEM((AZ, G, RAD), F32))
    else:
        outs = [_sds(AZ, AX, RAD), _sds(AZ, AX, RAD), _sds(nextw, AX, RAD), _sds(nextw, AX, RAD)]
        out_specs = [tr(x) for x in outs]
    return pl.pallas_call(
        functools.partial(_phase_kernel, first, width, nextw, last),
        grid=(NG,),
        in_specs=specs,
        out_specs=out_specs,
        out_shape=outs,
        scratch_shapes=scratch,
        compiler_params=_params(),
        name=f"field_{index}",
    )(*ins)


def _gathered(x_ref):
    blk = lax.broadcasted_iota(jnp.int32, (RL, 128), 1) // REGION
    tiles = []
    for s in range(SEC // 8):
        x = [x_ref[s * 8 + j, 0] for j in range(8)]
        for b in (4, 2, 1):
            keep = (blk & b) == 0
            for j in range(8):
                if j & b == 0:
                    p, q = x[j], x[j + b]
                    x[j] = jnp.where(keep, p, pltpu.roll(q, b * REGION, 1))
                    x[j + b] = jnp.where(keep, pltpu.roll(p, 128 - b * REGION, 1), q)
        tiles.append(x)
    return [jnp.concatenate([t[q] for t in tiles], axis=1) for q in range(8)]


def _half_cond(lab, temp):
    k0 = jnp.where(lab == 0.0, 1.0, jnp.where(lab == 1.0, 1.5, jnp.where(lab == 2.0, 0.1, 0.4)))
    return (0.5 * k0) * (1.0 + 0.5 * jnp.tanh(temp))


def _capacity(lab):
    return jnp.where(lab == 1.0, 3.5, jnp.where(lab == 2.0, 0.5, 3.0)).astype(F32)


def _materials_kernel(x_ref, temp_ref, lab_out, h_out, in_out, out_out):
    planes = _gathered(x_ref)
    for q in range(8):
        lab = planes[q]
        t = temp_ref[q]
        h = _half_cond(lab, t)
        lab_out[q] = lab
        h_out[q] = h
        _radial_edges(in_out, out_out, q, t, h)


def _radial_edges(in_out, out_out, q, t, h):
    in_out[0, q : q + 1, :] = t[0:1]
    in_out[1, q : q + 1, :] = h[0:1]
    out_out[0, q : q + 1, :] = t[RL - 1 :]
    out_out[1, q : q + 1, :] = h[RL - 1 :]


_PLANES = pl.BlockSpec((G, RL, ANG), lambda i: (i, 0, 0))
_BLOCKS = pl.BlockSpec((SEC, 1, RL, G * AZ), lambda i: (0, i, 0, 0))
_RADIAL = pl.BlockSpec((2, G, ANG), lambda i: (0, i, 0))


def _materials(x, temp):
    return pl.pallas_call(
        _materials_kernel,
        grid=(NG,),
        in_specs=[_BLOCKS, _PLANES],
        out_specs=[_PLANES, _PLANES, _RADIAL, _RADIAL],
        out_shape=[_sds(AX, RL, ANG)] * 2 + [_sds(2, AX, ANG)] * 2,
        compiler_params=_params(),
        name="materials",
    )(x, temp)


def _first_kernel(x_ref, base_ref, gain_ref, lab_ref, d_out, temp_out, h_out, in_out, out_out):
    planes = _gathered(x_ref)
    for q in range(8):
        d = planes[q]
        t = base_ref[q] + d * gain_ref[q]
        h = _half_cond(lab_ref[q], t)
        d_out[q] = d
        temp_out[q] = t
        h_out[q] = h
        _radial_edges(in_out, out_out, q, t, h)


def _first(x, base, gain, lab):
    return pl.pallas_call(
        _first_kernel,
        grid=(NG,),
        in_specs=[_BLOCKS, _PLANES, _PLANES, _PLANES],
        out_specs=[_PLANES, _PLANES, _PLANES, _RADIAL, _RADIAL],
        out_shape=[_sds(AX, RL, ANG)] * 3 + [_sds(2, AX, ANG)] * 2,
        compiler_params=_params(),
        name="first_sweep",
    )(x, base, gain, lab)


def _faces(i, t_ref, h_ref, inner_ref, outer_ref, below_ref, above_ref):
    t, h = t_ref[i], h_ref[i]
    row = lax.broadcasted_iota(jnp.int32, (RL, ANG), 0)
    prev, following = jnp.maximum(i - 1, 0), jnp.minimum(i + 1, AX - 1)

    def others(ref, k, x):
        lower = jnp.where(i == 0, below_ref[k], ref[prev])
        upper = jnp.where(i == AX - 1, above_ref[k], ref[following])
        inward = jnp.where(row == 0, inner_ref[k, pl.ds(i, 1), :], pltpu.roll(x, 1, 0))
        outward = jnp.where(row == RL - 1, outer_ref[k, pl.ds(i, 1), :], pltpu.roll(x, RL - 1, 0))
        return lower, upper, inward, outward, pltpu.roll(x, 1, 1), pltpu.roll(x, ANG - 1, 1)

    flux, total = None, None
    for tn, hn in zip(others(t_ref, 0, t), others(h_ref, 1, h)):
        kf = h + hn
        term = kf * (tn - t)
        flux = term if flux is None else flux + term
        total = kf if total is None else total + kf
    return t, flux, total


def _ready_kernel(t_ref, h_ref, inner_ref, outer_ref, below_ref, above_ref, lab_ref, base_out, gain_out):
    def plane(i, _):
        t, flux, total = _faces(i, t_ref, h_ref, inner_ref, outer_ref, below_ref, above_ref)
        gain = 1.0 / (_capacity(lab_ref[i]) + total)
        base_out[i] = t + flux * gain
        gain_out[i] = gain
        return 0

    lax.fori_loop(0, AX, plane, 0)


def _second_kernel(t_ref, h_ref, inner_ref, outer_ref, below_ref, above_ref, lab_ref, prior_ref, d_ref, out):
    def plane(i, _):
        t, flux, total = _faces(i, t_ref, h_ref, inner_ref, outer_ref, below_ref, above_ref)
        cap = _capacity(lab_ref[i])
        mismatch = cap * (t - prior_ref[i]) - flux - d_ref[i]
        out[i] = t - mismatch / (cap + total)
        return 0

    lax.fori_loop(0, AX, plane, 0)


def _whole(kernel, n_out, name, *ins):
    return pl.pallas_call(
        kernel,
        out_shape=[_sds(AX, RL, ANG)] * n_out,
        compiler_params=_params(32),
        name=name,
    )(*ins)


def _ring(axis, x, step, closed):
    count = lax.axis_size(axis)
    if step > 0:
        perm = [(i, (i + 1) % count) for i in range(count if closed else count - 1)]
    else:
        perm = [((i + 1) % count, i) for i in range(count if closed else count - 1)]
    return lax.ppermute(x, axis, perm)


def _thermal_halo(t, h, inner_edge, outer_edge):
    inner = _ring("sec", outer_edge, 1, False)
    outer = _ring("sec", inner_edge, -1, False)
    below = _ring("ax", jnp.stack([t[-1], h[-1]]), 1, False)
    above = _ring("ax", jnp.stack([t[0], h[0]]), -1, False)
    return inner, outer, below, above


def shards(labels, exc, a0, prior):
    e_low, e_high = _edges(labels, exc, a0)
    clow = _ring("sec", e_high, 1, True)
    chigh = _ring("sec", e_low, -1, True)
    a, nu, oc, os, lt = _prepare(labels, exc, a0)
    lab_blocks = lax.all_to_all(lt, "sec", 0, 0)
    lab, h0, in0, out0 = _materials(lab_blocks, prior)
    halo0 = _thermal_halo(prior, h0, in0, out0)
    base, gain = _whole(_ready_kernel, 2, "first_ready", prior, h0, *halo0, lab)
    low, high, q = clow, chigh, None
    for index in range(len(WIDTHS)):
        if index:
            low = _ring("sec", e_high, 1, True)
            high = _ring("sec", e_low, -1, True)
        outs = _phase(index, a, low, high, nu, oc, os, clow, chigh, q, labels)
        if index < len(WIDTHS) - 1:
            a, q, e_low, e_high = outs
    closing, dissipation, dt = outs
    blocks = lax.all_to_all(dt, "sec", 0, 0)
    d, t1, h1, in1, out1 = _first(blocks, base, gain, lab)
    halo1 = _thermal_halo(t1, h1, in1, out1)
    (t2,) = _whole(_second_kernel, 1, "second_sweep", t1, h1, *halo1, lab, prior, d)
    return closing, dissipation, t2


def solution(mesh):
    spec = P("ax", "sec", None)
    return jax.shard_map(
        shards,
        mesh=mesh,
        in_specs=(spec, P(None, "ax", "sec", None), spec, spec),
        out_specs=(spec, spec, spec),
        check_vma=False,
    )
```

time: 497 us -> 169 us (0.34)
  other arithmetic: 145 us -> 0.02 us
  local copies, waits for them, and re-layouts: 131 us -> 17 us
  starting transfers between devices: 150 us -> 75.8 us
  Pallas kernels: 0 us -> 43.6 us
  waiting for transfers between devices: 62.2 us -> 30.8 us
    add x16 -> x0, other arithmetic: 74.4 us -> none  [advance(): return (fresh, induced_dissipation + sigma * change * change)]
    ppermute x40 -> x16, starting transfers between devices: 121 us -> 55.5 us  [_ring(): return lax.ppermute(x, axis, perm)]
    slice x28 -> x3, local copies, waits for them, and re-layouts: 46 us -> 0.02 us  [_thermal_halo(): above = _ring('ax', jnp.stack([t[0], h[0]]), -1, False)]
    pallas_call x0 -> x10, Pallas kernels: none -> 43.6 us  [the longest x4 18.4 us: _phase(): pl.pallas_call(functools.partial(_phase_kernel, first, width, nextw, last...]
    while x17 -> x0, local copies, waits for them, and re-layouts: 23.7 us -> none
    sub x1 -> x0, other arithmetic: 21.8 us -> none  [damping_weight(): return warmth_distribution - mismatch_amount / main_entries]
    ppermute x4 -> x0, local copies, waits for them, and re-layouts: 20.7 us -> none  [the longest x2 10.6 us: with_halo(): lax.ppermute(head, axis, [((i + 1) % count, i) for i in range(ends)])]
    all_to_all x1 -> x2, waiting for transfers between devices: 19 us -> 0.01 us  [the longest x1 0.01 us: shards(): lab_blocks = lax.all_to_all(lt, 'sec', 0, 0)]
  transfers between devices with their start and end apart: 41 -> 18, of which waited for: 21 -> 7; matrix products, arithmetic and copies ran while one was open for 6% -> 0% of each run, Pallas kernels for 0% -> 18%
where the time goes in v1:
time: 169 us; the launch traced here: 168 us
  starting transfers between devices  75.8 us (45%)
  Pallas kernels  43.6 us (26%)
  waiting for transfers between devices  30.8 us (18%)
  local copies, waits for them, and re-layouts  17 us (10%)
    ppermute x16, starting transfers between devices, _ring(): return lax.ppermute(x, axis, perm)  55.5 us
    ppermute x16, waiting for transfers between devices, _ring(): return lax.ppermute(x, axis, perm)  30.8 us
    pallas_call x4, Pallas kernels, _phase(): pl.pallas_call(functools.partial(_phase_kernel, first, width, nextw, last...  18.4 us
    unnamed x38, local copies, waits for them, and re-layouts  17 us
    all_to_all x1, starting transfers between devices, shards(): blocks = lax.all_to_all(dt, 'sec', 0, 0)  13.6 us
    pallas_call x2, Pallas kernels, _whole(): pl.pallas_call(kernel, out_shape=[_sds(AX, RL, ANG)] * n_out, compiler_pa...  12.7 us
    all_to_all x1, starting transfers between devices, shards(): lab_blocks = lax.all_to_all(lt, 'sec', 0, 0)  6.77 us
    pallas_call x1, Pallas kernels, _materials(): pl.pallas_call(_materials_kernel, grid=(NG,), in_specs=[_BLOCKS, _PLANES]...  5.09 us
  transfers between devices with their start and end apart: 18, of which 7 were waited for; matrix products, arithmetic and copies ran while one was open for 0% of the time, Pallas kernels for 18%

profile of v1, /device:TPU:3, one launch (start us, length us, event | category | flops | bytes accessed | tf_op | source)
XLA Modules:
  0.0 168.2 jit_solution(5789646164857267934)
XLA Ops:
  1.9 1.6 copy-done.9
  4.7 3.2 %edge_layers.1 = (f32[13,64,256]{2,1,0:T(8,128)}, f32[13,64,256]{2,1,0:T(8,128)}) custom-call(s32[64,16,256]{2,1,0:T(8,128)S(1)} %copy-done.7, f32[2,64,16,256]{3,2,1,0:T(8,128)S(1)} %copy-done.9, f32[64,16,256]{2,1,0:T(8,128)S(1)} %copy-done.10), custom_call_target="tpu_custom_call" | custom-call | tf_op jit(solution)/shard_map/edge_layers/pallas_call | solution.py:64
  7.8 1.6 collective-permute-start
  9.5 3.1 %collective-permute-start.1 = (f32[13,64,256]{2,1,0:T(8,128)}, f32[13,64,256]{2,1,0:T(8,128)S(1)}, u32[]{:S(2)}, u32[]{:S(2)}) collective-permute-start(f32[13,64,256]{2,1,0:T(8,128)} %get-tuple-element.38), channel_id=1, source_target_pairs={{4,0},{8,4},{12,8},{16,12},{20,16},{24,20},{28,24},{32,28},{36,32}... | collective-permute-start | bytes 2555912 | tf_op jit(solution)/shard_map/ppermute | solution.py:350
  12.6 1.7 prepare.1
  18.2 6.8 %all-to-all-start.1 = ((f32[32,8,8,128]{3,2,1,0:T(8,128)}), f32[32,8,8,128]{3,2,1,0:T(8,128)}, u32[]{:S(2)}, u32[]{:S(2)}) async-start(f32[32,8,8,128]{3,2,1,0:T(8,128)} %copy-done.11), calls=%async_computation.1 | async-start | bytes 2097152 | tf_op jit(solution)/shard_map/all_to_all | solution.py:366
  24.9 7.8 %collective-permute-done.refs_1_.refs_6_ = f32[13,64,256]{2,1,0:T(8,128)S(1)} collective-permute-done((f32[13,64,256]{2,1,0:T(8,128)}, f32[13,64,256]{2,1,0:T(8,128)S(1)}, u32[]{:S(2)}, u32[]{:S(2)}) %collective-permute-start) | collective-permute-done | bytes 852000 | tf_op jit(solution)/shard_map/ppermute | solution.py:350
  32.8 6.0 %collective-permute-done.1.refs_2_.refs_7_ = f32[13,64,256]{2,1,0:T(8,128)S(1)} collective-permute-done((f32[13,64,256]{2,1,0:T(8,128)}, f32[13,64,256]{2,1,0:T(8,128)S(1)}, u32[]{:S(2)}, u32[]{:S(2)}) %collective-permute-start.1) | collective-permute-done | bytes 852000 | tf_op jit(solution)/shard_map/ppermute | solution.py:350
  42.5 4.1 %field_0.1 = (f32[16,64,256]{2,1,0:T(8,128)S(1)}, f32[16,64,256]{2,1,0:T(8,128)S(1)}, f32[4,64,256]{2,1,0:T(8,128)S(1)}, f32[4,64,256]{2,1,0:T(8,128)S(1)}) custom-call(f32[16,64,256]{2,1,0:T(8,128)S(1)} %copy-done.18, f32[13,64,256]{2,1,0:T(8,128)S(1)} %collective-permute-done.refs_1_.refs_6_, f32[13,64,256]{2,1,0:T(8,128)S(1)} %collective-permute-done.1.refs_2_.refs_7_, ...), custom_call_target="tpu_custom_call" | custom-call | tf_op jit(solution)/shard_map/field_0/pallas_call | solution.py:196
  46.7 4.5 %collective-permute-start.3 = (f32[4,64,256]{2,1,0:T(8,128)S(1)}, f32[4,64,256]{2,1,0:T(8,128)S(1)}, u32[]{:S(2)}, u32[]{:S(2)}) collective-permute-start(f32[4,64,256]{2,1,0:T(8,128)S(1)} %get-tuple-element.44), channel_id=1, source_target_pairs={{4,0},{8,4},{12,8},{16,12},{20,16},{24,20},{28,24},{32,28},{36,32}... | collective-permute-start | bytes 786440 | tf_op jit(solution)/shard_map/ppermute | solution.py:350
  51.1 3.8 %collective-permute-done.2.refs_1_ = f32[4,64,256]{2,1,0:T(8,128)S(1)} collective-permute-done((f32[4,64,256]{2,1,0:T(8,128)S(1)}, f32[4,64,256]{2,1,0:T(8,128)S(1)}, u32[]{:S(2)}, u32[]{:S(2)}) %collective-permute-start.2) | collective-permute-done | bytes 262176 | tf_op jit(solution)/shard_map/ppermute | solution.py:350
  54.9 4.2 %field_1.1 = (f32[16,64,256]{2,1,0:T(8,128)S(1)}, f32[16,64,256]{2,1,0:T(8,128)S(1)}, f32[4,64,256]{2,1,0:T(8,128)S(1)}, f32[4,64,256]{2,1,0:T(8,128)S(1)}) custom-call(f32[16,64,256]{2,1,0:T(8,128)S(1)} %get-tuple-element.42.refs_0_, f32[4,64,256]{2,1,0:T(8,128)S(1)} %collective-permute-done.2.refs_1_, f32[4,64,256]{2,1,0:T(8,128)S(1)} %collective-permute-done.3.refs_2_, ...), custom_call_target="tpu_custom_call" | custom-call | tf_op jit(solution)/shard_map/field_1/pallas_call | solution.py:196
  59.2 4.5 %collective-permute-start.5 = (f32[4,64,256]{2,1,0:T(8,128)S(1)}, f32[4,64,256]{2,1,0:T(8,128)S(1)}, u32[]{:S(2)}, u32[]{:S(2)}) collective-permute-start(f32[4,64,256]{2,1,0:T(8,128)S(1)} %get-tuple-element.48), channel_id=1, source_target_pairs={{4,0},{8,4},{12,8},{16,12},{20,16},{24,20},{28,24},{32,28},{36,32}... | collective-permute-start | bytes 786440 | tf_op jit(solution)/shard_map/ppermute | solution.py:350
  63.7 3.7 %collective-permute-done.4.refs_1_ = f32[4,64,256]{2,1,0:T(8,128)S(1)} collective-permute-done((f32[4,64,256]{2,1,0:T(8,128)S(1)}, f32[4,64,256]{2,1,0:T(8,128)S(1)}, u32[]{:S(2)}, u32[]{:S(2)}) %collective-permute-start.4) | collective-permute-done | bytes 262176 | tf_op jit(solution)/shard_map/ppermute | solution.py:350
  67.4 4.2 %field_2.1 = (f32[16,64,256]{2,1,0:T(8,128)S(1)}, f32[16,64,256]{2,1,0:T(8,128)S(1)}, f32[4,64,256]{2,1,0:T(8,128)S(1)}, f32[4,64,256]{2,1,0:T(8,128)S(1)}) custom-call(f32[16,64,256]{2,1,0:T(8,128)S(1)} %get-tuple-element.46.refs_0_, f32[4,64,256]{2,1,0:T(8,128)S(1)} %collective-permute-done.4.refs_1_, f32[4,64,256]{2,1,0:T(8,128)S(1)} %collective-permute-done.5.refs_2_, ...), custom_call_target="tpu_custom_call" | custom-call | tf_op jit(solution)/shard_map/field_2/pallas_call | solution.py:196
  71.6 4.6 %collective-permute-start.7 = (f32[4,64,256]{2,1,0:T(8,128)S(1)}, f32[4,64,256]{2,1,0:T(8,128)S(1)}, u32[]{:S(2)}, u32[]{:S(2)}) collective-permute-start(f32[4,64,256]{2,1,0:T(8,128)S(1)} %get-tuple-element.52), channel_id=1, source_target_pairs={{4,0},{8,4},{12,8},{16,12},{20,16},{24,20},{28,24},{32,28},{36,32}... | collective-permute-start | bytes 786440 | tf_op jit(solution)/shard_map/ppermute | solution.py:350
  76.2 3.7 %collective-permute-done.6.refs_1_ = f32[4,64,256]{2,1,0:T(8,128)S(1)} collective-permute-done((f32[4,64,256]{2,1,0:T(8,128)S(1)}, f32[4,64,256]{2,1,0:T(8,128)S(1)}, u32[]{:S(2)}, u32[]{:S(2)}) %collective-permute-start.6) | collective-permute-done | bytes 262176 | tf_op jit(solution)/shard_map/ppermute | solution.py:350
  79.9 5.9 %field_3.1 = (f32[64,16,256]{2,1,0:T(8,128)}, f32[64,16,256]{2,1,0:T(8,128)}, f32[32,8,8,128]{3,2,1,0:T(8,128)S(1)}) custom-call(f32[16,64,256]{2,1,0:T(8,128)S(1)} %get-tuple-element.50.refs_0_, f32[4,64,256]{2,1,0:T(8,128)S(1)} %collective-permute-done.6.refs_1_, f32[4,64,256]{2,1,0:T(8,128)S(1)} %collective-permute-done.7.refs_2_, ...), custom_call_target="tpu_custom_call" | custom-call | tf_op jit(solution)/shard_map/field_3/pallas_call | solution.py:196
  86.8 13.6 %all-to-all-start = ((f32[32,8,8,128]{3,2,1,0:T(8,128)}), f32[32,8,8,128]{3,2,1,0:T(8,128)S(1)}, u32[]{:S(2)}, u32[]{:S(2)}) async-start(f32[32,8,8,128]{3,2,1,0:T(8,128)} %copy-done.12), calls=%async_computation | async-start | bytes 2097152 | tf_op jit(solution)/shard_map/all_to_all | solution.py:379
  100.4 5.1 %materials.1 = (f32[64,8,512]{2,1,0:T(8,128)S(1)}, f32[64,8,512]{2,1,0:T(8,128)S(1)}, f32[2,64,512]{2,1,0:T(8,128)S(1)}, f32[2,64,512]{2,1,0:T(8,128)S(1)}) custom-call(f32[32,8,8,128]{3,2,1,0:T(8,128)} %all-to-all-done.1.x_ref, f32[64,8,512]{2,1,0:T(8,128)S(1)} %copy-done.6), custom_call_target="tpu_custom_call" | custom-call | tf_op jit(solution)/shard_map/materials/pallas_call | solution.py:257
  105.5 3.1 %collective-permute-start.8 = (f32[2,64,512]{2,1,0:T(8,128)S(1)}, f32[2,64,512]{2,1,0:T(8,128)S(1)}, u32[]{:S(2)}, u32[]{:S(2)}) collective-permute-start(f32[2,64,512]{2,1,0:T(8,128)S(1)} %get-tuple-element.59), channel_id=1, source_target_pairs={{0,4},{4,8},{8,12},{12,16},{16,20},{20,24},{24,28},{28,32},{32,36}... | collective-permute-start | bytes 786440 | tf_op jit(solution)/shard_map/ppermute | solution.py:350
  108.6 5.2 %collective-permute-start.9 = (f32[2,64,512]{2,1,0:T(8,128)S(1)}, f32[2,64,512]{2,1,0:T(8,128)S(1)}, u32[]{:S(2)}, u32[]{:S(2)}) collective-permute-start(f32[2,64,512]{2,1,0:T(8,128)S(1)} %get-tuple-element.60), channel_id=1, source_target_pairs={{4,0},{8,4},{12,8},{16,12},{20,16},{24,20},{28,24},{32,28},{36,32}... | collective-permute-start | bytes 786440 | tf_op jit(solution)/shard_map/ppermute | solution.py:350
  113.9 11.3 %collective-permute-start.10 = (f32[2,8,512]{2,1,0:T(8,128)S(1)}, f32[2,8,512]{2,1,0:T(8,128)S(1)}, u32[]{:S(2)}, u32[]{:S(2)}) collective-permute-start(f32[2,8,512]{2,1,0:T(8,128)S(1)} %pad_maximum_fusion), channel_id=1, source_target_pairs={{0,1},{1,2},{2,3},{4,5},{5,6},{6,7},{8,9},{9,10},{10,11},{12,13},{... | collective-permute-start | bytes 98312 | tf_op jit(solution)/shard_map/ppermute | solution.py:350
  125.2 1.9 %collective-permute-start.11 = (f32[2,8,512]{2,1,0:T(8,128)S(1)}, f32[2,8,512]{2,1,0:T(8,128)S(1)}, u32[]{:S(2)}, u32[]{:S(2)}) collective-permute-start(f32[2,8,512]{2,1,0:T(8,128)S(1)} %pad_maximum_fusion.1), channel_id=1, source_target_pairs={{1,0},{2,1},{3,2},{5,4},{6,5},{7,6},{9,8},{10,9},{11,10},{13,12},{... | collective-permute-start | bytes 98312 | tf_op jit(solution)/shard_map/ppermute | solution.py:350
  127.2 4.8 %collective-permute-done.11.above_ref = f32[2,8,512]{2,1,0:T(8,128)S(1)} collective-permute-done((f32[2,8,512]{2,1,0:T(8,128)S(1)}, f32[2,8,512]{2,1,0:T(8,128)S(1)}, u32[]{:S(2)}, u32[]{:S(2)}) %collective-permute-start.11) | collective-permute-done | bytes 32800 | tf_op jit(solution)/shard_map/ppermute | solution.py:350
  132.0 5.8 %first_ready.1 = (f32[64,8,512]{2,1,0:T(8,128)S(1)}, f32[64,8,512]{2,1,0:T(8,128)S(1)}) custom-call(f32[64,8,512]{2,1,0:T(8,128)S(1)} %copy-done.6, f32[64,8,512]{2,1,0:T(8,128)S(1)} %get-tuple-element.58.h_ref, f32[2,64,512]{2,1,0:T(8,128)S(1)} %collective-permute-done.8.inner_ref, f32[2,64,512]{2,1,0:T(8,128)S(1)} %collective-permute-done.9.outer_ref, ...), custom_call_target="tpu_custom_call" | custom-call | tf_op jit(solution)/shard_map/first_ready/pallas_call | solution.py:336
  142.2 2.6 %first_sweep.1 = (f32[64,8,512]{2,1,0:T(8,128)S(1)}, f32[64,8,512]{2,1,0:T(8,128)S(1)}, f32[64,8,512]{2,1,0:T(8,128)S(1)}, f32[2,64,512]{2,1,0:T(8,128)S(1)}, f32[2,64,512]{2,1,0:T(8,128)S(1)}) custom-call(f32[32,8,8,128]{3,2,1,0:T(8,128)S(1)} %all-to-all-done.x_ref, f32[64,8,512]{2,1,0:T(8,128)S(1)} %copy-done.14, f32[64,8,512]{2,1,0:T(8,128)S(1)} %copy-done.16, ...), custom_call_target="tpu_custom_call" | custom-call | tf_op jit(solution)/shard_map/first_sweep/pallas_call | solution.py:281
  144.8 1.9 %collective-permute-start.12 = (f32[2,64,512]{2,1,0:T(8,128)S(1)}, f32[2,64,512]{2,1,0:T(8,128)S(1)}, u32[]{:S(2)}, u32[]{:S(2)}) collective-permute-start(f32[2,64,512]{2,1,0:T(8,128)S(1)} %get-tuple-element.66), channel_id=1, source_target_pairs={{0,4},{4,8},{8,12},{12,16},{16,20},{20,24},{24,28},{28,32},{32,36}... | collective-permute-start | bytes 786440 | tf_op jit(solution)/shard_map/ppermute | solution.py:350
  146.8 6.4 %collective-permute-start.13 = (f32[2,64,512]{2,1,0:T(8,128)S(1)}, f32[2,64,512]{2,1,0:T(8,128)S(1)}, u32[]{:S(2)}, u32[]{:S(2)}) collective-permute-start(f32[2,64,512]{2,1,0:T(8,128)S(1)} %get-tuple-element.67), channel_id=1, source_target_pairs={{4,0},{8,4},{12,8},{16,12},{20,16},{24,20},{28,24},{32,28},{36,32}... | collective-permute-start | bytes 786440 | tf_op jit(solution)/shard_map/ppermute | solution.py:350
  153.2 1.9 %collective-permute-start.15 = (f32[2,8,512]{2,1,0:T(8,128)S(1)}, f32[2,8,512]{2,1,0:T(8,128)S(1)}, u32[]{:S(2)}, u32[]{:S(2)}) collective-permute-start(f32[2,8,512]{2,1,0:T(8,128)S(1)} %pad_maximum_fusion.3), channel_id=1, source_target_pairs={{1,0},{2,1},{3,2},{5,4},{6,5},{7,6},{9,8},{10,9},{11,10},{13,12},{... | collective-permute-start | bytes 98312 | tf_op jit(solution)/shard_map/ppermute | solution.py:350
  155.1 5.1 %collective-permute-start.14 = (f32[2,8,512]{2,1,0:T(8,128)S(1)}, f32[2,8,512]{2,1,0:T(8,128)S(1)}, u32[]{:S(2)}, u32[]{:S(2)}) collective-permute-start(f32[2,8,512]{2,1,0:T(8,128)S(1)} %pad_maximum_fusion.2), channel_id=1, source_target_pairs={{0,1},{1,2},{2,3},{4,5},{5,6},{6,7},{8,9},{9,10},{10,11},{12,13},{... | collective-permute-start | bytes 98312 | tf_op jit(solution)/shard_map/ppermute | solution.py:350
  161.3 6.9 %second_sweep.1 = f32[64,8,512]{2,1,0:T(8,128)} custom-call(f32[64,8,512]{2,1,0:T(8,128)S(1)} %get-tuple-element.64.t_ref, f32[64,8,512]{2,1,0:T(8,128)S(1)} %get-tuple-element.65.h_ref, f32[2,64,512]{2,1,0:T(8,128)S(1)} %collective-permute-done.12.inner_ref, f32[2,64,512]{2,1,0:T(8,128)S(1)} %collective-permute-done.13.outer_ref, ...), custom_call_target="tpu_custom_call" | custom-call | tf_op jit(solution)/shard_map/second_sweep/pallas_call | solution.py:336
  (59 shorter events, 16.8 us)
Async XLA Ops:
  0.6 1.2 copy-start.7
  1.9 1.6 copy-start.9
  3.5 1.2 copy-start.10
  7.8 24.9 %collective-permute-start = (f32[13,64,256]{2,1,0:T(8,128)}, f32[13,64,256]{2,1,0:T(8,128)S(1)}, u32[]{:S(2)}, u32[]{:S(2)}) collective-permute-start(f32[13,64,256]{2,1,0:T(8,128)} %get-tuple-element.37), channel_id=1, source_target_pairs={{0,4},{4,8},{8,12},{12,16},{16,20},{20,24},{24,28},{28,32},{32,36}... | collective-permute-start | bytes 2555912 | tf_op jit(solution)/shard_map/ppermute | solution.py:350
  9.5 29.3 %collective-permute-start.1 = (f32[13,64,256]{2,1,0:T(8,128)}, f32[13,64,256]{2,1,0:T(8,128)S(1)}, u32[]{:S(2)}, u32[]{:S(2)}) collective-permute-start(f32[13,64,256]{2,1,0:T(8,128)} %get-tuple-element.38), channel_id=1, source_target_pairs={{4,0},{8,4},{12,8},{16,12},{20,16},{24,20},{28,24},{32,28},{36,32}... | collective-permute-start | bytes 2555912 | tf_op jit(solution)/shard_map/ppermute | solution.py:350
  16.2 1.0 copy-start.11
  18.2 68.7 %all-to-all-start.1 = ((f32[32,8,8,128]{3,2,1,0:T(8,128)}), f32[32,8,8,128]{3,2,1,0:T(8,128)}, u32[]{:S(2)}, u32[]{:S(2)}) async-start(f32[32,8,8,128]{3,2,1,0:T(8,128)} %copy-done.11), calls=%async_computation.1 | async-start | bytes 2097152 | tf_op jit(solution)/shard_map/all_to_all | solution.py:366
  38.8 1.2 copy-start.1
  40.0 1.2 copy-start.4
  41.2 1.2 copy-start.18
  42.5 12.4 %copy-start.2 = (f32[16,64,256]{2,1,0:T(8,128)S(1)}, f32[16,64,256]{2,1,0:T(8,128)}, u32[]{:S(2)}) copy-start(f32[16,64,256]{2,1,0:T(8,128)} %copy-done) | copy-start | bytes 3145732
  42.5 12.4 %copy-start.5 = (f32[16,64,256]{2,1,0:T(8,128)S(1)}, f32[16,64,256]{2,1,0:T(8,128)}, u32[]{:S(2)}) copy-start(f32[16,64,256]{2,1,0:T(8,128)} %copy-done.3) | copy-start | bytes 3145732
  46.6 8.3 %collective-permute-start.2 = (f32[4,64,256]{2,1,0:T(8,128)S(1)}, f32[4,64,256]{2,1,0:T(8,128)S(1)}, u32[]{:S(2)}, u32[]{:S(2)}) collective-permute-start(f32[4,64,256]{2,1,0:T(8,128)S(1)} %get-tuple-element.43), channel_id=1, source_target_pairs={{0,4},{4,8},{8,12},{12,16},{16,20},{20,24},{24,28},{28,32},{32,36}... | collective-permute-start | bytes 786440 | tf_op jit(solution)/shard_map/ppermute | solution.py:350
  46.7 8.2 %collective-permute-start.3 = (f32[4,64,256]{2,1,0:T(8,128)S(1)}, f32[4,64,256]{2,1,0:T(8,128)S(1)}, u32[]{:S(2)}, u32[]{:S(2)}) collective-permute-start(f32[4,64,256]{2,1,0:T(8,128)S(1)} %get-tuple-element.44), channel_id=1, source_target_pairs={{4,0},{8,4},{12,8},{16,12},{20,16},{24,20},{28,24},{32,28},{36,32}... | collective-permute-start | bytes 786440 | tf_op jit(solution)/shard_map/ppermute | solution.py:350
  59.1 8.3 %collective-permute-start.4 = (f32[4,64,256]{2,1,0:T(8,128)S(1)}, f32[4,64,256]{2,1,0:T(8,128)S(1)}, u32[]{:S(2)}, u32[]{:S(2)}) collective-permute-start(f32[4,64,256]{2,1,0:T(8,128)S(1)} %get-tuple-element.47), channel_id=1, source_target_pairs={{0,4},{4,8},{8,12},{12,16},{16,20},{20,24},{24,28},{28,32},{32,36}... | collective-permute-start | bytes 786440 | tf_op jit(solution)/shard_map/ppermute | solution.py:350
  59.2 8.2 %collective-permute-start.5 = (f32[4,64,256]{2,1,0:T(8,128)S(1)}, f32[4,64,256]{2,1,0:T(8,128)S(1)}, u32[]{:S(2)}, u32[]{:S(2)}) collective-permute-start(f32[4,64,256]{2,1,0:T(8,128)S(1)} %get-tuple-element.48), channel_id=1, source_target_pairs={{4,0},{8,4},{12,8},{16,12},{20,16},{24,20},{28,24},{32,28},{36,32}... | collective-permute-start | bytes 786440 | tf_op jit(solution)/shard_map/ppermute | solution.py:350
  67.4 12.5 %copy-start.8 = (s32[64,16,256]{2,1,0:T(8,128)S(1)}, s32[64,16,256]{2,1,0:T(8,128)}, u32[]{:S(2)}) copy-start(s32[64,16,256]{2,1,0:T(8,128)} %refs_9_.1) | copy-start | bytes 3145732
  71.6 8.4 %collective-permute-start.6 = (f32[4,64,256]{2,1,0:T(8,128)S(1)}, f32[4,64,256]{2,1,0:T(8,128)S(1)}, u32[]{:S(2)}, u32[]{:S(2)}) collective-permute-start(f32[4,64,256]{2,1,0:T(8,128)S(1)} %get-tuple-element.51), channel_id=1, source_target_pairs={{0,4},{4,8},{8,12},{12,16},{16,20},{20,24},{24,28},{28,32},{32,36}... | collective-permute-start | bytes 786440 | tf_op jit(solution)/shard_map/ppermute | solution.py:350
  71.6 8.3 %collective-permute-start.7 = (f32[4,64,256]{2,1,0:T(8,128)S(1)}, f32[4,64,256]{2,1,0:T(8,128)S(1)}, u32[]{:S(2)}, u32[]{:S(2)}) collective-permute-start(f32[4,64,256]{2,1,0:T(8,128)S(1)} %get-tuple-element.52), channel_id=1, source_target_pairs={{4,0},{8,4},{12,8},{16,12},{20,16},{24,20},{28,24},{32,28},{36,32}... | collective-permute-start | bytes 786440 | tf_op jit(solution)/shard_map/ppermute | solution.py:350
  86.8 13.6 %copy-start.6 = (f32[64,8,512]{2,1,0:T(8,128)S(1)}, f32[64,8,512]{2,1,0:T(8,128)}, u32[]{:S(2)}) copy-start(f32[64,8,512]{2,1,0:T(8,128)} %prior_ref.1) | copy-start | bytes 3145732
  86.8 52.9 %all-to-all-start = ((f32[32,8,8,128]{3,2,1,0:T(8,128)}), f32[32,8,8,128]{3,2,1,0:T(8,128)S(1)}, u32[]{:S(2)}, u32[]{:S(2)}) async-start(f32[32,8,8,128]{3,2,1,0:T(8,128)} %copy-done.12), calls=%async_computation | async-start | bytes 2097152 | tf_op jit(solution)/shard_map/all_to_all | solution.py:379
  105.5 26.4 %collective-permute-start.8 = (f32[2,64,512]{2,1,0:T(8,128)S(1)}, f32[2,64,512]{2,1,0:T(8,128)S(1)}, u32[]{:S(2)}, u32[]{:S(2)}) collective-permute-start(f32[2,64,512]{2,1,0:T(8,128)S(1)} %get-tuple-element.59), channel_id=1, source_target_pairs={{0,4},{4,8},{8,12},{12,16},{16,20},{20,24},{24,28},{28,32},{32,36}... | collective-permute-start | bytes 786440 | tf_op jit(solution)/shard_map/ppermute | solution.py:350
  108.6 23.3 %collective-permute-start.9 = (f32[2,64,512]{2,1,0:T(8,128)S(1)}, f32[2,64,512]{2,1,0:T(8,128)S(1)}, u32[]{:S(2)}, u32[]{:S(2)}) collective-permute-start(f32[2,64,512]{2,1,0:T(8,128)S(1)} %get-tuple-element.60), channel_id=1, source_target_pairs={{4,0},{8,4},{12,8},{16,12},{20,16},{24,20},{28,24},{32,28},{36,32}... | collective-permute-start | bytes 786440 | tf_op jit(solution)/shard_map/ppermute | solution.py:350
  113.9 13.3 %collective-permute-start.10 = (f32[2,8,512]{2,1,0:T(8,128)S(1)}, f32[2,8,512]{2,1,0:T(8,128)S(1)}, u32[]{:S(2)}, u32[]{:S(2)}) collective-permute-start(f32[2,8,512]{2,1,0:T(8,128)S(1)} %pad_maximum_fusion), channel_id=1, source_target_pairs={{0,1},{1,2},{2,3},{4,5},{5,6},{6,7},{8,9},{9,10},{10,11},{12,13},{... | collective-permute-start | bytes 98312 | tf_op jit(solution)/shard_map/ppermute | solution.py:350
  125.2 6.7 %collective-permute-start.11 = (f32[2,8,512]{2,1,0:T(8,128)S(1)}, f32[2,8,512]{2,1,0:T(8,128)S(1)}, u32[]{:S(2)}, u32[]{:S(2)}) collective-permute-start(f32[2,8,512]{2,1,0:T(8,128)S(1)} %pad_maximum_fusion.1), channel_id=1, source_target_pairs={{1,0},{2,1},{3,2},{5,4},{6,5},{7,6},{9,8},{10,9},{11,10},{13,12},{... | collective-permute-start | bytes 98312 | tf_op jit(solution)/shard_map/ppermute | solution.py:350
  137.8 1.0 copy-start.13
  139.8 1.2 copy-start.14
  141.0 1.2 copy-start.16
  144.8 16.4 %collective-permute-start.12 = (f32[2,64,512]{2,1,0:T(8,128)S(1)}, f32[2,64,512]{2,1,0:T(8,128)S(1)}, u32[]{:S(2)}, u32[]{:S(2)}) collective-permute-start(f32[2,64,512]{2,1,0:T(8,128)S(1)} %get-tuple-element.66), channel_id=1, source_target_pairs={{0,4},{4,8},{8,12},{12,16},{16,20},{20,24},{24,28},{28,32},{32,36}... | collective-permute-start | bytes 786440 | tf_op jit(solution)/shard_map/ppermute | solution.py:350
  146.8 14.5 %collective-permute-start.13 = (f32[2,64,512]{2,1,0:T(8,128)S(1)}, f32[2,64,512]{2,1,0:T(8,128)S(1)}, u32[]{:S(2)}, u32[]{:S(2)}) collective-permute-start(f32[2,64,512]{2,1,0:T(8,128)S(1)} %get-tuple-element.67), channel_id=1, source_target_pairs={{4,0},{8,4},{12,8},{16,12},{20,16},{24,20},{28,24},{32,28},{36,32}... | collective-permute-start | bytes 786440 | tf_op jit(solution)/shard_map/ppermute | solution.py:350
  153.2 7.1 %collective-permute-start.15 = (f32[2,8,512]{2,1,0:T(8,128)S(1)}, f32[2,8,512]{2,1,0:T(8,128)S(1)}, u32[]{:S(2)}, u32[]{:S(2)}) collective-permute-start(f32[2,8,512]{2,1,0:T(8,128)S(1)} %pad_maximum_fusion.3), channel_id=1, source_target_pairs={{1,0},{2,1},{3,2},{5,4},{6,5},{7,6},{9,8},{10,9},{11,10},{13,12},{... | collective-permute-start | bytes 98312 | tf_op jit(solution)/shard_map/ppermute | solution.py:350
  155.1 6.2 %collective-permute-start.14 = (f32[2,8,512]{2,1,0:T(8,128)S(1)}, f32[2,8,512]{2,1,0:T(8,128)S(1)}, u32[]{:S(2)}, u32[]{:S(2)}) collective-permute-start(f32[2,8,512]{2,1,0:T(8,128)S(1)} %pad_maximum_fusion.2), channel_id=1, source_target_pairs={{0,1},{1,2},{2,3},{4,5},{5,6},{6,7},{8,9},{9,10},{10,11},{12,13},{... | collective-permute-start | bytes 98312 | tf_op jit(solution)/shard_map/ppermute | solution.py:350
  (5 other events, 4.9 us)

commit v2 on v1

v2 whole, which is shorter than its diff:
```python
import functools
import math

import jax
import jax.numpy as jnp
from jax import lax
from jax.experimental import pallas as pl
from jax.experimental.pallas import tpu as pltpu
from jax.sharding import PartitionSpec as P

SAMPLES = 16
PERIOD = 32
WIDTHS = (4, 4, 4, 4)
KMAX = max(WIDTHS)
W0 = WIDTHS[0]
C0 = W0 - 1
CH = KMAX - 1
FIRST = (C0, C0, C0 - 1 if KMAX > W0 else C0)
REST = tuple(CH - n for n in FIRST)

F32 = jnp.float32
AX, AZ, RAD, ANG = 64, 16, 256, 512
SEC = 32
RL = RAD // SEC
G = 8
NG = AX // G


def _params(mib=16):
    return pltpu.CompilerParams(vmem_limit_bytes=mib * 2**20)


def _sds(*shape):
    return jax.ShapeDtypeStruct(shape, F32)


def _cost(flops, nbytes):
    return pl.CostEstimate(flops=flops, bytes_accessed=nbytes, transcendentals=0)


def _loop(body):
    def step(g, _):
        body(g)
        return 0

    lax.fori_loop(0, NG, step, 0)


def _planes(g):
    return pl.ds(pl.multiple_of(g * G, G), G)


def _reluct(lab):
    return jnp.where(lab == 0, 0.05, jnp.where(lab == 3, 0.2, 0.24)).astype(F32)


def _sigma(lab):
    return jnp.where(lab == 0, 0.3, jnp.where(lab == 1, 1.0, jnp.where(lab == 2, 0.0, 0.6))).astype(F32)


def _driven(lab, x):
    return jnp.where((lab == 1) | (lab == 3), x, 0.0)


def _edges_kernel(lab_hbm, exc_hbm, a_hbm, low_ref, high_ref, lab_v, exc_v, a_v, sems):
    copies = []
    for g in range(NG):
        at = pl.ds(g * G, G)
        copies.append(
            [
                pltpu.make_async_copy(lab_hbm.at[at], lab_v.at[at], sems.at[g, 0]),
                pltpu.make_async_copy(exc_hbm.at[0, at], exc_v.at[0, at], sems.at[g, 1]),
                pltpu.make_async_copy(exc_hbm.at[1, at], exc_v.at[1, at], sems.at[g, 2]),
                pltpu.make_async_copy(a_hbm.at[at], a_v.at[at], sems.at[g, 3]),
            ]
        )
        for copy in copies[-1]:
            copy.start()
    for g in range(NG):
        for copy in copies[g]:
            copy.wait()
        at = pl.ds(g * G, G)
        lab = jnp.swapaxes(lab_v[at], 0, 1)
        c = jnp.swapaxes(exc_v[0, at], 0, 1)
        s = jnp.swapaxes(exc_v[1, at], 0, 1)
        a = jnp.swapaxes(a_v[at], 0, 1)
        for out, high in ((low_ref, False), (high_ref, True)):

            def edge(x, n):
                return x[AZ - n :] if high else x[:n]

            out[0:W0, g] = edge(a, W0)
            n1, n2, n3 = FIRST
            at1, at2 = W0 + n1, W0 + n1 + n2
            out[W0:at1, g] = _reluct(edge(lab, n1))
            out[at1:at2, g] = _driven(edge(lab, n2), edge(c, n2))
            out[at2 : at2 + n3, g] = _driven(edge(lab, n3), edge(s, n3))


def _edges(labels, exc, a):
    n = W0 + sum(FIRST)
    return pl.pallas_call(
        _edges_kernel,
        in_specs=[pl.BlockSpec(memory_space=pl.ANY)] * 3,
        out_shape=[_sds(n, NG, G, RAD)] * 2,
        scratch_shapes=[
            pltpu.VMEM((AX, AZ, RAD), jnp.int32),
            pltpu.VMEM((2, AX, AZ, RAD), F32),
            pltpu.VMEM((AX, AZ, RAD), F32),
            pltpu.SemaphoreType.DMA((NG, 4)),
        ],
        compiler_params=_params(56),
        cost_estimate=_cost(2**20, 6 * 2**20),
        name="edge_layers",
    )(labels, exc, a)


def _prepare_kernel(lab_ref, exc_ref, a_ref, a_out, nu_out, oc_out, os_out, *rest):
    def group(g):
        at = _planes(g)
        lab = jnp.swapaxes(lab_ref[at], 0, 1)
        a_out[:, g] = jnp.swapaxes(a_ref[at], 0, 1)
        nu = _reluct(lab)
        oc = _driven(lab, jnp.swapaxes(exc_ref[0, at], 0, 1))
        os = _driven(lab, jnp.swapaxes(exc_ref[1, at], 0, 1))
        nu_out[:, g] = nu
        oc_out[:, g] = oc
        os_out[:, g] = os
        to = 0
        for x, n, m in zip((nu, oc, os), FIRST, REST):
            if m:
                rest[0][to : to + m, g] = x[n : n + m]
                rest[1][to : to + m, g] = x[AZ - n - m : AZ - n]
                to += m

    _loop(group)


def _prepare(labels, exc, a):
    n = sum(REST)
    return pl.pallas_call(
        _prepare_kernel,
        out_shape=[_sds(AZ, NG, G, RAD)] * 4 + ([_sds(n, NG, G, RAD)] * 2 if n else []),
        compiler_params=_params(),
        cost_estimate=_cost(2**22, 8 * 2**20),
        name="prepare",
    )(labels, exc, a)


def _labels_kernel(lab_ref, lt_out):
    def group(g):
        lab = lab_ref[_planes(g)].astype(F32)
        lt_out[:, g] = jnp.transpose(lab.reshape(G * AZ, RAD)).reshape(SEC, RL, G * AZ)

    _loop(group)


def _turned_labels(labels):
    return pl.pallas_call(
        _labels_kernel,
        out_shape=_sds(SEC, NG, RL, G * AZ),
        compiler_params=_params(),
        cost_estimate=_cost(2**22, 2 * 2**20),
        name="turned_labels",
    )(labels)


def _advance(first, width, a_rows, nu_of, oc_of, os_of, add_square, bufs):
    half = RAD // 2
    lane = lax.broadcasted_iota(jnp.int32, (G, half), 1)
    at_low, at_high = lane == 0, lane == half - 1

    def get(t, r):
        return a_rows(r) if t == 0 else bufs[(t - 1) % 2, r + KMAX]

    for t in range(width):
        phase = 2.0 * math.pi / PERIOD * (first + t)
        cc, ss = math.cos(phase), math.sin(phase)
        lo, hi = -width + 1 + t, AZ - 1 + width - 1 - t
        down, mid = get(t, lo - 1), get(t, lo)
        for r in range(lo, hi + 1):
            up = get(t, r + 1)
            m0, m1 = mid[:, :half], mid[:, half:]
            f0, f1 = pltpu.roll(m0, 1, 1), pltpu.roll(m1, 1, 1)
            b0, b1 = pltpu.roll(m0, half - 1, 1), pltpu.roll(m1, half - 1, 1)
            side0 = jnp.where(at_low, 0.0, f0) + jnp.where(at_high, b1, b0)
            side1 = jnp.where(at_low, f0, f1) + jnp.where(at_high, 0.0, b1)
            side = jnp.concatenate([side0, side1], axis=1)
            source = cc * oc_of(r) if first + t == 0 else cc * oc_of(r) + ss * os_of(r)
            change = nu_of(r) * ((down + up) + side - 4.0 * mid) + source
            new = mid + change
            if 0 <= r < AZ:
                add_square(t, r, change * change)
            bufs[t % 2, r + KMAX] = new
            down, mid = mid, up


def _phase_kernel(first, width, nextw, last, *refs):
    refs = list(refs)
    a_ref, low_ref, high_ref, nu_ref, oc_ref, os_ref, clow_ref, chigh_ref = refs[:8]
    refs = refs[8:]
    fresh = first == 0
    if not fresh:
        if any(REST):
            rlow_ref, rhigh_ref = refs[:2]
            refs = refs[2:]
        q_in, refs = refs[0], refs[1:]
    if last:
        lab_ref, a_out, d_out, dt_out, bufs, q_ref = refs
    else:
        a_out, q_ref, e_low, e_high, bufs = refs

    def group(g):
        def rows(r):
            if r < 0:
                return low_ref[width + r, g]
            if r >= AZ:
                return high_ref[r - AZ, g]
            return a_ref[r, g]

        def const(ref, k):
            n, m = FIRST[k], REST[k]
            at, rest_at = W0 + sum(FIRST[:k]), sum(REST[:k])

            def get(r):
                if 0 <= r < AZ:
                    return ref[r, g]
                if r < 0:
                    return clow_ref[at + n + r, g] if r >= -n else rlow_ref[rest_at + n + m + r, g]
                r -= AZ
                return chigh_ref[at + r, g] if r < n else rhigh_ref[rest_at + r - n, g]

            return get

        def slot(r):
            return (r,) if last else (r, g)

        def add_square(t, r, sq):
            if t > 0:
                sq = q_ref[slot(r)] + sq
            elif not fresh:
                sq = q_in[r, g] + sq
            q_ref[slot(r)] = sq

        _advance(first, width, rows, const(nu_ref, 0), const(oc_ref, 1), const(os_ref, 2), add_square, bufs)
        a = bufs[(width - 1) % 2, KMAX : KMAX + AZ]
        if last:
            at = _planes(g)
            a_out[at] = jnp.swapaxes(a, 0, 1)
            d = _sigma(lab_ref[at]) * jnp.swapaxes(q_ref[...], 0, 1)
            d_out[at] = d
            dt_out[:, g] = jnp.transpose(d.reshape(G * AZ, RAD)).reshape(SEC, RL, G * AZ)
        else:
            a_out[:, g] = a
            e_low[:, g] = a[0:nextw]
            e_high[:, g] = a[AZ - nextw :]

    _loop(group)


def _phase(index, a, low, high, consts, first_halo, rest_halo, q, labels):
    first, width = sum(WIDTHS[:index]), WIDTHS[index]
    last = index == len(WIDTHS) - 1
    nextw = None if last else WIDTHS[index + 1]
    ins = [a, low, high, *consts, *first_halo] + ([*rest_halo, q] if index else [])
    scratch = [pltpu.VMEM((2, AZ + 2 * KMAX, G, RAD), F32)]
    if last:
        ins.append(labels)
        outs = [_sds(AX, AZ, RAD), _sds(AX, AZ, RAD), _sds(SEC, NG, RL, G * AZ)]
        scratch.append(pltpu.VMEM((AZ, G, RAD), F32))
    else:
        outs = [_sds(AZ, NG, G, RAD)] * 2 + [_sds(nextw, NG, G, RAD)] * 2
    return pl.pallas_call(
        functools.partial(_phase_kernel, first, width, nextw, last),
        out_shape=outs,
        scratch_shapes=scratch,
        compiler_params=_params(),
        cost_estimate=_cost(2**24, 2**23),
        name=f"field_{index}",
    )(*ins)


def _gathered(x_ref, g):
    blk = lax.broadcasted_iota(jnp.int32, (RL, 128), 1) // AZ
    tiles = []
    for s in range(SEC // 8):
        x = [x_ref[s * 8 + j, g] for j in range(8)]
        for b in (4, 2, 1):
            keep = (blk & b) == 0
            for j in range(8):
                if j & b == 0:
                    p, q = x[j], x[j + b]
                    x[j] = jnp.where(keep, p, pltpu.roll(q, b * AZ, 1))
                    x[j + b] = jnp.where(keep, pltpu.roll(p, 128 - b * AZ, 1), q)
        tiles.append(x)
    return [jnp.concatenate([t[q] for t in tiles], axis=1) for q in range(8)]


def _half_cond(lab, temp):
    k0 = jnp.where(lab == 0.0, 1.0, jnp.where(lab == 1.0, 1.5, jnp.where(lab == 2.0, 0.1, 0.4)))
    return (0.5 * k0) * (1.0 + 0.5 * jnp.tanh(temp))


def _capacity(lab):
    return jnp.where(lab == 1.0, 3.5, jnp.where(lab == 2.0, 0.5, 3.0)).astype(F32)


def _store_edges(g, q, t, h, in_out, out_out, lo_out, hi_out):
    for k, x in enumerate((t, h)):
        in_out[k, g, q : q + 1, :] = x[0:1]
        out_out[k, g, q : q + 1, :] = x[RL - 1 :]
        if q == 0:

            @pl.when(g == 0)
            def _():
                lo_out[k] = x

        if q == G - 1:

            @pl.when(g == NG - 1)
            def _():
                hi_out[k] = x


_EDGES = [_sds(2, NG, G, ANG)] * 2 + [_sds(2, RL, ANG)] * 2


def _materials_kernel(x_ref, temp_ref, lab_out, h_out, *edges):
    def group(g):
        planes = _gathered(x_ref, g)
        for q in range(G):
            lab = planes[q]
            t = temp_ref[g * G + q]
            h = _half_cond(lab, t)
            lab_out[g * G + q] = lab
            h_out[g * G + q] = h
            _store_edges(g, q, t, h, *edges)

    _loop(group)


def _materials(x, temp):
    return pl.pallas_call(
        _materials_kernel,
        out_shape=[_sds(AX, RL, ANG)] * 2 + _EDGES,
        compiler_params=_params(),
        cost_estimate=_cost(2**22, 2**22),
        name="materials",
    )(x, temp)


def _first_kernel(x_ref, base_ref, gain_ref, lab_ref, d_out, temp_out, h_out, *edges):
    def group(g):
        planes = _gathered(x_ref, g)
        for q in range(G):
            at = g * G + q
            d = planes[q]
            t = base_ref[at] + d * gain_ref[at]
            h = _half_cond(lab_ref[at], t)
            d_out[at] = d
            temp_out[at] = t
            h_out[at] = h
            _store_edges(g, q, t, h, *edges)

    _loop(group)


def _first(x, base, gain, lab):
    return pl.pallas_call(
        _first_kernel,
        out_shape=[_sds(AX, RL, ANG)] * 3 + _EDGES,
        compiler_params=_params(),
        cost_estimate=_cost(2**22, 2**22),
        name="first_sweep",
    )(x, base, gain, lab)


def _faces(g, q, t_ref, h_ref, inner_ref, outer_ref, below_ref, above_ref):
    i = g * G + q
    row = lax.broadcasted_iota(jnp.int32, (RL, ANG), 0)

    def others(ref, k, x):
        lower = ref[i - 1] if q else jnp.where(g == 0, below_ref[k], ref[jnp.maximum(i - 1, 0)])
        upper = ref[i + 1] if q < G - 1 else jnp.where(g == NG - 1, above_ref[k], ref[jnp.minimum(i + 1, AX - 1)])
        inward = jnp.where(row == 0, inner_ref[k, g, q : q + 1, :], pltpu.roll(x, 1, 0))
        outward = jnp.where(row == RL - 1, outer_ref[k, g, q : q + 1, :], pltpu.roll(x, RL - 1, 0))
        return lower, upper, inward, outward, pltpu.roll(x, 1, 1), pltpu.roll(x, ANG - 1, 1)

    t, h = t_ref[i], h_ref[i]
    flux, total = None, None
    for tn, hn in zip(others(t_ref, 0, t), others(h_ref, 1, h)):
        kf = h + hn
        term = kf * (tn - t)
        flux = term if flux is None else flux + term
        total = kf if total is None else total + kf
    return t, flux, total


def _ready_kernel(t_ref, h_ref, inner_ref, outer_ref, below_ref, above_ref, lab_ref, base_out, gain_out):
    def group(g):
        for q in range(G):
            i = g * G + q
            t, flux, total = _faces(g, q, t_ref, h_ref, inner_ref, outer_ref, below_ref, above_ref)
            gain = 1.0 / (_capacity(lab_ref[i]) + total)
            base_out[i] = t + flux * gain
            gain_out[i] = gain

    _loop(group)


def _second_kernel(t_ref, h_ref, inner_ref, outer_ref, below_ref, above_ref, lab_ref, prior_ref, d_ref, out):
    def group(g):
        for q in range(G):
            i = g * G + q
            t, flux, total = _faces(g, q, t_ref, h_ref, inner_ref, outer_ref, below_ref, above_ref)
            cap = _capacity(lab_ref[i])
            mismatch = cap * (t - prior_ref[i]) - flux - d_ref[i]
            out[i] = t - mismatch / (cap + total)

    _loop(group)


def _whole(kernel, n_out, name, *ins):
    return pl.pallas_call(
        kernel,
        out_shape=[_sds(AX, RL, ANG)] * n_out,
        compiler_params=_params(),
        cost_estimate=_cost(2**24, 2**23),
        name=name,
    )(*ins)


def _ring(axis, x, step, closed):
    count = lax.axis_size(axis)
    if step > 0:
        perm = [(i, (i + 1) % count) for i in range(count if closed else count - 1)]
    else:
        perm = [((i + 1) % count, i) for i in range(count if closed else count - 1)]
    return lax.ppermute(x, axis, perm)


def _around(low_edge, high_edge):
    return _ring("sec", high_edge, 1, True), _ring("sec", low_edge, -1, True)


def _thermal_halo(inner_edge, outer_edge, lo_plane, hi_plane):
    inner = _ring("sec", outer_edge, 1, False)
    outer = _ring("sec", inner_edge, -1, False)
    below = _ring("ax", hi_plane, 1, False)
    above = _ring("ax", lo_plane, -1, False)
    return inner, outer, below, above


def shards(labels, exc, a0, prior):
    first_halo = _around(*_edges(labels, exc, a0))
    lt = _turned_labels(labels)
    lab_blocks = lax.all_to_all(lt, "sec", 0, 0)
    a, nu, oc, os, *rest = _prepare(labels, exc, a0)
    rest_halo = _around(*rest) if rest else ()
    low, high = first_halo
    q = None
    for index in range(len(WIDTHS)):
        outs = _phase(index, a, low, high, (nu, oc, os), first_halo, rest_halo, q, labels)
        if index < len(WIDTHS) - 1:
            a, q, *edges = outs
            low, high = _around(*edges)
    closing, dissipation, dt = outs
    lab, h0, *edges = _materials(lab_blocks, prior)
    halo0 = _thermal_halo(*edges)
    base, gain = _whole(_ready_kernel, 2, "first_ready", prior, h0, *halo0, lab)
    blocks = lax.all_to_all(dt, "sec", 0, 0)
    d, t1, h1, *edges = _first(blocks, base, gain, lab)
    halo1 = _thermal_halo(*edges)
    (t2,) = _whole(_second_kernel, 1, "second_sweep", t1, h1, *halo1, lab, prior, d)
    return closing, dissipation, t2


def solution(mesh):
    spec = P("ax", "sec", None)
    return jax.shard_map(
        shards,
        mesh=mesh,
        in_specs=(spec, P(None, "ax", "sec", None), spec, spec),
        out_specs=(spec, spec, spec),
        check_vma=False,
    )
```

time: 169 us -> 153 us (0.905)
  Pallas kernels: 43.6 us -> 32.1 us
  waiting for transfers between devices: 30.8 us -> 41.5 us
  local copies, waits for them, and re-layouts: 17 us -> 9.16 us
  starting transfers between devices: 75.8 us -> 68.4 us
    ppermute x16, waiting for transfers between devices: 30.8 us -> 41.5 us  [_ring(): return lax.ppermute(x, axis, perm)]
    pallas_call x2, Pallas kernels: 12.7 us -> 4.64 us  [_whole(): pl.pallas_call(kernel, out_shape=[_sds(AX, RL, ANG)] * n_out, compiler_pa...]
    unnamed x38 -> x20, local copies, waits for them, and re-layouts: 17 us -> 9.16 us
    all_to_all x1, starting transfers between devices: 13.6 us -> 9.63 us  [shards(): blocks = lax.all_to_all(dt, 'sec', 0, 0)]
    ppermute x16, starting transfers between devices: 55.5 us -> 52 us  [_ring(): return lax.ppermute(x, axis, perm)]
    pallas_call x4, Pallas kernels: 18.4 us -> 15.4 us  [_phase(): pl.pallas_call(functools.partial(_phase_kernel, first, width, nextw, last...]
    pallas_call x4 -> x5, Pallas kernels: 12.5 us -> 12.1 us  [the longest x1 3.81 us: _materials(): pl.pallas_call(_materials_kernel, out_shape=[_sds(AX, RL, ANG)] * 2 + _ED...]
  transfers between devices with their start and end apart: 18 -> 18, of which waited for: 7 -> 8; matrix products, arithmetic and copies ran while one was open for 0% -> 0% of each run, Pallas kernels for 18% -> 15%
where the time goes in v2:
time: 153 us; the launch traced here: 152 us
  starting transfers between devices  68.4 us (45%)
  waiting for transfers between devices  41.5 us (27%)
  Pallas kernels  32.1 us (21%)
  local copies, waits for them, and re-layouts  9.16 us (6%)
    ppermute x16, starting transfers between devices, _ring(): return lax.ppermute(x, axis, perm)  52 us
    ppermute x16, waiting for transfers between devices, _ring(): return lax.ppermute(x, axis, perm)  41.5 us
    pallas_call x4, Pallas kernels, _phase(): pl.pallas_call(functools.partial(_phase_kernel, first, width, nextw, last...  15.4 us
    all_to_all x1, starting transfers between devices, shards(): blocks = lax.all_to_all(dt, 'sec', 0, 0)  9.63 us
    unnamed x20, local copies, waits for them, and re-layouts  9.16 us
    all_to_all x1, starting transfers between devices, shards(): lab_blocks = lax.all_to_all(lt, 'sec', 0, 0)  6.78 us
    pallas_call x2, Pallas kernels, _whole(): pl.pallas_call(kernel, out_shape=[_sds(AX, RL, ANG)] * n_out, compiler_pa...  4.64 us
    pallas_call x1, Pallas kernels, _materials(): pl.pallas_call(_materials_kernel, out_shape=[_sds(AX, RL, ANG)] * 2 + _ED...  3.81 us
  transfers between devices with their start and end apart: 18, of which 8 were waited for; matrix products, arithmetic and copies ran while one was open for 0% of the time, Pallas kernels for 15%

profile of v2, /device:TPU:3, one launch (start us, length us, event | category | flops | bytes accessed | tf_op | source)
XLA Modules:
  0.0 152.0 jit_solution(6908648879655325864)
XLA Ops:
  0.6 3.8 %edge_layers.1 = (f32[13,8,8,256]{3,2,1,0:T(8,128)}, f32[13,8,8,256]{3,2,1,0:T(8,128)}) custom-call(s32[64,16,256]{2,1,0:T(8,128)} %lab_ref.3, f32[2,64,16,256]{3,2,1,0:T(8,128)} %exc_hbm.1, f32[64,16,256]{2,1,0:T(8,128)} %a_hbm.1), custom_call_target="tpu_custom_call" | custom-call | flops 1048576 | bytes 6291456 | tf_op jit(solution)/shard_map/edge_layers/pallas_call | solution.py:102
  4.4 1.7 %collective-permute-start = (f32[13,8,8,256]{3,2,1,0:T(8,128)}, f32[13,8,8,256]{3,2,1,0:T(8,128)S(1)}, u32[]{:S(2)}, u32[]{:S(2)}) collective-permute-start(f32[13,8,8,256]{3,2,1,0:T(8,128)} %get-tuple-element.40), channel_id=1, source_target_pairs={{0,4},{4,8},{8,12},{12,16},{16,20},{20,24},{24,28},{28,32},{32,36}... | collective-permute-start | bytes 2555912 | tf_op jit(solution)/shard_map/ppermute | solution.py:439
  6.1 3.2 %collective-permute-start.1 = (f32[13,8,8,256]{3,2,1,0:T(8,128)}, f32[13,8,8,256]{3,2,1,0:T(8,128)S(1)}, u32[]{:S(2)}, u32[]{:S(2)}) collective-permute-start(f32[13,8,8,256]{3,2,1,0:T(8,128)} %get-tuple-element.41), channel_id=1, source_target_pairs={{4,0},{8,4},{12,8},{16,12},{20,16},{24,20},{28,24},{32,28},{36,32}... | collective-permute-start | bytes 2555912 | tf_op jit(solution)/shard_map/ppermute | solution.py:439
  11.1 6.8 %all-to-all-start.1 = ((f32[32,8,8,128]{3,2,1,0:T(8,128)}), f32[32,8,8,128]{3,2,1,0:T(8,128)}, u32[]{:S(2)}, u32[]{:S(2)}) async-start(f32[32,8,8,128]{3,2,1,0:T(8,128)} %copy-done.3), calls=%async_computation.1 | async-start | bytes 2097152 | tf_op jit(solution)/shard_map/all_to_all | solution.py:457
  17.9 1.6 %copy-done.2 = f32[2,64,16,256]{3,2,1,0:T(8,128)S(1)} copy-done((f32[2,64,16,256]{3,2,1,0:T(8,128)S(1)}, f32[2,64,16,256]{3,2,1,0:T(8,128)}, u32[]{:S(2)}) %copy-start.2) | copy-done | bytes 2097176
  21.8 14.6 %collective-permute-done.refs_1_.refs_6_ = f32[13,8,8,256]{3,2,1,0:T(8,128)S(1)} collective-permute-done((f32[13,8,8,256]{3,2,1,0:T(8,128)}, f32[13,8,8,256]{3,2,1,0:T(8,128)S(1)}, u32[]{:S(2)}, u32[]{:S(2)}) %collective-permute-start) | collective-permute-done | bytes 852000 | tf_op jit(solution)/shard_map/ppermute | solution.py:439
  36.4 3.2 %field_0.1 = (f32[16,8,8,256]{3,2,1,0:T(8,128)S(1)}, f32[16,8,8,256]{3,2,1,0:T(8,128)S(1)}, f32[4,8,8,256]{3,2,1,0:T(8,128)S(1)}, f32[4,8,8,256]{3,2,1,0:T(8,128)S(1)}) custom-call(f32[16,8,8,256]{3,2,1,0:T(8,128)S(1)} %get-tuple-element.39.refs_0_, f32[13,8,8,256]{3,2,1,0:T(8,128)S(1)} %collective-permute-done.refs_1_.refs_6_, ...), custom_call_target="tpu_custom_call" | custom-call | flops 16777216 | bytes 8388608 | tf_op jit(solution)/shard_map/field_0/pallas_call | solution.py:273
  39.7 4.7 %collective-permute-start.3 = (f32[4,8,8,256]{3,2,1,0:T(8,128)S(1)}, f32[4,8,8,256]{3,2,1,0:T(8,128)S(1)}, u32[]{:S(2)}, u32[]{:S(2)}) collective-permute-start(f32[4,8,8,256]{3,2,1,0:T(8,128)S(1)} %get-tuple-element.47), channel_id=1, source_target_pairs={{4,0},{8,4},{12,8},{16,12},{20,16},{24,20},{28,24},{32,28},{36,32}... | collective-permute-start | bytes 786440 | tf_op jit(solution)/shard_map/ppermute | solution.py:439
  44.4 5.9 %collective-permute-done.2.refs_1_ = f32[4,8,8,256]{3,2,1,0:T(8,128)S(1)} collective-permute-done((f32[4,8,8,256]{3,2,1,0:T(8,128)S(1)}, f32[4,8,8,256]{3,2,1,0:T(8,128)S(1)}, u32[]{:S(2)}, u32[]{:S(2)}) %collective-permute-start.2) | collective-permute-done | bytes 262176 | tf_op jit(solution)/shard_map/ppermute | solution.py:439
  50.3 2.3 %collective-permute-done.3.refs_2_ = f32[4,8,8,256]{3,2,1,0:T(8,128)S(1)} collective-permute-done((f32[4,8,8,256]{3,2,1,0:T(8,128)S(1)}, f32[4,8,8,256]{3,2,1,0:T(8,128)S(1)}, u32[]{:S(2)}, u32[]{:S(2)}) %collective-permute-start.3) | collective-permute-done | bytes 262176 | tf_op jit(solution)/shard_map/ppermute | solution.py:439
  52.6 3.3 %field_1.1 = (f32[16,8,8,256]{3,2,1,0:T(8,128)S(1)}, f32[16,8,8,256]{3,2,1,0:T(8,128)S(1)}, f32[4,8,8,256]{3,2,1,0:T(8,128)S(1)}, f32[4,8,8,256]{3,2,1,0:T(8,128)S(1)}) custom-call(f32[16,8,8,256]{3,2,1,0:T(8,128)S(1)} %get-tuple-element.45.refs_0_, f32[4,8,8,256]{3,2,1,0:T(8,128)S(1)} %collective-permute-done.2.refs_1_, ...), custom_call_target="tpu_custom_call" | custom-call | flops 16777216 | bytes 8388608 | tf_op jit(solution)/shard_map/field_1/pallas_call | solution.py:273
  55.9 5.3 %collective-permute-start.5 = (f32[4,8,8,256]{3,2,1,0:T(8,128)S(1)}, f32[4,8,8,256]{3,2,1,0:T(8,128)S(1)}, u32[]{:S(2)}, u32[]{:S(2)}) collective-permute-start(f32[4,8,8,256]{3,2,1,0:T(8,128)S(1)} %get-tuple-element.51), channel_id=1, source_target_pairs={{4,0},{8,4},{12,8},{16,12},{20,16},{24,20},{28,24},{32,28},{36,32}... | collective-permute-start | bytes 786440 | tf_op jit(solution)/shard_map/ppermute | solution.py:439
  61.2 5.0 %collective-permute-done.4.refs_1_ = f32[4,8,8,256]{3,2,1,0:T(8,128)S(1)} collective-permute-done((f32[4,8,8,256]{3,2,1,0:T(8,128)S(1)}, f32[4,8,8,256]{3,2,1,0:T(8,128)S(1)}, u32[]{:S(2)}, u32[]{:S(2)}) %collective-permute-start.4) | collective-permute-done | bytes 262176 | tf_op jit(solution)/shard_map/ppermute | solution.py:439
  66.2 3.3 %field_2.1 = (f32[16,8,8,256]{3,2,1,0:T(8,128)S(1)}, f32[16,8,8,256]{3,2,1,0:T(8,128)S(1)}, f32[4,8,8,256]{3,2,1,0:T(8,128)S(1)}, f32[4,8,8,256]{3,2,1,0:T(8,128)S(1)}) custom-call(f32[16,8,8,256]{3,2,1,0:T(8,128)S(1)} %get-tuple-element.49.refs_0_, f32[4,8,8,256]{3,2,1,0:T(8,128)S(1)} %collective-permute-done.4.refs_1_, ...), custom_call_target="tpu_custom_call" | custom-call | flops 16777216 | bytes 8388608 | tf_op jit(solution)/shard_map/field_2/pallas_call | solution.py:273
  69.6 4.5 %collective-permute-start.7 = (f32[4,8,8,256]{3,2,1,0:T(8,128)S(1)}, f32[4,8,8,256]{3,2,1,0:T(8,128)S(1)}, u32[]{:S(2)}, u32[]{:S(2)}) collective-permute-start(f32[4,8,8,256]{3,2,1,0:T(8,128)S(1)} %get-tuple-element.55), channel_id=1, source_target_pairs={{4,0},{8,4},{12,8},{16,12},{20,16},{24,20},{28,24},{32,28},{36,32}... | collective-permute-start | bytes 786440 | tf_op jit(solution)/shard_map/ppermute | solution.py:439
  74.0 4.1 %collective-permute-done.6.refs_1_ = f32[4,8,8,256]{3,2,1,0:T(8,128)S(1)} collective-permute-done((f32[4,8,8,256]{3,2,1,0:T(8,128)S(1)}, f32[4,8,8,256]{3,2,1,0:T(8,128)S(1)}, u32[]{:S(2)}, u32[]{:S(2)}) %collective-permute-start.6) | collective-permute-done | bytes 262176 | tf_op jit(solution)/shard_map/ppermute | solution.py:439
  78.2 5.6 %field_3.1 = (f32[64,16,256]{2,1,0:T(8,128)}, f32[64,16,256]{2,1,0:T(8,128)}, f32[32,8,8,128]{3,2,1,0:T(8,128)S(1)}) custom-call(f32[16,8,8,256]{3,2,1,0:T(8,128)S(1)} %get-tuple-element.53.refs_0_, f32[4,8,8,256]{3,2,1,0:T(8,128)S(1)} %collective-permute-done.6.refs_1_, f32[4,8,8,256]{3,2,1,0:T(8,128)S(1)} %collective-permute-done.7.refs_2_, ...), custom_call_target="tpu_custom_call" | custom-call | flops 16777216 | bytes 8388608 | tf_op jit(solution)/shard_map/field_3/pallas_call | solution.py:273
  84.8 9.6 %all-to-all-start = ((f32[32,8,8,128]{3,2,1,0:T(8,128)}), f32[32,8,8,128]{3,2,1,0:T(8,128)S(1)}, u32[]{:S(2)}, u32[]{:S(2)}) async-start(f32[32,8,8,128]{3,2,1,0:T(8,128)} %copy-done.5), calls=%async_computation | async-start | bytes 2097152 | tf_op jit(solution)/shard_map/all_to_all | solution.py:471
  94.4 3.8 %materials.1 = (f32[64,8,512]{2,1,0:T(8,128)S(1)}, f32[64,8,512]{2,1,0:T(8,128)S(1)}, f32[2,8,8,512]{3,2,1,0:T(8,128)S(1)}, f32[2,8,8,512]{3,2,1,0:T(8,128)S(1)}...) custom-call(f32[32,8,8,128]{3,2,1,0:T(8,128)} %all-to-all-done.1.x_ref, f32[64,8,512]{2,1,0:T(8,128)S(1)} %copy-done.1), custom_call_target="tpu_custom_call" | custom-call | flops 4194304 | bytes 4194304 | tf_op jit(solution)/shard_map/materials/pallas_call | solution.py:343
  98.2 3.1 %collective-permute-start.8 = (f32[2,8,8,512]{3,2,1,0:T(8,128)S(1)}, f32[2,8,8,512]{3,2,1,0:T(8,128)S(1)}, u32[]{:S(2)}, u32[]{:S(2)}) collective-permute-start(f32[2,8,8,512]{3,2,1,0:T(8,128)S(1)} %get-tuple-element.61), channel_id=1, source_target_pairs={{0,4},{4,8},{8,12},{12,16},{16,20},{20,24},{24,28},{28,32},{32,36}... | collective-permute-start | bytes 786440 | tf_op jit(solution)/shard_map/ppermute | solution.py:439
  101.3 5.2 %collective-permute-start.9 = (f32[2,8,8,512]{3,2,1,0:T(8,128)S(1)}, f32[2,8,8,512]{3,2,1,0:T(8,128)S(1)}, u32[]{:S(2)}, u32[]{:S(2)}) collective-permute-start(f32[2,8,8,512]{3,2,1,0:T(8,128)S(1)} %get-tuple-element.62), channel_id=1, source_target_pairs={{4,0},{8,4},{12,8},{16,12},{20,16},{24,20},{28,24},{32,28},{36,32}... | collective-permute-start | bytes 786440 | tf_op jit(solution)/shard_map/ppermute | solution.py:439
  106.5 9.5 %collective-permute-start.10 = (f32[2,8,512]{2,1,0:T(8,128)S(1)}, f32[2,8,512]{2,1,0:T(8,128)S(1)}, u32[]{:S(2)}, u32[]{:S(2)}) collective-permute-start(f32[2,8,512]{2,1,0:T(8,128)S(1)} %get-tuple-element.63), channel_id=1, source_target_pairs={{0,1},{1,2},{2,3},{4,5},{5,6},{6,7},{8,9},{9,10},{10,11},{12,13},{... | collective-permute-start | bytes 98312 | tf_op jit(solution)/shard_map/ppermute | solution.py:439
  116.0 1.9 %collective-permute-start.11 = (f32[2,8,512]{2,1,0:T(8,128)S(1)}, f32[2,8,512]{2,1,0:T(8,128)S(1)}, u32[]{:S(2)}, u32[]{:S(2)}) collective-permute-start(f32[2,8,512]{2,1,0:T(8,128)S(1)} %get-tuple-element.64), channel_id=1, source_target_pairs={{1,0},{2,1},{3,2},{5,4},{6,5},{7,6},{9,8},{10,9},{11,10},{13,12},{... | collective-permute-start | bytes 98312 | tf_op jit(solution)/shard_map/ppermute | solution.py:439
  118.0 4.8 %collective-permute-done.11.above_ref = f32[2,8,512]{2,1,0:T(8,128)S(1)} collective-permute-done((f32[2,8,512]{2,1,0:T(8,128)S(1)}, f32[2,8,512]{2,1,0:T(8,128)S(1)}, u32[]{:S(2)}, u32[]{:S(2)}) %collective-permute-start.11) | collective-permute-done | bytes 32800 | tf_op jit(solution)/shard_map/ppermute | solution.py:439
  122.8 1.8 %first_ready.1 = (f32[64,8,512]{2,1,0:T(8,128)S(1)}, f32[64,8,512]{2,1,0:T(8,128)S(1)}) custom-call(f32[64,8,512]{2,1,0:T(8,128)S(1)} %copy-done.1, f32[64,8,512]{2,1,0:T(8,128)S(1)} %get-tuple-element.60.h_ref, f32[2,8,8,512]{3,2,1,0:T(8,128)S(1)} %collective-permute-done.8.inner_ref, f32[2,8,8,512]{3,2,1,0:T(8,128)S(1)} %collective-permute-done.9.outer_ref, ...), custom_call_target="tpu_custom_call" | custom-call | flops 16777216 | bytes 8388608 | tf_op jit(solution)/shard_map/first_ready/pallas_call | solution.py:424
  129.0 2.7 %first_sweep.1 = (f32[64,8,512]{2,1,0:T(8,128)S(1)}, f32[64,8,512]{2,1,0:T(8,128)S(1)}, f32[64,8,512]{2,1,0:T(8,128)S(1)}, f32[2,8,8,512]{3,2,1,0:T(8,128)S(1)},...) custom-call(f32[32,8,8,128]{3,2,1,0:T(8,128)S(1)} %all-to-all-done.x_ref, ...), custom_call_target="tpu_custom_call" | custom-call | flops 4194304 | bytes 4194304 | tf_op jit(solution)/shard_map/first_sweep/pallas_call | solution.py:369
  131.6 1.9 %collective-permute-start.12 = (f32[2,8,8,512]{3,2,1,0:T(8,128)S(1)}, f32[2,8,8,512]{3,2,1,0:T(8,128)S(1)}, u32[]{:S(2)}, u32[]{:S(2)}) collective-permute-start(f32[2,8,8,512]{3,2,1,0:T(8,128)S(1)} %get-tuple-element.70), channel_id=1, source_target_pairs={{0,4},{4,8},{8,12},{12,16},{16,20},{20,24},{24,28},{28,32},{32,36}... | collective-permute-start | bytes 786440 | tf_op jit(solution)/shard_map/ppermute | solution.py:439
  133.6 6.4 %collective-permute-start.13 = (f32[2,8,8,512]{3,2,1,0:T(8,128)S(1)}, f32[2,8,8,512]{3,2,1,0:T(8,128)S(1)}, u32[]{:S(2)}, u32[]{:S(2)}) collective-permute-start(f32[2,8,8,512]{3,2,1,0:T(8,128)S(1)} %get-tuple-element.71), channel_id=1, source_target_pairs={{4,0},{8,4},{12,8},{16,12},{20,16},{24,20},{28,24},{32,28},{36,32}... | collective-permute-start | bytes 786440 | tf_op jit(solution)/shard_map/ppermute | solution.py:439
  139.9 2.5 %collective-permute-start.14 = (f32[2,8,512]{2,1,0:T(8,128)S(1)}, f32[2,8,512]{2,1,0:T(8,128)S(1)}, u32[]{:S(2)}, u32[]{:S(2)}) collective-permute-start(f32[2,8,512]{2,1,0:T(8,128)S(1)} %get-tuple-element.72), channel_id=1, source_target_pairs={{0,1},{1,2},{2,3},{4,5},{5,6},{6,7},{8,9},{9,10},{10,11},{12,13},{... | collective-permute-start | bytes 98312 | tf_op jit(solution)/shard_map/ppermute | solution.py:439
  142.4 1.9 %collective-permute-start.15 = (f32[2,8,512]{2,1,0:T(8,128)S(1)}, f32[2,8,512]{2,1,0:T(8,128)S(1)}, u32[]{:S(2)}, u32[]{:S(2)}) collective-permute-start(f32[2,8,512]{2,1,0:T(8,128)S(1)} %get-tuple-element.73), channel_id=1, source_target_pairs={{1,0},{2,1},{3,2},{5,4},{6,5},{7,6},{9,8},{10,9},{11,10},{13,12},{... | collective-permute-start | bytes 98312 | tf_op jit(solution)/shard_map/ppermute | solution.py:439
  144.5 4.7 %collective-permute-done.15.above_ref = f32[2,8,512]{2,1,0:T(8,128)S(1)} collective-permute-done((f32[2,8,512]{2,1,0:T(8,128)S(1)}, f32[2,8,512]{2,1,0:T(8,128)S(1)}, u32[]{:S(2)}, u32[]{:S(2)}) %collective-permute-start.15) | collective-permute-done | bytes 32800 | tf_op jit(solution)/shard_map/ppermute | solution.py:439
  149.2 2.9 %second_sweep.1 = f32[64,8,512]{2,1,0:T(8,128)} custom-call(f32[64,8,512]{2,1,0:T(8,128)S(1)} %get-tuple-element.68.t_ref, f32[64,8,512]{2,1,0:T(8,128)S(1)} %get-tuple-element.69.h_ref, f32[2,8,8,512]{3,2,1,0:T(8,128)S(1)} %collective-permute-done.12.inner_ref, f32[2,8,8,512]{3,2,1,0:T(8,128)S(1)} %collective-permute-done.13.outer_ref, ...), custom_call_target="tpu_custom_call" | custom-call | flops 16777216 | bytes 8388608 | tf_op jit(solution)/shard_map/second_sweep/pallas_call | solution.py:424
  (35 shorter events, 9.8 us)
Async XLA Ops:
  0.6 8.7 %copy-start = (s32[64,16,256]{2,1,0:T(8,128)S(1)}, s32[64,16,256]{2,1,0:T(8,128)}, u32[]{:S(2)}) copy-start(s32[64,16,256]{2,1,0:T(8,128)} %lab_ref.3) | copy-start | bytes 3145732
  4.4 31.9 %collective-permute-start = (f32[13,8,8,256]{3,2,1,0:T(8,128)}, f32[13,8,8,256]{3,2,1,0:T(8,128)S(1)}, u32[]{:S(2)}, u32[]{:S(2)}) collective-permute-start(f32[13,8,8,256]{3,2,1,0:T(8,128)} %get-tuple-element.40), channel_id=1, source_target_pairs={{0,4},{4,8},{8,12},{12,16},{16,20},{20,24},{24,28},{28,32},{32,36}... | collective-permute-start | bytes 2555912 | tf_op jit(solution)/shard_map/ppermute | solution.py:439
  6.1 30.2 %collective-permute-start.1 = (f32[13,8,8,256]{3,2,1,0:T(8,128)}, f32[13,8,8,256]{3,2,1,0:T(8,128)S(1)}, u32[]{:S(2)}, u32[]{:S(2)}) collective-permute-start(f32[13,8,8,256]{3,2,1,0:T(8,128)} %get-tuple-element.41), channel_id=1, source_target_pairs={{4,0},{8,4},{12,8},{16,12},{20,16},{24,20},{28,24},{32,28},{36,32}... | collective-permute-start | bytes 2555912 | tf_op jit(solution)/shard_map/ppermute | solution.py:439
  10.1 1.0 copy-start.3
  11.1 73.6 %all-to-all-start.1 = ((f32[32,8,8,128]{3,2,1,0:T(8,128)}), f32[32,8,8,128]{3,2,1,0:T(8,128)}, u32[]{:S(2)}, u32[]{:S(2)}) async-start(f32[32,8,8,128]{3,2,1,0:T(8,128)} %copy-done.3), calls=%async_computation.1 | async-start | bytes 2097152 | tf_op jit(solution)/shard_map/all_to_all | solution.py:457
  17.9 1.6 %copy-start.2 = (f32[2,64,16,256]{3,2,1,0:T(8,128)S(1)}, f32[2,64,16,256]{3,2,1,0:T(8,128)}, u32[]{:S(2)}) copy-start(f32[2,64,16,256]{3,2,1,0:T(8,128)} %exc_hbm.1) | copy-start | bytes 6291460
  19.5 1.2 copy-start.4
  39.6 10.7 %collective-permute-start.2 = (f32[4,8,8,256]{3,2,1,0:T(8,128)S(1)}, f32[4,8,8,256]{3,2,1,0:T(8,128)S(1)}, u32[]{:S(2)}, u32[]{:S(2)}) collective-permute-start(f32[4,8,8,256]{3,2,1,0:T(8,128)S(1)} %get-tuple-element.46), channel_id=1, source_target_pairs={{0,4},{4,8},{8,12},{12,16},{16,20},{20,24},{24,28},{28,32},{32,36}... | collective-permute-start | bytes 786440 | tf_op jit(solution)/shard_map/ppermute | solution.py:439
  39.7 12.9 %collective-permute-start.3 = (f32[4,8,8,256]{3,2,1,0:T(8,128)S(1)}, f32[4,8,8,256]{3,2,1,0:T(8,128)S(1)}, u32[]{:S(2)}, u32[]{:S(2)}) collective-permute-start(f32[4,8,8,256]{3,2,1,0:T(8,128)S(1)} %get-tuple-element.47), channel_id=1, source_target_pairs={{4,0},{8,4},{12,8},{16,12},{20,16},{24,20},{28,24},{32,28},{36,32}... | collective-permute-start | bytes 786440 | tf_op jit(solution)/shard_map/ppermute | solution.py:439
  55.9 10.3 %collective-permute-start.4 = (f32[4,8,8,256]{3,2,1,0:T(8,128)S(1)}, f32[4,8,8,256]{3,2,1,0:T(8,128)S(1)}, u32[]{:S(2)}, u32[]{:S(2)}) collective-permute-start(f32[4,8,8,256]{3,2,1,0:T(8,128)S(1)} %get-tuple-element.50), channel_id=1, source_target_pairs={{0,4},{4,8},{8,12},{12,16},{16,20},{20,24},{24,28},{28,32},{32,36}... | collective-permute-start | bytes 786440 | tf_op jit(solution)/shard_map/ppermute | solution.py:439
  55.9 10.3 %collective-permute-start.5 = (f32[4,8,8,256]{3,2,1,0:T(8,128)S(1)}, f32[4,8,8,256]{3,2,1,0:T(8,128)S(1)}, u32[]{:S(2)}, u32[]{:S(2)}) collective-permute-start(f32[4,8,8,256]{3,2,1,0:T(8,128)S(1)} %get-tuple-element.51), channel_id=1, source_target_pairs={{4,0},{8,4},{12,8},{16,12},{20,16},{24,20},{28,24},{32,28},{36,32}... | collective-permute-start | bytes 786440 | tf_op jit(solution)/shard_map/ppermute | solution.py:439
  69.5 8.7 %collective-permute-start.6 = (f32[4,8,8,256]{3,2,1,0:T(8,128)S(1)}, f32[4,8,8,256]{3,2,1,0:T(8,128)S(1)}, u32[]{:S(2)}, u32[]{:S(2)}) collective-permute-start(f32[4,8,8,256]{3,2,1,0:T(8,128)S(1)} %get-tuple-element.54), channel_id=1, source_target_pairs={{0,4},{4,8},{8,12},{12,16},{16,20},{20,24},{24,28},{28,32},{32,36}... | collective-permute-start | bytes 786440 | tf_op jit(solution)/shard_map/ppermute | solution.py:439
  69.6 8.6 %collective-permute-start.7 = (f32[4,8,8,256]{3,2,1,0:T(8,128)S(1)}, f32[4,8,8,256]{3,2,1,0:T(8,128)S(1)}, u32[]{:S(2)}, u32[]{:S(2)}) collective-permute-start(f32[4,8,8,256]{3,2,1,0:T(8,128)S(1)} %get-tuple-element.55), channel_id=1, source_target_pairs={{4,0},{8,4},{12,8},{16,12},{20,16},{24,20},{28,24},{32,28},{36,32}... | collective-permute-start | bytes 786440 | tf_op jit(solution)/shard_map/ppermute | solution.py:439
  83.8 1.0 copy-start.5
  84.8 9.6 %copy-start.1 = (f32[64,8,512]{2,1,0:T(8,128)S(1)}, f32[64,8,512]{2,1,0:T(8,128)}, u32[]{:S(2)}) copy-start(f32[64,8,512]{2,1,0:T(8,128)} %prior_ref.1) | copy-start | bytes 3145732
  84.8 41.8 %all-to-all-start = ((f32[32,8,8,128]{3,2,1,0:T(8,128)}), f32[32,8,8,128]{3,2,1,0:T(8,128)S(1)}, u32[]{:S(2)}, u32[]{:S(2)}) async-start(f32[32,8,8,128]{3,2,1,0:T(8,128)} %copy-done.5), calls=%async_computation | async-start | bytes 2097152 | tf_op jit(solution)/shard_map/all_to_all | solution.py:471
  98.2 24.6 %collective-permute-start.8 = (f32[2,8,8,512]{3,2,1,0:T(8,128)S(1)}, f32[2,8,8,512]{3,2,1,0:T(8,128)S(1)}, u32[]{:S(2)}, u32[]{:S(2)}) collective-permute-start(f32[2,8,8,512]{3,2,1,0:T(8,128)S(1)} %get-tuple-element.61), channel_id=1, source_target_pairs={{0,4},{4,8},{8,12},{12,16},{16,20},{20,24},{24,28},{28,32},{32,36}... | collective-permute-start | bytes 786440 | tf_op jit(solution)/shard_map/ppermute | solution.py:439
  101.3 21.5 %collective-permute-start.9 = (f32[2,8,8,512]{3,2,1,0:T(8,128)S(1)}, f32[2,8,8,512]{3,2,1,0:T(8,128)S(1)}, u32[]{:S(2)}, u32[]{:S(2)}) collective-permute-start(f32[2,8,8,512]{3,2,1,0:T(8,128)S(1)} %get-tuple-element.62), channel_id=1, source_target_pairs={{4,0},{8,4},{12,8},{16,12},{20,16},{24,20},{28,24},{32,28},{36,32}... | collective-permute-start | bytes 786440 | tf_op jit(solution)/shard_map/ppermute | solution.py:439
  106.5 11.4 %collective-permute-start.10 = (f32[2,8,512]{2,1,0:T(8,128)S(1)}, f32[2,8,512]{2,1,0:T(8,128)S(1)}, u32[]{:S(2)}, u32[]{:S(2)}) collective-permute-start(f32[2,8,512]{2,1,0:T(8,128)S(1)} %get-tuple-element.63), channel_id=1, source_target_pairs={{0,1},{1,2},{2,3},{4,5},{5,6},{6,7},{8,9},{9,10},{10,11},{12,13},{... | collective-permute-start | bytes 98312 | tf_op jit(solution)/shard_map/ppermute | solution.py:439
  116.0 6.7 %collective-permute-start.11 = (f32[2,8,512]{2,1,0:T(8,128)S(1)}, f32[2,8,512]{2,1,0:T(8,128)S(1)}, u32[]{:S(2)}, u32[]{:S(2)}) collective-permute-start(f32[2,8,512]{2,1,0:T(8,128)S(1)} %get-tuple-element.64), channel_id=1, source_target_pairs={{1,0},{2,1},{3,2},{5,4},{6,5},{7,6},{9,8},{10,9},{11,10},{13,12},{... | collective-permute-start | bytes 98312 | tf_op jit(solution)/shard_map/ppermute | solution.py:439
  124.6 1.0 copy-start.6
  125.5 1.0 copy-start.8
  126.5 1.2 copy-start.7
  127.8 1.2 copy-start.9
  131.6 17.5 %collective-permute-start.12 = (f32[2,8,8,512]{3,2,1,0:T(8,128)S(1)}, f32[2,8,8,512]{3,2,1,0:T(8,128)S(1)}, u32[]{:S(2)}, u32[]{:S(2)}) collective-permute-start(f32[2,8,8,512]{3,2,1,0:T(8,128)S(1)} %get-tuple-element.70), channel_id=1, source_target_pairs={{0,4},{4,8},{8,12},{12,16},{16,20},{20,24},{24,28},{28,32},{32,36}... | collective-permute-start | bytes 786440 | tf_op jit(solution)/shard_map/ppermute | solution.py:439
  133.6 15.6 %collective-permute-start.13 = (f32[2,8,8,512]{3,2,1,0:T(8,128)S(1)}, f32[2,8,8,512]{3,2,1,0:T(8,128)S(1)}, u32[]{:S(2)}, u32[]{:S(2)}) collective-permute-start(f32[2,8,8,512]{3,2,1,0:T(8,128)S(1)} %get-tuple-element.71), channel_id=1, source_target_pairs={{4,0},{8,4},{12,8},{16,12},{20,16},{24,20},{28,24},{32,28},{36,32}... | collective-permute-start | bytes 786440 | tf_op jit(solution)/shard_map/ppermute | solution.py:439
  139.9 4.5 %collective-permute-start.14 = (f32[2,8,512]{2,1,0:T(8,128)S(1)}, f32[2,8,512]{2,1,0:T(8,128)S(1)}, u32[]{:S(2)}, u32[]{:S(2)}) collective-permute-start(f32[2,8,512]{2,1,0:T(8,128)S(1)} %get-tuple-element.72), channel_id=1, source_target_pairs={{0,1},{1,2},{2,3},{4,5},{5,6},{6,7},{8,9},{9,10},{10,11},{12,13},{... | collective-permute-start | bytes 98312 | tf_op jit(solution)/shard_map/ppermute | solution.py:439
  142.4 6.7 %collective-permute-start.15 = (f32[2,8,512]{2,1,0:T(8,128)S(1)}, f32[2,8,512]{2,1,0:T(8,128)S(1)}, u32[]{:S(2)}, u32[]{:S(2)}) collective-permute-start(f32[2,8,512]{2,1,0:T(8,128)S(1)} %get-tuple-element.73), channel_id=1, source_target_pairs={{1,0},{2,1},{3,2},{5,4},{6,5},{7,6},{9,8},{10,9},{11,10},{13,12},{... | collective-permute-start | bytes 98312 | tf_op jit(solution)/shard_map/ppermute | solution.py:439

commit v3 on v0

v3 whole, which is shorter than its diff:
```python
import functools
import math

import jax
import jax.numpy as jnp
from jax import lax
from jax.experimental import pallas as pl
from jax.experimental.pallas import tpu as pltpu
from jax.sharding import PartitionSpec as P

SAMPLES = 16
PERIOD = 32
WIDTHS = (5, 4, 4, 3)
REACH = (5, 4, 4, 4)
PRIOR_AT = 2
H0 = REACH[0]
HMAX = max(REACH)
C = HMAX - 1
LAYERS = (C, C, C - 1)
AT = (H0, H0 + C, H0 + 2 * C)
NSEND = H0 + sum(LAYERS)

F32 = jnp.float32
AX, AZ, RAD, ANG = 64, 16, 256, 512
SEC = 32
RL = RAD // SEC
G = 8
NG = AX // G
ENDS = (0, NG - 1)
HALF = RAD // 2


def _params(mib=16):
    return pltpu.CompilerParams(vmem_limit_bytes=mib * 2**20)


def _sds(*shape):
    return jax.ShapeDtypeStruct(shape, F32)


def _cost(flops, nbytes):
    return pl.CostEstimate(flops=flops, bytes_accessed=nbytes, transcendentals=0)


def _loop(n, body):
    def step(i, _):
        body(i)
        return 0

    lax.fori_loop(0, n, step, 0)


def _planes(g):
    return pl.ds(pl.multiple_of(g * G, G), G)


def _reluct(lab):
    return jnp.where(lab == 0, 0.05, jnp.where(lab == 3, 0.2, 0.24)).astype(F32)


def _sigma(lab):
    return jnp.where(lab == 0, 0.3, jnp.where(lab == 1, 1.0, jnp.where(lab == 2, 0.0, 0.6))).astype(F32)


def _driven(lab, x):
    return jnp.where((lab == 1) | (lab == 3), x, 0.0)


def _half_cond(lab, temp):
    half_k0 = jnp.where(lab == 0, 0.5, jnp.where(lab == 1, 0.75, jnp.where(lab == 2, 0.05, 0.2)))
    return half_k0 * (1.0 + 0.5 * jnp.tanh(temp))


def _capacity(lab):
    return jnp.where(lab == 1, 3.5, jnp.where(lab == 2, 0.5, 3.0)).astype(F32)


def _send_layers(store, high, a, lab, c, s):
    def edge(x, n):
        return x[AZ - n :] if high else x[:n]

    store(0, edge(a, H0))
    store(AT[0], edge(lab, LAYERS[0]).astype(F32))
    store(AT[1], _driven(edge(lab, LAYERS[1]), edge(c, LAYERS[1])))
    store(AT[2], _driven(edge(lab, LAYERS[2]), edge(s, LAYERS[2])))


def _edges_kernel(lab_hbm, exc_hbm, a_hbm, low_ref, high_ref, lab_v, exc_v, a_v, sems):
    copies = []
    for g in range(NG):
        at = pl.ds(g * G, G)
        copies.append(
            [
                pltpu.make_async_copy(lab_hbm.at[at], lab_v.at[at], sems.at[g, 0]),
                pltpu.make_async_copy(exc_hbm.at[0, at], exc_v.at[0, at], sems.at[g, 1]),
                pltpu.make_async_copy(exc_hbm.at[1, at], exc_v.at[1, at], sems.at[g, 2]),
                pltpu.make_async_copy(a_hbm.at[at], a_v.at[at], sems.at[g, 3]),
            ]
        )
        for copy in copies[-1]:
            copy.start()

    def group(g, a, c, s, lab):
        for out, high in ((low_ref, False), (high_ref, True)):

            def store(k, x, out=out):
                out[k : k + x.shape[0], g] = x

            _send_layers(store, high, a, lab, c, s)

    for g in range(NG):
        for copy in copies[g]:
            copy.wait()
        at = pl.ds(g * G, G)
        group(g, *[jnp.swapaxes(x, 0, 1) for x in (a_v[at], exc_v[0, at], exc_v[1, at], lab_v[at])])


def _edges(labels, exc, a):
    return pl.pallas_call(
        _edges_kernel,
        in_specs=[pl.BlockSpec(memory_space=pl.ANY)] * 3,
        out_shape=[_sds(NSEND, NG, G, RAD)] * 2,
        scratch_shapes=[
            pltpu.VMEM((AX, AZ, RAD), jnp.int32),
            pltpu.VMEM((2, AX, AZ, RAD), F32),
            pltpu.VMEM((AX, AZ, RAD), F32),
            pltpu.SemaphoreType.DMA((NG, 4)),
        ],
        compiler_params=_params(56),
        cost_estimate=_cost(2**20, 6 * 2**20),
        name="edge_layers",
    )(labels, exc, a)


def _prepare_kernel(lab_ref, exc_ref, a_ref, a_out, lab_out, nu_out, oc_out, os_out):
    def group(g, a, c, s, lab):
        a_out[:, g] = a
        lab_out[:, g] = lab.astype(F32)
        nu_out[:, g] = _reluct(lab)
        oc_out[:, g] = _driven(lab, c)
        os_out[:, g] = _driven(lab, s)

    def own(g):
        at = _planes(g)
        group(g, *[jnp.swapaxes(x, 0, 1) for x in (a_ref[at], exc_ref[0, at], exc_ref[1, at], lab_ref[at])])

    _loop(NG, own)


def _prepare(labels, exc, a):
    return pl.pallas_call(
        _prepare_kernel,
        out_shape=[_sds(AZ, NG, G, RAD)] * 5,
        compiler_params=_params(),
        cost_estimate=_cost(2**22, 8 * 2**20),
        name="prepare",
    )(labels, exc, a)


PG = 16
NP = AX // PG


def _prior_send_kernel(prior_ref, out):
    def block(p):
        x = prior_ref[pl.ds(pl.multiple_of(p * PG, PG), PG)]
        out[:, p] = jnp.transpose(x.reshape(PG * RL, ANG)).reshape(SEC, AZ, PG * RL)

    _loop(NP, block)


def _prior_send(prior):
    return pl.pallas_call(
        _prior_send_kernel,
        out_shape=_sds(SEC, NP, AZ, PG * RL),
        compiler_params=_params(),
        cost_estimate=_cost(2**20, 3 * 2**20),
        name="prior_send",
    )(prior)


def _swap_blocks(x, lanes):
    count = 128 // lanes
    blk = lax.broadcasted_iota(jnp.int32, (8, 128), 1) // lanes
    x = list(x)
    b = count // 2
    while b:
        keep = (blk & b) == 0
        for j in range(count):
            if j & b == 0:
                p, q = x[j], x[j + b]
                x[j] = jnp.where(keep, p, pltpu.roll(q, b * lanes, 1))
                x[j + b] = jnp.where(keep, pltpu.roll(p, 128 - b * lanes, 1), q)
        b //= 2
    return x


def _prior_take_kernel(x_ref, out, nat):
    def block(p):
        for tile in range(AZ // 8):
            rows = slice(tile * 8, tile * 8 + 8)
            for half in range(2):
                got = _swap_blocks([x_ref[half * PG + j, p, rows] for j in range(PG)], RL)
                for k in range(PG):
                    nat[k, rows, half * 128 : half * 128 + 128] = got[k]
        for k in range(PG // G):
            out[:, p * (PG // G) + k] = jnp.swapaxes(nat[k * G : k * G + G], 0, 1)

    _loop(NP, block)


def _prior_take(x):
    return pl.pallas_call(
        _prior_take_kernel,
        out_shape=_sds(AZ, NG, G, RAD),
        scratch_shapes=[pltpu.VMEM((PG, AZ, RAD), F32)],
        compiler_params=_params(),
        cost_estimate=_cost(2**22, 3 * 2**20),
        name="prior_take",
    )(x)


def _temperature_take_kernel(x_ref, out):
    def group(g):
        tiles = [_swap_blocks([x_ref[s * 8 + j, g] for j in range(8)], AZ) for s in range(SEC // 8)]
        for q in range(G):
            out[g * G + q] = jnp.concatenate([t[q] for t in tiles], axis=1)

    _loop(NG, group)


def _temperature_take(x):
    return pl.pallas_call(
        _temperature_take_kernel,
        out_shape=_sds(AX, RL, ANG),
        compiler_params=_params(),
        cost_estimate=_cost(2**22, 2**21),
        name="temperature_take",
    )(x)


def _sides(x, lane):
    x0, x1 = x[:, :HALF], x[:, HALF:]
    f0, f1 = pltpu.roll(x0, 1, 1), pltpu.roll(x1, 1, 1)
    b0, b1 = pltpu.roll(x0, HALF - 1, 1), pltpu.roll(x1, HALF - 1, 1)
    at_low, at_high = lane == 0, lane == HALF - 1
    inward = jnp.concatenate([jnp.where(at_low, 0.0, f0), jnp.where(at_low, f0, f1)], axis=1)
    outward = jnp.concatenate([jnp.where(at_high, b1, b0), jnp.where(at_high, 0.0, b1)], axis=1)
    return inward, outward


def _axial(row, first, last, i, g, x, sub):
    before = pltpu.roll(row(i, g - 1), 1, 0) if g else first
    after = pltpu.roll(row(i, g + 1), G - 1, 0) if g < NG - 1 else last
    lower = jnp.where(sub == 0, before, pltpu.roll(x, 1, 0))
    return lower, jnp.where(sub == G - 1, after, pltpu.roll(x, G - 1, 0))


def _faces(t_row, h_row, i, g, beside, lane, sub):
    t, h = t_row(i, g), h_row(i, g)
    pairs = [(t_row(i - 1, g), h_row(i - 1, g)), (t_row(i + 1, g), h_row(i + 1, g))]
    pairs += list(zip(_sides(t, lane), _sides(h, lane)))
    if beside is None:
        (t_lo, h_lo), (t_hi, h_hi) = (t, -h), (t, -h)
    else:
        (t_lo, h_lo), (t_hi, h_hi) = beside
    pairs += list(zip(_axial(t_row, t_lo, t_hi, i, g, t, sub), _axial(h_row, h_lo, h_hi, i, g, h, sub)))
    flux, total = None, None
    for tn, hn in pairs:
        kf = h + hn
        term = kf * (tn - t)
        flux = term if flux is None else flux + term
        total = kf if total is None else total + kf
    return t, flux, total


def _iotas():
    lane = lax.broadcasted_iota(jnp.int32, (G, HALF), 1)
    sub = lax.broadcasted_iota(jnp.int32, (G, RAD), 0)
    return lane, sub


def _advance(first, width, reach, state, nu_of, oc_of, os_of, add_square, bufs, lane):
    def get(t, r):
        return state(r) if t == 0 else bufs[(t - 1) % 2, r + HMAX]

    for t in range(width):
        phase = 2.0 * math.pi / PERIOD * (first + t)
        cc, ss = math.cos(phase), math.sin(phase)
        lo, hi = -reach + 1 + t, AZ - 1 + reach - 1 - t
        down, mid = get(t, lo - 1), get(t, lo)
        for r in range(lo, hi + 1):
            up = get(t, r + 1)
            inward, outward = _sides(mid, lane)
            source = cc * oc_of(r) if first + t == 0 else cc * oc_of(r) + ss * os_of(r)
            change = nu_of(r) * ((down + up) + (inward + outward) - 4.0 * mid) + source
            if -1 <= r <= AZ:
                add_square(t, r, change * change)
            bufs[t % 2, r + HMAX] = mid + change
            down, mid = mid, up
    return lambda r: get(width - 1, r)


_CONSTS = ["lab", "nu", "oc", "os", "f_low", "f_high"]


def _getters(R, g):
    low, high = R["f_low"], R["f_high"]

    def const(name, k):
        def get(r):
            if r < 0:
                return low[AT[k] + LAYERS[k] + r, g]
            if r >= AZ:
                return high[AT[k] + r - AZ, g]
            return R[name][r, g]

        return get

    label, oc, os = const("lab", 0), const("oc", 1), const("os", 2)
    kept = {}

    def nu(r):
        if 0 <= r < AZ:
            return R["nu"][r, g]
        if r not in kept:
            kept[r] = _reluct(label(r))
        return kept[r]

    def start(r):
        if r < 0:
            return low[H0 + r, g]
        if r >= AZ:
            return high[r - AZ, g]
        return R["a"][r, g]

    return label, nu, oc, os, start


def _run(index, R, g, bufs, lane):
    first, width, reach = sum(WIDTHS[:index]), WIDTHS[index], REACH[index]
    last = index == len(WIDTHS) - 1
    label, nu, oc, os, start = _getters(R, g)

    def state(r):
        if index == 0:
            return start(r)
        if r < 0:
            return R["low"][reach + r, g]
        if r >= AZ:
            return R["high"][r - AZ, g]
        return R["a"][r, g]

    def slot(r):
        return (r + 1,) if last else (r + 1, g)

    def add_square(t, r, sq):
        if t > 0:
            sq = R["q_out"][slot(r)] + sq
        elif index:
            sq = R["q"][r + 1, g] + sq
            if not 0 <= r < AZ:
                missed = state(r) - R["before"][0 if r < 0 else 1, g]
                sq = sq + missed * missed
        R["q_out"][slot(r)] = sq

    return label, _advance(first, width, reach, state, nu, oc, os, add_square, bufs, lane)


def _phase_kernel(index, names, *refs):
    R = dict(zip(names, refs))
    bufs = R["bufs"]
    lane, _ = _iotas()
    n = REACH[index + 1]

    def group(g):
        _, previous = _run(index, R, g, bufs, lane)
        a = bufs[(WIDTHS[index] - 1) % 2, HMAX : HMAX + AZ]
        R["a_out"][:, g] = a
        R["before_out"][0, g] = previous(-1)
        R["before_out"][1, g] = previous(AZ)
        R["e_low"][0:n, g] = a[0:n]
        R["e_high"][0:n, g] = a[AZ - n :]
        if index + 1 == PRIOR_AT:
            R["e_low"][n : n + 2, g] = R["prior"][0:2, g]
            R["e_high"][n : n + 2, g] = R["prior"][AZ - 2 :, g]

    _loop(NG, group)


def _losses(R, g, bufs, lane, store):
    label, _ = _run(len(WIDTHS) - 1, R, g, bufs, lane)
    for r in range(-1, AZ + 1):
        lab = label(r)
        store(r, _sigma(lab) * R["q_out"][r + 1], lab)


_T, _H, _J, _N, _L = range(5)
_END = (5, AZ + 2, RAD)


def _ends_kernel(names, *refs):
    R = dict(zip(names, refs))
    lane, _ = _iotas()
    for out, part, g, q in ((R["down"], R["part_lo"], ENDS[0], 0), (R["up"], R["part_hi"], ENDS[1], G - 1)):
        out[...] = part[...]

        def store(r, d, lab, out=out, part=part, q=q):
            out[_N, r + 1 : r + 2, :] = part[_N, r + 1 : r + 2, :] + d[q : q + 1]

        _losses(R, g, R["bufs"], lane, store)


def _last_kernel(names, *refs):
    R = dict(zip(names, refs))
    bufs = R["bufs"]
    lane, _ = _iotas()

    def group(g):
        def store(r, d, lab):
            t = R["base"][r + 1, g] + d * R["gain"][r + 1, g]
            R["t1"][r + 1, g] = t
            R["h1"][r + 1, g] = _half_cond(lab, t)
            if 0 <= r < AZ:
                R["loss"][r, g] = d

        _losses(R, g, bufs, lane, store)
        a = bufs[(WIDTHS[-1] - 1) % 2, HMAX : HMAX + AZ]
        R["closing"][_planes(g)] = jnp.swapaxes(a, 0, 1)
        R["dissipation"][_planes(g)] = jnp.swapaxes(R["loss"][:, g], 0, 1)

    _loop(NG, group)


def _second_kernel(names, *refs):
    R = dict(zip(names, refs))
    lane, sub = _iotas()
    ax = lax.axis_index("ax")
    exists = (ax > 0, ax < lax.axis_size("ax") - 1)
    for side, (own, other) in enumerate(((R["down"], R["t_lo"]), (R["up"], R["t_hi"]))):
        kf = own[_H] + other[_H]
        jump = kf * (other[_T] - own[_T])
        t = own[_T] + (own[_N] + jump) / (own[_J] + kf)
        R["own1"][side, 0] = t
        R["own1"][side, 1] = _half_cond(own[_L], t)
        t = other[_T] + (other[_N] - jump) / (other[_J] + kf)
        R["beside1"][side, 0] = jnp.where(exists[side], t, 0.0)
        R["beside1"][side, 1] = jnp.where(exists[side], _half_cond(other[_L], t), 0.0)

    def patched(name, k):
        def row(i, g):
            x = R[name][i, g]
            if g == ENDS[0]:
                x = jnp.where(sub == 0, R["own1"][0, k, pl.ds(i, 1), :], x)
            if g == ENDS[1]:
                x = jnp.where(sub == G - 1, R["own1"][1, k, pl.ds(i, 1), :], x)
            return x

        return row

    t_row, h_row = patched("t1", 0), patched("h1", 1)

    def row(r):
        at = pl.ds(r + 1, 1)
        beside = [[R["beside1"][side, k, at, :] for k in range(2)] for side in range(2)]
        for g in range(NG):
            t, flux, total = _faces(t_row, h_row, r + 1, g, beside, lane, sub)
            cap = _capacity(R["lab"][r, g])
            mismatch = cap * (t - R["prior"][r, g]) - flux - R["loss"][r, g]
            R["t2"][r, g] = t - mismatch / (cap + total)

    _loop(AZ, row)

    def turn(g):
        nat = jnp.swapaxes(R["t2"][:, g], 0, 1).reshape(G * AZ, RAD)
        R["blocks"][:, g] = jnp.transpose(nat).reshape(SEC, RL, G * AZ)

    _loop(NG, turn)


def _prior_rows(R, g):
    n = REACH[PRIOR_AT]
    label = _getters(R, g)[0]

    def row(r):
        if r < 0:
            return R["low1"][n + 2 + r, g]
        if r >= AZ:
            return R["high1"][n + r - AZ, g]
        return R["prior"][r, g]

    return row, label


def _ready_kernel(names, *refs):
    R = dict(zip(names, refs))
    lane, sub = _iotas()

    def fill(g):
        prior, label = _prior_rows(R, g)
        for r in range(-2, AZ + 2):
            t, lab = prior(r), label(r)
            R["t0"][r + 2, g] = t
            R["h0"][r + 2, g] = _half_cond(lab, t)
            R["cap"][r + 2, g] = _capacity(lab)

    _loop(NG, fill)

    def row(k):
        for g in range(NG):
            t, flux, total = _faces(
                lambda i, g: R["t0"][i, g], lambda i, g: R["h0"][i, g], k + 1, g, None, lane, sub
            )
            jac = R["cap"][k + 1, g] + total
            gain = 1.0 / jac
            R["base"][k, g] = t + flux * gain
            R["gain"][k, g] = gain
            if g in ENDS:
                end = 0 if g == ENDS[0] else 1
                R["jac"][end, k] = jac
                R["flux"][end, k] = flux

    _loop(AZ + 2, row)
    for end, (out, g, q) in enumerate(((R["part_lo"], ENDS[0], 0), (R["part_hi"], ENDS[1], G - 1))):
        label = _prior_rows(R, g)[1]
        plane = slice(q, q + 1)
        for k in range(AZ + 2):
            at = slice(k, k + 1)
            out[_T, at, :] = R["t0"][k + 1, g, plane, :]
            out[_H, at, :] = R["h0"][k + 1, g, plane, :]
            out[_J, at, :] = R["jac"][end, k, plane, :]
            out[_N, at, :] = R["flux"][end, k, plane, :]
            out[_L, at, :] = label(k - 1)[plane]


def _call(kernel, name, given, names, outs, scratch, *bound):
    results = pl.pallas_call(
        functools.partial(kernel, *bound, names + list(outs) + list(scratch)),
        out_shape=[_sds(*shape) for shape in outs.values()],
        scratch_shapes=[pltpu.VMEM(shape, F32) for shape in scratch.values()],
        compiler_params=_params(),
        cost_estimate=_cost(2**24, 2**23),
        name=name,
    )(*[given[key] for key in names])
    return dict(zip(outs, results))


_OWN = (AZ, NG, G, RAD)
_MORE = (AZ + 2, NG, G, RAD)
_BUFS = (2, AZ + 2 * HMAX, G, RAD)
_STATE = ["a", "q", "before", "low", "high"]
_LAST = _CONSTS + _STATE
_PRIOR = ["lab", "f_low", "f_high", "nu", "oc", "os", "prior", "low1", "high1"]


def _phase(index, V):
    n = REACH[index + 1] + (2 if index + 1 == PRIOR_AT else 0)
    names = _CONSTS + (_STATE if index else ["a"]) + (["prior"] if index + 1 == PRIOR_AT else [])
    outs = {"a_out": _OWN, "q_out": _MORE, "before_out": (2, NG, G, RAD)}
    outs.update(e_low=(n, NG, G, RAD), e_high=(n, NG, G, RAD))
    return _call(_phase_kernel, f"field_{index}", V, names, outs, {"bufs": _BUFS}, index)


def _ring(axis, x, step, closed):
    count = lax.axis_size(axis)
    pairs = [(i, (i + 1) % count) for i in range(count if closed else count - 1)]
    return lax.ppermute(x, axis, pairs if step > 0 else [(b, a) for a, b in pairs])


def _around(low_edge, high_edge):
    return _ring("sec", high_edge, 1, True), _ring("sec", low_edge, -1, True)


def shards(labels, exc, a0, prior):
    V = {}
    V["f_low"], V["f_high"] = _around(*_edges(labels, exc, a0))
    got = lax.all_to_all(_prior_send(prior), "sec", 0, 0)
    V["prior"] = _prior_take(got)
    V.update(zip(("a", "lab", "nu", "oc", "os"), _prepare(labels, exc, a0)))
    last = len(WIDTHS) - 1
    for index in range(last):
        out = _phase(index, V)
        V["a"], V["q"], V["before"] = out["a_out"], out["q_out"], out["before_out"]
        V["low"], V["high"] = _around(out["e_low"], out["e_high"])
        if index + 1 == PRIOR_AT:
            V["low1"], V["high1"] = V["low"], V["high"]
        if index + 1 == last:
            scratch = {name: (AZ + 4, NG, G, RAD) for name in ("t0", "h0", "cap")}
            scratch.update(jac=(2, AZ + 2, G, RAD), flux=(2, AZ + 2, G, RAD))
            outs = {"base": _MORE, "gain": _MORE, "part_lo": _END, "part_hi": _END}
            V.update(_call(_ready_kernel, "first_ready", V, _PRIOR, outs, scratch))
    scratch = {"bufs": _BUFS, "q_out": (AZ + 2, G, RAD)}
    outs = {"down": _END, "up": _END}
    V.update(_call(_ends_kernel, "last_ends", V, _LAST + ["part_lo", "part_hi"], outs, scratch))
    V["t_lo"], V["t_hi"] = _ring("ax", V["up"], 1, False), _ring("ax", V["down"], -1, False)
    outs = {"closing": (AX, AZ, RAD), "dissipation": (AX, AZ, RAD), "t1": _MORE, "h1": _MORE, "loss": _OWN}
    V.update(_call(_last_kernel, "field_last", V, _LAST + ["base", "gain"], outs, scratch))
    names = ["t1", "h1", "down", "up", "t_lo", "t_hi", "lab", "prior", "loss"]
    shape = (2, 2, AZ + 2, RAD)
    scratch = {"t2": _OWN, "own1": shape, "beside1": shape}
    out = _call(_second_kernel, "second_sweep", V, names, {"blocks": (SEC, NG, RL, G * AZ)}, scratch)
    temperature = _temperature_take(lax.all_to_all(out["blocks"], "sec", 0, 0))
    return V["closing"], V["dissipation"], temperature


def solution(mesh):
    spec = P("ax", "sec", None)
    return jax.shard_map(
        shards,
        mesh=mesh,
        in_specs=(spec, P(None, "ax", "sec", None), spec, spec),
        out_specs=(spec, spec, spec),
        check_vma=False,
    )
```

time: 497 us -> 140 us (0.28)
  other arithmetic: 145 us -> 0 us
  local copies, waits for them, and re-layouts: 131 us -> 9.8 us
  starting transfers between devices: 150 us -> 36.3 us
  Pallas kernels: 0 us -> 37.6 us
  waiting for transfers between devices: 62.2 us -> 26.4 us
  blocking collectives: 0 us -> 26.4 us
    ppermute x40 -> x10, starting transfers between devices: 121 us -> 29.6 us  [_ring(): lax.ppermute(x, axis, pairs if step > 0 else [(b, a) for a, b in pairs])]
    add x16 -> x0, other arithmetic: 74.4 us -> none  [advance(): return (fresh, induced_dissipation + sigma * change * change)]
    slice x28 -> x0, local copies, waits for them, and re-layouts: 46 us -> none  [the longest x4 24.7 us: with_halo(): lax.slice_in_dim(cells, cells.shape[dim] - width, cells.shape[dim], axis=...]
    pallas_call x0 -> x12, Pallas kernels: none -> 37.6 us  [the longest x7 24.7 us: _call(): pl.pallas_call(functools.partial(kernel, *bound, names + list(outs) + lis...]
    all_to_all x0 -> x1, blocking collectives: none -> 26.4 us  [shards(): temperature = _temperature_take(lax.all_to_all(out['blocks'], 'sec', 0, 0))]
    unnamed x23 -> x28, local copies, waits for them, and re-layouts: 34.4 us -> 9.8 us
    while x17 -> x0, local copies, waits for them, and re-layouts: 23.7 us -> none
    sub x1 -> x0, other arithmetic: 21.8 us -> none  [damping_weight(): return warmth_distribution - mismatch_amount / main_entries]
  transfers between devices with their start and end apart: 41 -> 11, of which waited for: 21 -> 4; matrix products, arithmetic and copies ran while one was open for 6% -> 0% of each run, Pallas kernels for 0% -> 14%
where the time goes in v3:
time: 140 us; the launch traced here: 137 us
  Pallas kernels  37.6 us (27%)
  starting transfers between devices  36.3 us (26%)
  waiting for transfers between devices  26.4 us (19%)
  blocking collectives  26.4 us (19%)
  local copies, waits for them, and re-layouts  9.8 us (7%)
    ppermute x10, starting transfers between devices, _ring(): lax.ppermute(x, axis, pairs if step > 0 else [(b, a) for a, b in pairs])  29.6 us
    all_to_all x1, blocking collectives, shards(): temperature = _temperature_take(lax.all_to_all(out['blocks'], 'sec', 0, 0))  26.4 us
    ppermute x10, waiting for transfers between devices, _ring(): lax.ppermute(x, axis, pairs if step > 0 else [(b, a) for a, b in pairs])  24.8 us
    pallas_call x7, Pallas kernels, _call(): pl.pallas_call(functools.partial(kernel, *bound, names + list(outs) + lis...  24.7 us
    unnamed x28, local copies, waits for them, and re-layouts  9.8 us
    all_to_all x1, starting transfers between devices, shards(): got = lax.all_to_all(_prior_send(prior), 'sec', 0, 0)  6.76 us
    pallas_call x1, Pallas kernels, _edges(): pl.pallas_call(_edges_kernel, in_specs=[pl.BlockSpec(memory_space=pl.ANY)...  3.99 us
    pallas_call x1, Pallas kernels, _prior_take(): pl.pallas_call(_prior_take_kernel, out_shape=_sds(AZ, NG, G, RAD), scratc...  3.31 us
  transfers between devices with their start and end apart: 11, of which 4 were waited for; matrix products, arithmetic and copies ran while one was open for 0% of the time, Pallas kernels for 14%

profile of v3, /device:TPU:3, one launch (start us, length us, event | category | flops | bytes accessed | tf_op | source)
XLA Modules:
  0.0 137.4 jit_solution(14827566847294660480)
XLA Ops:
  0.6 4.0 %edge_layers.1 = (f32[16,8,8,256]{3,2,1,0:T(8,128)}, f32[16,8,8,256]{3,2,1,0:T(8,128)}) custom-call(s32[64,16,256]{2,1,0:T(8,128)} %lab_hbm.1, f32[2,64,16,256]{3,2,1,0:T(8,128)} %exc_hbm.1, f32[64,16,256]{2,1,0:T(8,128)} %a_hbm.1), custom_call_target="tpu_custom_call" | custom-call | flops 1048576 | bytes 6291456 | tf_op jit(solution)/shard_map/edge_layers/pallas_call | solution.py:119
  4.6 1.7 %collective-permute-start = (f32[16,8,8,256]{3,2,1,0:T(8,128)}, f32[16,8,8,256]{3,2,1,0:T(8,128)S(1)}, u32[]{:S(2)}, u32[]{:S(2)}) collective-permute-start(f32[16,8,8,256]{3,2,1,0:T(8,128)} %get-tuple-element.40), channel_id=1, source_target_pairs={{0,4},{4,8},{8,12},{12,16},{16,20},{20,24},{24,28},{28,32},{32,36}... | collective-permute-start | bytes 3145736 | tf_op jit(solution)/shard_map/ppermute | solution.py:567
  6.3 3.2 %collective-permute-start.1 = (f32[16,8,8,256]{3,2,1,0:T(8,128)}, f32[16,8,8,256]{3,2,1,0:T(8,128)S(1)}, u32[]{:S(2)}, u32[]{:S(2)}) collective-permute-start(f32[16,8,8,256]{3,2,1,0:T(8,128)} %get-tuple-element.41), channel_id=1, source_target_pairs={{4,0},{8,4},{12,8},{16,12},{20,16},{24,20},{28,24},{32,28},{36,32}... | collective-permute-start | bytes 3145736 | tf_op jit(solution)/shard_map/ppermute | solution.py:567
  9.5 1.5 %prior_send.1 = f32[32,4,16,128]{3,2,1,0:T(8,128)} custom-call(f32[64,8,512]{2,1,0:T(8,128)S(1)} %copy-done.13), custom_call_target="tpu_custom_call" | custom-call | flops 1048576 | bytes 3145728 | tf_op jit(solution)/shard_map/prior_send/pallas_call | solution.py:173
  11.1 6.8 %all-to-all-start = ((f32[32,4,16,128]{3,2,1,0:T(8,128)}), f32[32,4,16,128]{3,2,1,0:T(8,128)}, u32[]{:S(2)}, u32[]{:S(2)}) async-start(f32[32,4,16,128]{3,2,1,0:T(8,128)} %prior_send.1), calls=%async_computation | async-start | bytes 2097152 | tf_op jit(solution)/shard_map/all_to_all | solution.py:577
  17.8 1.6 %copy-done.6 = f32[2,64,16,256]{3,2,1,0:T(8,128)S(1)} copy-done((f32[2,64,16,256]{3,2,1,0:T(8,128)S(1)}, f32[2,64,16,256]{3,2,1,0:T(8,128)}, u32[]{:S(2)}) %copy-start.6) | copy-done | bytes 2097176
  19.4 1.2 copy-done.7
  20.6 1.2 copy-done.8
  21.9 1.1 prepare.1
  23.0 17.9 %collective-permute-done.refs_4_.refs_1_ = f32[16,8,8,256]{3,2,1,0:T(8,128)S(1)} collective-permute-done((f32[16,8,8,256]{3,2,1,0:T(8,128)}, f32[16,8,8,256]{3,2,1,0:T(8,128)S(1)}, u32[]{:S(2)}, u32[]{:S(2)}) %collective-permute-start) | collective-permute-done | bytes 1048608 | tf_op jit(solution)/shard_map/ppermute | solution.py:567
  40.9 4.9 %field_0.1 = (f32[16,8,8,256]{3,2,1,0:T(8,128)S(1)}, f32[18,8,8,256]{3,2,1,0:T(8,128)S(1)}, f32[2,8,8,256]{3,2,1,0:T(8,128)S(1)}, f32[4,8,8,256]{3,2,1,0:T(8,128)}, f32[4,8,8,256]{3,2,1,0:T(8,128)}) custom-call(f32[16,8,8,256]{3,2,1,0:T(8,128)S(1)} %get-tuple-element.36.refs_0_.refs_6_, f32[16,8,8,256]{3,2,1,0:T(8,128)S(1)} %get-tuple-element.37.refs_1_.refs_3_, ...), custom_call_target="tpu_custom_call" | custom-call | flops 16777216 | bytes 8388608 | tf_op jit(solution)/shard_map/field_0/pallas_call | solution.py:537
  45.9 1.0 copy-done.9
  46.9 1.0 copy-done.11
  47.9 4.5 %collective-permute-start.3 = (f32[4,8,8,256]{3,2,1,0:T(8,128)}, f32[4,8,8,256]{3,2,1,0:T(8,128)}, u32[]{:S(2)}, u32[]{:S(2)}) collective-permute-start(f32[4,8,8,256]{3,2,1,0:T(8,128)} %get-tuple-element.47), channel_id=1, source_target_pairs={{4,0},{8,4},{12,8},{16,12},{20,16},{24,20},{28,24},{32,28},{36,32}... | collective-permute-start | bytes 786440 | tf_op jit(solution)/shard_map/ppermute | solution.py:567
  52.4 1.6 %all-to-all-done.x_ref = f32[32,4,16,128]{3,2,1,0:T(8,128)} async-done(((f32[32,4,16,128]{3,2,1,0:T(8,128)}), f32[32,4,16,128]{3,2,1,0:T(8,128)}, u32[]{:S(2)}, u32[]{:S(2)}) %all-to-all-start) | async-done | bytes 1048608 | tf_op jit(solution)/shard_map/all_to_all | solution.py:577
  54.0 3.3 %prior_take.1.refs_11_.refs_6_.refs_7_ = f32[16,8,8,256]{3,2,1,0:T(8,128)S(1)} custom-call(f32[32,4,16,128]{3,2,1,0:T(8,128)} %all-to-all-done.x_ref), custom_call_target="tpu_custom_call" | custom-call | flops 4194304 | bytes 3145728 | tf_op jit(solution)/shard_map/prior_take/pallas_call | solution.py:213
  57.4 1.2 copy-done.5
  58.6 1.3 copy-done.10
  59.9 1.2 copy-done.12
  61.1 4.2 %field_1.1 = (f32[16,8,8,256]{3,2,1,0:T(8,128)S(1)}, f32[18,8,8,256]{3,2,1,0:T(8,128)S(1)}, f32[2,8,8,256]{3,2,1,0:T(8,128)S(1)}, f32[6,8,8,256]{3,2,1,0:T(8,128)S(1)}, f32[6,8,8,256]{3,2,1,0:T(8,128)S(1)}) custom-call(f32[16,8,8,256]{3,2,1,0:T(8,128)S(1)} %get-tuple-element.36.refs_0_.refs_6_, f32[16,8,8,256]{3,2,1,0:T(8,128)S(1)} %copy-done.1, ...), custom_call_target="tpu_custom_call" | custom-call | flops 16777216 | bytes 8388608 | tf_op jit(solution)/shard_map/field_1/pallas_call | solution.py:537
  65.4 4.5 %collective-permute-start.5 = (f32[6,8,8,256]{3,2,1,0:T(8,128)S(1)}, f32[6,8,8,256]{3,2,1,0:T(8,128)S(1)}, u32[]{:S(2)}, u32[]{:S(2)}) collective-permute-start(f32[6,8,8,256]{3,2,1,0:T(8,128)S(1)} %get-tuple-element.52), channel_id=1, source_target_pairs={{4,0},{8,4},{12,8},{16,12},{20,16},{24,20},{28,24},{32,28},{36,32}... | collective-permute-start | bytes 1179656 | tf_op jit(solution)/shard_map/ppermute | solution.py:567
  69.8 6.4 %collective-permute-done.4.refs_9_.refs_7_ = f32[6,8,8,256]{3,2,1,0:T(8,128)S(1)} collective-permute-done((f32[6,8,8,256]{3,2,1,0:T(8,128)S(1)}, f32[6,8,8,256]{3,2,1,0:T(8,128)S(1)}, u32[]{:S(2)}, u32[]{:S(2)}) %collective-permute-start.4) | collective-permute-done | bytes 393248 | tf_op jit(solution)/shard_map/ppermute | solution.py:567
  76.3 3.3 %field_2.1 = (f32[16,8,8,256]{3,2,1,0:T(8,128)S(1)}, f32[18,8,8,256]{3,2,1,0:T(8,128)S(1)}, f32[2,8,8,256]{3,2,1,0:T(8,128)S(1)}, f32[4,8,8,256]{3,2,1,0:T(8,128)S(1)}, f32[4,8,8,256]{3,2,1,0:T(8,128)S(1)}) custom-call(f32[16,8,8,256]{3,2,1,0:T(8,128)S(1)} %get-tuple-element.36.refs_0_.refs_6_, f32[16,8,8,256]{3,2,1,0:T(8,128)S(1)} %copy-done.1, ...), custom_call_target="tpu_custom_call" | custom-call | flops 16777216 | bytes 8388608 | tf_op jit(solution)/shard_map/field_2/pallas_call | solution.py:537
  79.6 4.5 %collective-permute-start.7 = (f32[4,8,8,256]{3,2,1,0:T(8,128)S(1)}, f32[4,8,8,256]{3,2,1,0:T(8,128)S(1)}, u32[]{:S(2)}, u32[]{:S(2)}) collective-permute-start(f32[4,8,8,256]{3,2,1,0:T(8,128)S(1)} %get-tuple-element.57), channel_id=1, source_target_pairs={{4,0},{8,4},{12,8},{16,12},{20,16},{24,20},{28,24},{32,28},{36,32}... | collective-permute-start | bytes 786440 | tf_op jit(solution)/shard_map/ppermute | solution.py:567
  84.1 3.3 %first_ready.1 = (f32[18,8,8,256]{3,2,1,0:T(8,128)S(1)}, f32[18,8,8,256]{3,2,1,0:T(8,128)S(1)}, f32[5,18,256]{2,1,0:T(8,128)S(1)}, f32[5,18,256]{2,1,0:T(8,128)S(1)}) custom-call(f32[16,8,8,256]{3,2,1,0:T(8,128)S(1)} %get-tuple-element.36.refs_0_.refs_6_, f32[16,8,8,256]{3,2,1,0:T(8,128)S(1)} %collective-permute-done.refs_4_.refs_1_, ...), custom_call_target="tpu_custom_call" | custom-call | flops 16777216 | bytes 8388608 | tf_op jit(solution)/shard_map/first_ready/pallas_call | solution.py:537
  87.8 0.7 last_ends.1
  88.5 6.7 %collective-permute-start.9 = (f32[5,18,256]{2,1,0:T(8,128)S(1)}, f32[5,18,256]{2,1,0:T(8,128)S(1)}, u32[]{:S(2)}, u32[]{:S(2)}) collective-permute-start(f32[5,18,256]{2,1,0:T(8,128)S(1)} %get-tuple-element.66.refs_2_), channel_id=1, source_target_pairs={{1,0},{2,1},{3,2},{5,4},{6,5},{7,6},{9,8},{10,9},{11,10},{13,12},{... | collective-permute-start | bytes 276488 | tf_op jit(solution)/shard_map/ppermute | solution.py:567
  95.2 4.4 %collective-permute-start.8 = (f32[5,18,256]{2,1,0:T(8,128)S(1)}, f32[5,18,256]{2,1,0:T(8,128)S(1)}, u32[]{:S(2)}, u32[]{:S(2)}) collective-permute-start(f32[5,18,256]{2,1,0:T(8,128)S(1)} %get-tuple-element.67.refs_3_), channel_id=1, source_target_pairs={{0,1},{1,2},{2,3},{4,5},{5,6},{6,7},{8,9},{9,10},{10,11},{12,13},{... | collective-permute-start | bytes 276488 | tf_op jit(solution)/shard_map/ppermute | solution.py:567
  99.6 5.1 %field_last.1 = (f32[64,16,256]{2,1,0:T(8,128)}, f32[64,16,256]{2,1,0:T(8,128)}, f32[18,8,8,256]{3,2,1,0:T(8,128)S(1)}, f32[18,8,8,256]{3,2,1,0:T(8,128)S(1)}, f32[16,8,8,256]{3,2,1,0:T(8,128)S(1)}) custom-call(f32[16,8,8,256]{3,2,1,0:T(8,128)S(1)} %get-tuple-element.36.refs_0_.refs_6_, f32[16,8,8,256]{3,2,1,0:T(8,128)S(1)} %copy-done.1, ...), custom_call_target="tpu_custom_call" | custom-call | flops 16777216 | bytes 8388608 | tf_op jit(solution)/shard_map/field_last/pallas_call | solution.py:537
  104.7 3.4 %second_sweep.1 = f32[32,8,8,128]{3,2,1,0:T(8,128)S(1)} custom-call(f32[18,8,8,256]{3,2,1,0:T(8,128)S(1)} %get-tuple-element.62.refs_0_, f32[18,8,8,256]{3,2,1,0:T(8,128)S(1)} %get-tuple-element.63.refs_1_, f32[5,18,256]{2,1,0:T(8,128)S(1)} %get-tuple-element.66.refs_2_, f32[5,18,256]{2,1,0:T(8,128)S(1)} %get-tuple-element.67.refs_3_, ...), custom_call_target="tpu_custom_call" | custom-call | flops 16777216 | bytes 8388608 | tf_op jit(solution)/shard_map/second_sweep/pallas_call | solution.py:537
  108.1 26.4 %all_to_all.10.x_ref = f32[32,8,8,128]{3,2,1,0:T(8,128)S(1)} all-to-all(f32[32,8,8,128]{3,2,1,0:T(8,128)S(1)} %second_sweep.1), channel_id=1, replica_groups=mesh['sec'=32,'ax'=4] {'sec'}, dimensions={0} | all-to-all | bytes 2097152 | tf_op jit(solution)/shard_map/all_to_all | solution.py:602
  134.5 2.9 %temperature_take.1 = f32[64,8,512]{2,1,0:T(8,128)} custom-call(f32[32,8,8,128]{3,2,1,0:T(8,128)S(1)} %all_to_all.10.x_ref), custom_call_target="tpu_custom_call" | custom-call | flops 4194304 | bytes 2097152 | tf_op jit(solution)/shard_map/temperature_take/pallas_call | solution.py:233
  (31 shorter events, 0.7 us)
Async XLA Ops:
  0.6 8.9 %copy-start.13 = (f32[64,8,512]{2,1,0:T(8,128)S(1)}, f32[64,8,512]{2,1,0:T(8,128)}, u32[]{:S(2)}) copy-start(f32[64,8,512]{2,1,0:T(8,128)} %prior_ref.1) | copy-start | bytes 3145732
  4.6 36.3 %collective-permute-start = (f32[16,8,8,256]{3,2,1,0:T(8,128)}, f32[16,8,8,256]{3,2,1,0:T(8,128)S(1)}, u32[]{:S(2)}, u32[]{:S(2)}) collective-permute-start(f32[16,8,8,256]{3,2,1,0:T(8,128)} %get-tuple-element.40), channel_id=1, source_target_pairs={{0,4},{4,8},{8,12},{12,16},{16,20},{20,24},{24,28},{28,32},{32,36}... | collective-permute-start | bytes 3145736 | tf_op jit(solution)/shard_map/ppermute | solution.py:567
  6.3 34.6 %collective-permute-start.1 = (f32[16,8,8,256]{3,2,1,0:T(8,128)}, f32[16,8,8,256]{3,2,1,0:T(8,128)S(1)}, u32[]{:S(2)}, u32[]{:S(2)}) collective-permute-start(f32[16,8,8,256]{3,2,1,0:T(8,128)} %get-tuple-element.41), channel_id=1, source_target_pairs={{4,0},{8,4},{12,8},{16,12},{20,16},{24,20},{28,24},{32,28},{36,32}... | collective-permute-start | bytes 3145736 | tf_op jit(solution)/shard_map/ppermute | solution.py:567
  11.1 42.9 %all-to-all-start = ((f32[32,4,16,128]{3,2,1,0:T(8,128)}), f32[32,4,16,128]{3,2,1,0:T(8,128)}, u32[]{:S(2)}, u32[]{:S(2)}) async-start(f32[32,4,16,128]{3,2,1,0:T(8,128)} %prior_send.1), calls=%async_computation | async-start | bytes 2097152 | tf_op jit(solution)/shard_map/all_to_all | solution.py:577
  17.8 1.6 %copy-start.6 = (f32[2,64,16,256]{3,2,1,0:T(8,128)S(1)}, f32[2,64,16,256]{3,2,1,0:T(8,128)}, u32[]{:S(2)}) copy-start(f32[2,64,16,256]{3,2,1,0:T(8,128)} %exc_hbm.1) | copy-start | bytes 6291460
  19.4 1.2 copy-start.7
  20.6 1.2 copy-start.8
  23.0 22.9 %copy-start = (f32[16,8,8,256]{3,2,1,0:T(8,128)}, f32[16,8,8,256]{3,2,1,0:T(8,128)S(1)}, u32[]{:S(2)}) copy-start(f32[16,8,8,256]{3,2,1,0:T(8,128)S(1)} %get-tuple-element.37.refs_1_.refs_3_) | copy-start | bytes 3145732
  23.0 22.8 %copy-start.2 = (f32[16,8,8,256]{3,2,1,0:T(8,128)}, f32[16,8,8,256]{3,2,1,0:T(8,128)S(1)}, u32[]{:S(2)}) copy-start(f32[16,8,8,256]{3,2,1,0:T(8,128)S(1)} %get-tuple-element.38.refs_2_.refs_4_) | copy-start | bytes 3145732
  23.0 22.8 %copy-start.4 = (f32[16,8,8,256]{3,2,1,0:T(8,128)}, f32[16,8,8,256]{3,2,1,0:T(8,128)S(1)}, u32[]{:S(2)}) copy-start(f32[16,8,8,256]{3,2,1,0:T(8,128)S(1)} %get-tuple-element.39.refs_3_.refs_5_) | copy-start | bytes 3145732
  45.9 1.0 copy-start.9
  46.9 1.0 copy-start.11
  47.9 9.4 %collective-permute-start.2 = (f32[4,8,8,256]{3,2,1,0:T(8,128)}, f32[4,8,8,256]{3,2,1,0:T(8,128)S(1)}, u32[]{:S(2)}, u32[]{:S(2)}) collective-permute-start(f32[4,8,8,256]{3,2,1,0:T(8,128)} %get-tuple-element.46), channel_id=1, source_target_pairs={{0,4},{4,8},{8,12},{12,16},{16,20},{20,24},{24,28},{28,32},{32,36}... | collective-permute-start | bytes 786440 | tf_op jit(solution)/shard_map/ppermute | solution.py:567
  47.9 9.4 %collective-permute-start.3 = (f32[4,8,8,256]{3,2,1,0:T(8,128)}, f32[4,8,8,256]{3,2,1,0:T(8,128)}, u32[]{:S(2)}, u32[]{:S(2)}) collective-permute-start(f32[4,8,8,256]{3,2,1,0:T(8,128)} %get-tuple-element.47), channel_id=1, source_target_pairs={{4,0},{8,4},{12,8},{16,12},{20,16},{24,20},{28,24},{32,28},{36,32}... | collective-permute-start | bytes 786440 | tf_op jit(solution)/shard_map/ppermute | solution.py:567
  54.0 3.3 %copy-start.1 = (f32[16,8,8,256]{3,2,1,0:T(8,128)S(1)}, f32[16,8,8,256]{3,2,1,0:T(8,128)}, u32[]{:S(2)}) copy-start(f32[16,8,8,256]{3,2,1,0:T(8,128)} %copy-done) | copy-start | bytes 3145732
  54.0 3.4 %copy-start.3 = (f32[16,8,8,256]{3,2,1,0:T(8,128)S(1)}, f32[16,8,8,256]{3,2,1,0:T(8,128)}, u32[]{:S(2)}) copy-start(f32[16,8,8,256]{3,2,1,0:T(8,128)} %copy-done.2) | copy-start | bytes 3145732
  57.3 1.2 copy-start.5
  58.6 1.3 copy-start.10
  59.8 1.2 copy-start.12
  65.3 11.0 %collective-permute-start.4 = (f32[6,8,8,256]{3,2,1,0:T(8,128)S(1)}, f32[6,8,8,256]{3,2,1,0:T(8,128)S(1)}, u32[]{:S(2)}, u32[]{:S(2)}) collective-permute-start(f32[6,8,8,256]{3,2,1,0:T(8,128)S(1)} %get-tuple-element.51), channel_id=1, source_target_pairs={{0,4},{4,8},{8,12},{12,16},{16,20},{20,24},{24,28},{28,32},{32,36}... | collective-permute-start | bytes 1179656 | tf_op jit(solution)/shard_map/ppermute | solution.py:567
  65.4 10.9 %collective-permute-start.5 = (f32[6,8,8,256]{3,2,1,0:T(8,128)S(1)}, f32[6,8,8,256]{3,2,1,0:T(8,128)S(1)}, u32[]{:S(2)}, u32[]{:S(2)}) collective-permute-start(f32[6,8,8,256]{3,2,1,0:T(8,128)S(1)} %get-tuple-element.52), channel_id=1, source_target_pairs={{4,0},{8,4},{12,8},{16,12},{20,16},{24,20},{28,24},{32,28},{36,32}... | collective-permute-start | bytes 1179656 | tf_op jit(solution)/shard_map/ppermute | solution.py:567
  79.5 8.3 %collective-permute-start.6 = (f32[4,8,8,256]{3,2,1,0:T(8,128)S(1)}, f32[4,8,8,256]{3,2,1,0:T(8,128)S(1)}, u32[]{:S(2)}, u32[]{:S(2)}) collective-permute-start(f32[4,8,8,256]{3,2,1,0:T(8,128)S(1)} %get-tuple-element.56), channel_id=1, source_target_pairs={{0,4},{4,8},{8,12},{12,16},{16,20},{20,24},{24,28},{28,32},{32,36}... | collective-permute-start | bytes 786440 | tf_op jit(solution)/shard_map/ppermute | solution.py:567
  79.6 8.2 %collective-permute-start.7 = (f32[4,8,8,256]{3,2,1,0:T(8,128)S(1)}, f32[4,8,8,256]{3,2,1,0:T(8,128)S(1)}, u32[]{:S(2)}, u32[]{:S(2)}) collective-permute-start(f32[4,8,8,256]{3,2,1,0:T(8,128)S(1)} %get-tuple-element.57), channel_id=1, source_target_pairs={{4,0},{8,4},{12,8},{16,12},{20,16},{24,20},{28,24},{32,28},{36,32}... | collective-permute-start | bytes 786440 | tf_op jit(solution)/shard_map/ppermute | solution.py:567
  88.5 16.2 %collective-permute-start.9 = (f32[5,18,256]{2,1,0:T(8,128)S(1)}, f32[5,18,256]{2,1,0:T(8,128)S(1)}, u32[]{:S(2)}, u32[]{:S(2)}) collective-permute-start(f32[5,18,256]{2,1,0:T(8,128)S(1)} %get-tuple-element.66.refs_2_), channel_id=1, source_target_pairs={{1,0},{2,1},{3,2},{5,4},{6,5},{7,6},{9,8},{10,9},{11,10},{13,12},{... | collective-permute-start | bytes 276488 | tf_op jit(solution)/shard_map/ppermute | solution.py:567
  95.2 9.5 %collective-permute-start.8 = (f32[5,18,256]{2,1,0:T(8,128)S(1)}, f32[5,18,256]{2,1,0:T(8,128)S(1)}, u32[]{:S(2)}, u32[]{:S(2)}) collective-permute-start(f32[5,18,256]{2,1,0:T(8,128)S(1)} %get-tuple-element.67.refs_3_), channel_id=1, source_target_pairs={{0,1},{1,2},{2,3},{4,5},{5,6},{6,7},{8,9},{9,10},{10,11},{12,13},{... | collective-permute-start | bytes 276488 | tf_op jit(solution)/shard_map/ppermute | solution.py:567

commit v4 on v3

--- a/solution.py
+++ b/solution.py
@@ -10,15 +10,11 @@
 
 SAMPLES = 16
 PERIOD = 32
-WIDTHS = (5, 4, 4, 3)
-REACH = (5, 4, 4, 4)
-PRIOR_AT = 2
-H0 = REACH[0]
-HMAX = max(REACH)
-C = HMAX - 1
-LAYERS = (C, C, C - 1)
-AT = (H0, H0 + C, H0 + 2 * C)
-NSEND = H0 + sum(LAYERS)
+SPAN = 8
+DEPTH = SPAN // 2
+FIRST_AT = (0, DEPTH, 2 * DEPTH, 3 * DEPTH, 4 * DEPTH)
+NSEND = 5 * DEPTH
+NLATEST = DEPTH + 1
 
 F32 = jnp.float32
 AX, AZ, RAD, ANG = 64, 16, 256, 512
@@ -50,6 +46,23 @@
     lax.fori_loop(0, n, step, 0)
 
 
+def _lockstep(chains):
+    results = [None] * len(chains)
+    going = dict(enumerate(chains))
+    while going:
+        for k in list(going):
+            try:
+                next(going[k])
+            except StopIteration as end:
+                results[k] = end.value
+                del going[k]
+    return results
+
+
+def _pairs(body):
+    _loop(NG // 2, lambda i: body([2 * i, 2 * i + 1]))
+
+
 def _planes(g):
     return pl.ds(pl.multiple_of(g * G, G), G)
 
@@ -73,16 +86,6 @@
 
 def _capacity(lab):
     return jnp.where(lab == 1, 3.5, jnp.where(lab == 2, 0.5, 3.0)).astype(F32)
-
-
-def _send_layers(store, high, a, lab, c, s):
-    def edge(x, n):
-        return x[AZ - n :] if high else x[:n]
-
-    store(0, edge(a, H0))
-    store(AT[0], edge(lab, LAYERS[0]).astype(F32))
-    store(AT[1], _driven(edge(lab, LAYERS[1]), edge(c, LAYERS[1])))
-    store(AT[2], _driven(edge(lab, LAYERS[2]), edge(s, LAYERS[2])))
 
 
 def _edges_kernel(lab_hbm, exc_hbm, a_hbm, low_ref, high_ref, lab_v, exc_v, a_v, sems):
@@ -100,19 +103,37 @@
         for copy in copies[-1]:
             copy.start()
 
-    def group(g, a, c, s, lab):
-        for out, high in ((low_ref, False), (high_ref, True)):
-
-            def store(k, x, out=out):
-                out[k : k + x.shape[0], g] = x
-
-            _send_layers(store, high, a, lab, c, s)
-
-    for g in range(NG):
-        for copy in copies[g]:
-            copy.wait()
-        at = pl.ds(g * G, G)
-        group(g, *[jnp.swapaxes(x, 0, 1) for x in (a_v[at], exc_v[0, at], exc_v[1, at], lab_v[at])])
+    lane, _ = _iotas()
+
+    def corner(g, out, row, a, c, s, lab):
+        nu, oc, os = {}, {}, {}
+        for j in range(2 * DEPTH - 1):
+            r = row(j)
+            nu[j], oc[j], os[j] = _reluct(lab[r]), _driven(lab[r], c[r]), _driven(lab[r], s[r])
+            if j < DEPTH:
+                out[FIRST_AT[2] + j, g] = lab[r].astype(F32)
+                out[FIRST_AT[3] + j, g] = oc[j]
+                out[FIRST_AT[4] + j, g] = os[j]
+        level = {j: a[row(j)] for j in range(2 * DEPTH)}
+        for t in range(DEPTH):
+            yield
+            out[FIRST_AT[0] + t, g] = level[t]
+            out[FIRST_AT[1] + t, g] = level[t + 1]
+            level = {
+                j: _step(t, level[j - 1], level[j], level[j + 1], nu[j], oc[j], os[j], lane)[0]
+                for j in range(t + 1, 2 * DEPTH - 1 - t)
+            }
+
+    for pair in range(NG // 2):
+        chains = []
+        for g in (2 * pair, 2 * pair + 1):
+            for copy in copies[g]:
+                copy.wait()
+            at = pl.ds(g * G, G)
+            given = [jnp.swapaxes(x, 0, 1) for x in (a_v[at], exc_v[0, at], exc_v[1, at], lab_v[at])]
+            chains.append(corner(g, low_ref, lambda j: j, *given))
+            chains.append(corner(g, high_ref, lambda j: AZ - 1 - j, *given))
+        _lockstep(chains)
 
 
 def _edges(labels, exc, a):
@@ -132,25 +153,35 @@
     )(labels, exc, a)
 
 
-def _prepare_kernel(lab_ref, exc_ref, a_ref, a_out, lab_out, nu_out, oc_out, os_out):
-    def group(g, a, c, s, lab):
-        a_out[:, g] = a
+def _prepare_kernel(lab_ref, exc_ref, a_ref, latest, earlier, q, lab_out, nu_out, oc_out, os_out, bufs, a_v):
+    lane, _ = _iotas()
+
+    def group(g, k):
+        at = _planes(g)
+        lab = jnp.swapaxes(lab_ref[at], 0, 1)
         lab_out[:, g] = lab.astype(F32)
         nu_out[:, g] = _reluct(lab)
-        oc_out[:, g] = _driven(lab, c)
-        os_out[:, g] = _driven(lab, s)
-
-    def own(g):
-        at = _planes(g)
-        group(g, *[jnp.swapaxes(x, 0, 1) for x in (a_ref[at], exc_ref[0, at], exc_ref[1, at], lab_ref[at])])
-
-    _loop(NG, own)
+        oc_out[:, g] = _driven(lab, jnp.swapaxes(exc_ref[0, at], 0, 1))
+        os_out[:, g] = _driven(lab, jnp.swapaxes(exc_ref[1, at], 0, 1))
+        a_v[k] = jnp.swapaxes(a_ref[at], 0, 1)
+        zero = jnp.zeros((G, RAD), F32)
+        for r in (-1, 0, AZ - 1, AZ):
+            q[r + 1, g] = zero
+
+        def add_square(t, r, sq):
+            q[r + 1, g] = sq if t == 0 else q[r + 1, g] + sq
+
+        consts = [lambda r, ref=ref: ref[r, g] for ref in (nu_out, oc_out, os_out)]
+        return _triangle(0, lambda r: a_v[k, r], consts, add_square, latest, earlier, g, bufs.at[k], lane)
+
+    _pairs(lambda gs: _lockstep([group(g, k) for k, g in enumerate(gs)]))
 
 
 def _prepare(labels, exc, a):
     return pl.pallas_call(
         _prepare_kernel,
-        out_shape=[_sds(AZ, NG, G, RAD)] * 5,
+        out_shape=[_sds(AZ, NG, G, RAD)] * 2 + [_sds(AZ + 2, NG, G, RAD)] + [_sds(AZ, NG, G, RAD)] * 4,
+        scratch_shapes=[pltpu.VMEM((2, 2, AZ, G, RAD), F32), pltpu.VMEM((2, AZ, G, RAD), F32)],
         compiler_params=_params(),
         cost_estimate=_cost(2**22, 8 * 2**20),
         name="prepare",
@@ -162,17 +193,25 @@
 
 
 def _prior_send_kernel(prior_ref, out):
-    def block(p):
-        x = prior_ref[pl.ds(pl.multiple_of(p * PG, PG), PG)]
-        out[:, p] = jnp.transpose(x.reshape(PG * RL, ANG)).reshape(SEC, AZ, PG * RL)
-
-    _loop(NP, block)
+    for p in range(NP):
+        x = prior_ref[p * PG : p * PG + PG]
+        x = jnp.transpose(x.reshape(PG * RL, ANG)).reshape(SEC, AZ, PG * RL)
+        out[:, p] = x
+        for e, r in enumerate((AZ - 2, AZ - 1, 0, 1)):
+            line = x[:, r : r + 1, :]
+            at = slice(p * 4 + e, p * 4 + e + 1)
+            if e < 2:
+                out[1:, NP, at, :] = line[:-1]
+                out[0:1, NP, at, :] = line[-1:]
+            else:
+                out[:-1, NP, at, :] = line[1:]
+                out[SEC - 1 :, NP, at, :] = line[:1]
 
 
 def _prior_send(prior):
     return pl.pallas_call(
         _prior_send_kernel,
-        out_shape=_sds(SEC, NP, AZ, PG * RL),
+        out_shape=_sds(SEC, NP + 1, AZ, PG * RL),
         compiler_params=_params(),
         cost_estimate=_cost(2**20, 3 * 2**20),
         name="prior_send",
@@ -195,24 +234,32 @@
     return x
 
 
-def _prior_take_kernel(x_ref, out, nat):
-    def block(p):
+def _prior_take_kernel(x_ref, out, more, nat):
+    def fill(p):
         for tile in range(AZ // 8):
             rows = slice(tile * 8, tile * 8 + 8)
             for half in range(2):
                 got = _swap_blocks([x_ref[half * PG + j, p, rows] for j in range(PG)], RL)
                 for k in range(PG):
                     nat[k, rows, half * 128 : half * 128 + 128] = got[k]
+
+    def block(p):
+        fill(p)
         for k in range(PG // G):
             out[:, p * (PG // G) + k] = jnp.swapaxes(nat[k * G : k * G + G], 0, 1)
 
     _loop(NP, block)
+    fill(NP)
+    for k in range(PG // G):
+        x = jnp.swapaxes(nat[k * G : k * G + G], 0, 1)
+        for p in range(NP):
+            more[:, p * (PG // G) + k] = x[p * 4 : p * 4 + 4]
 
 
 def _prior_take(x):
     return pl.pallas_call(
         _prior_take_kernel,
-        out_shape=_sds(AZ, NG, G, RAD),
+        out_shape=[_sds(AZ, NG, G, RAD), _sds(4, NG, G, RAD)],
         scratch_shapes=[pltpu.VMEM((PG, AZ, RAD), F32)],
         compiler_params=_params(),
         cost_estimate=_cost(2**22, 3 * 2**20),
@@ -280,119 +327,190 @@
     return lane, sub
 
 
-def _advance(first, width, reach, state, nu_of, oc_of, os_of, add_square, bufs, lane):
+def _step(sample, down, mid, up, nu, oc, os, lane):
+    phase = 2.0 * math.pi / PERIOD * sample
+    cc, ss = math.cos(phase), math.sin(phase)
+    inward, outward = _sides(mid, lane)
+    source = cc * oc if sample == 0 else cc * oc + ss * os
+    change = nu * ((down + up) + (inward + outward) - 4.0 * mid) + source
+    return mid + change, change
+
+
+def _triangle(first, rows, consts, add_square, latest, earlier, g, bufs, lane):
+    nu, oc, os = consts
+
     def get(t, r):
-        return state(r) if t == 0 else bufs[(t - 1) % 2, r + HMAX]
-
-    for t in range(width):
-        phase = 2.0 * math.pi / PERIOD * (first + t)
-        cc, ss = math.cos(phase), math.sin(phase)
-        lo, hi = -reach + 1 + t, AZ - 1 + reach - 1 - t
+        return rows(r) if t == 0 else bufs[(t - 1) % 2, r]
+
+    latest[0, g] = rows(0)
+    latest[AZ - 1, g] = rows(AZ - 1)
+    earlier[1, g] = rows(1)
+    earlier[AZ - 2, g] = rows(AZ - 2)
+    for t in range(SPAN - 1):
+        yield
+        down, mid = get(t, t), get(t, t + 1)
+        for r in range(t + 1, AZ - 1 - t):
+            up = get(t, r + 1)
+            new, change = _step(first + t, down, mid, up, nu(r), oc(r), os(r), lane)
+            add_square(t, r, change * change)
+            bufs[t % 2, r] = new
+            if r in (t + 1, AZ - 2 - t):
+                latest[r, g] = new
+            elif r in (t + 2, AZ - 3 - t):
+                earlier[r, g] = new
+            down, mid = mid, up
+
+
+def _valley(first, limit, own, halo, consts, add_square, bufs, final, lane):
+    nu, oc, os = consts
+
+    def get(t, x):
+        j = x if x >= 0 else -1 - x
+        if j < t:
+            return bufs[(t - 1) % 2, x + DEPTH]
+        latest, earlier = own if x >= 0 else halo
+        if j == t or j == SPAN:
+            return latest(j)
+        return earlier(j)
+
+    for t in range(SPAN):
+        yield
+        lo = -1 - min(t, limit - 1 - t)
         down, mid = get(t, lo - 1), get(t, lo)
-        for r in range(lo, hi + 1):
-            up = get(t, r + 1)
-            inward, outward = _sides(mid, lane)
-            source = cc * oc_of(r) if first + t == 0 else cc * oc_of(r) + ss * os_of(r)
-            change = nu_of(r) * ((down + up) + (inward + outward) - 4.0 * mid) + source
-            if -1 <= r <= AZ:
-                add_square(t, r, change * change)
-            bufs[t % 2, r + HMAX] = mid + change
+        for x in range(lo, t + 1):
+            up = get(t, x + 1)
+            new, change = _step(first + t, down, mid, up, nu(x), oc(x), os(x), lane)
+            if x >= -1:
+                add_square(x, change * change)
+            if t == SPAN - 1 and x >= 0:
+                final(x, new)
+            else:
+                bufs[t % 2, x + DEPTH] = new
             down, mid = mid, up
-    return lambda r: get(width - 1, r)
+    return bufs[SPAN % 2, DEPTH - 1]
 
 
 _CONSTS = ["lab", "nu", "oc", "os", "f_low", "f_high"]
-
-
-def _getters(R, g):
-    low, high = R["f_low"], R["f_high"]
-
-    def const(name, k):
-        def get(r):
-            if r < 0:
-                return low[AT[k] + LAYERS[k] + r, g]
-            if r >= AZ:
-                return high[AT[k] + r - AZ, g]
-            return R[name][r, g]
-
-        return get
-
-    label, oc, os = const("lab", 0), const("oc", 1), const("os", 2)
-    kept = {}
-
-    def nu(r):
-        if 0 <= r < AZ:
-            return R["nu"][r, g]
-        if r not in kept:
-            kept[r] = _reluct(label(r))
-        return kept[r]
-
-    def start(r):
+_STATE = ["latest", "earlier", "q"]
+
+
+def _label(R, g):
+    def get(r):
         if r < 0:
-            return low[H0 + r, g]
+            return R["f_low"][FIRST_AT[2] - 1 - r, g]
         if r >= AZ:
-            return high[r - AZ, g]
-        return R["a"][r, g]
-
-    return label, nu, oc, os, start
-
-
-def _run(index, R, g, bufs, lane):
-    first, width, reach = sum(WIDTHS[:index]), WIDTHS[index], REACH[index]
-    last = index == len(WIDTHS) - 1
-    label, nu, oc, os, start = _getters(R, g)
-
-    def state(r):
-        if index == 0:
-            return start(r)
-        if r < 0:
-            return R["low"][reach + r, g]
-        if r >= AZ:
-            return R["high"][r - AZ, g]
-        return R["a"][r, g]
-
-    def slot(r):
-        return (r + 1,) if last else (r + 1, g)
-
-    def add_square(t, r, sq):
-        if t > 0:
-            sq = R["q_out"][slot(r)] + sq
-        elif index:
-            sq = R["q"][r + 1, g] + sq
-            if not 0 <= r < AZ:
-                missed = state(r) - R["before"][0 if r < 0 else 1, g]
-                sq = sq + missed * missed
-        R["q_out"][slot(r)] = sq
-
-    return label, _advance(first, width, reach, state, nu, oc, os, add_square, bufs, lane)
-
-
-def _phase_kernel(index, names, *refs):
+            return R["f_high"][FIRST_AT[2] + r - AZ, g]
+        return R["lab"][r, g]
+
+    return get
+
+
+def _fill(second, R, g, q_slot, final, bufs, lane):
+    chains = []
+    for high in (False, True):
+        name = "high" if high else "low"
+        consts_from = R["f_" + name]
+        halo_from = R[name] if second else consts_from
+        n = NLATEST if second else DEPTH
+
+        def row(x, high=high):
+            return AZ - 1 - x if high else x
+
+        def const(name, k, row=row, consts_from=consts_from):
+            return lambda x: R[name][row(x), g] if x >= 0 else consts_from[FIRST_AT[k] - 1 - x, g]
+
+        kept = {}
+
+        def nu(x, row=row, consts_from=consts_from, kept=kept):
+            if x >= 0:
+                return R["nu"][row(x), g]
+            if x not in kept:
+                kept[x] = _reluct(consts_from[FIRST_AT[2] - 1 - x, g])
+            return kept[x]
+
+        own = (lambda j, row=row: R["latest"][row(j), g], lambda j, row=row: R["earlier"][row(j), g])
+        halo = (
+            lambda j, halo_from=halo_from: halo_from[j, g],
+            lambda j, halo_from=halo_from, n=n: halo_from[n + j - 1, g],
+        )
+        seen = set()
+
+        def add_square(x, sq, row=row, seen=seen, high=high, halo=halo):
+            r = row(x)
+            if r in seen:
+                before = R["q_out"][q_slot(r)]
+            else:
+                seen.add(r)
+                before = R["q"][r + 1, g]
+                if second and x < 0:
+                    missed = halo[0](0) - R["gone"][int(high), g]
+                    before = before + missed * missed
+            R["q_out"][q_slot(r)] = before + sq
+
+        chains.append(
+            _valley(
+                SPAN if second else 0,
+                SPAN if second else SPAN - 1,
+                own,
+                halo,
+                (nu, const("oc", 3), const("os", 4)),
+                add_square,
+                bufs.at[int(high)],
+                lambda x, v, row=row: final(row(x), v),
+                lane,
+            )
+        )
+    return chains
+
+
+def _middle_kernel(names, *refs):
     R = dict(zip(names, refs))
-    bufs = R["bufs"]
     lane, _ = _iotas()
-    n = REACH[index + 1]
-
-    def group(g):
-        _, previous = _run(index, R, g, bufs, lane)
-        a = bufs[(WIDTHS[index] - 1) % 2, HMAX : HMAX + AZ]
-        R["a_out"][:, g] = a
-        R["before_out"][0, g] = previous(-1)
-        R["before_out"][1, g] = previous(AZ)
-        R["e_low"][0:n, g] = a[0:n]
-        R["e_high"][0:n, g] = a[AZ - n :]
-        if index + 1 == PRIOR_AT:
-            R["e_low"][n : n + 2, g] = R["prior"][0:2, g]
-            R["e_high"][n : n + 2, g] = R["prior"][AZ - 2 :, g]
-
-    _loop(NG, group)
-
-
-def _losses(R, g, bufs, lane, store):
-    label, _ = _run(len(WIDTHS) - 1, R, g, bufs, lane)
-    for r in range(-1, AZ + 1):
-        lab = label(r)
-        store(r, _sigma(lab) * R["q_out"][r + 1], lab)
+
+    def groups(gs):
+        chains = []
+        for k, g in enumerate(gs):
+
+            def final(r, v, k=k):
+                R["rows"][k, r] = v
+
+            chains += _fill(False, R, g, lambda r, g=g: (r + 1, g), final, R["ends"].at[k], lane)
+        gone = _lockstep(chains)
+        chains = []
+        for k, g in enumerate(gs):
+            for end in range(2):
+                R["gone"][end, g] = gone[2 * k + end]
+            consts = [lambda r, name=name, g=g: R[name][r, g] for name in ("nu", "oc", "os")]
+
+            def add_square(t, r, sq, g=g):
+                R["q_out"][r + 1, g] = R["q_out"][r + 1, g] + sq
+
+            latest, earlier = R["latest_out"], R["earlier_out"]
+            start = lambda r, k=k: R["rows"][k, r]
+            chains.append(_triangle(SPAN, start, consts, add_square, latest, earlier, g, R["bufs"].at[k], lane))
+        _lockstep(chains)
+        for g in gs:
+            for name, row in (("e_low", lambda j: j), ("e_high", lambda j: AZ - 1 - j)):
+                for j in range(NLATEST):
+                    R[name][j, g] = latest[row(j), g]
+                for j in range(1, DEPTH + 1):
+                    R[name][NLATEST + j - 1, g] = earlier[row(j), g]
+
+    _pairs(groups)
+
+
+def _losses(R, gs, lane, store, final):
+    chains = []
+    for k, g in enumerate(gs):
+        chains += _fill(
+            True, R, g, lambda r, k=k: (k, r + 1), lambda r, v, k=k: final(k, r, v), R["ends"].at[k], lane
+        )
+    _lockstep(chains)
+    for k, g in enumerate(gs):
+        label = _label(R, g)
+        for r in range(-1, AZ + 1):
+            lab = label(r)
+            store(k, r, _sigma(lab) * R["q_out"][k, r + 1], lab)
 
 
 _T, _H, _J, _N, _L = range(5)
@@ -402,34 +520,39 @@
 def _ends_kernel(names, *refs):
     R = dict(zip(names, refs))
     lane, _ = _iotas()
-    for out, part, g, q in ((R["down"], R["part_lo"], ENDS[0], 0), (R["up"], R["part_hi"], ENDS[1], G - 1)):
+    outs, parts = (R["down"], R["up"]), (R["part_lo"], R["part_hi"])
+    for out, part in zip(outs, parts):
         out[...] = part[...]
 
-        def store(r, d, lab, out=out, part=part, q=q):
-            out[_N, r + 1 : r + 2, :] = part[_N, r + 1 : r + 2, :] + d[q : q + 1]
-
-        _losses(R, g, R["bufs"], lane, store)
+    def store(k, r, d, lab):
+        at, q = slice(r + 1, r + 2), (0, G - 1)[k]
+        outs[k][_N, at, :] = parts[k][_N, at, :] + d[q : q + 1]
+
+    _losses(R, ENDS, lane, store, lambda k, r, v: None)
 
 
 def _last_kernel(names, *refs):
     R = dict(zip(names, refs))
-    bufs = R["bufs"]
     lane, _ = _iotas()
 
-    def group(g):
-        def store(r, d, lab):
+    def groups(gs):
+        def final(k, r, v):
+            R["rows"][k, r] = v
+
+        def store(k, r, d, lab):
+            g = gs[k]
             t = R["base"][r + 1, g] + d * R["gain"][r + 1, g]
             R["t1"][r + 1, g] = t
             R["h1"][r + 1, g] = _half_cond(lab, t)
             if 0 <= r < AZ:
                 R["loss"][r, g] = d
 
-        _losses(R, g, bufs, lane, store)
-        a = bufs[(WIDTHS[-1] - 1) % 2, HMAX : HMAX + AZ]
-        R["closing"][_planes(g)] = jnp.swapaxes(a, 0, 1)
-        R["dissipation"][_planes(g)] = jnp.swapaxes(R["loss"][:, g], 0, 1)
-
-    _loop(NG, group)
+        _losses(R, gs, lane, store, final)
+        for k, g in enumerate(gs):
+            R["closing"][_planes(g)] = jnp.swapaxes(R["rows"][k], 0, 1)
+            R["dissipation"][_planes(g)] = jnp.swapaxes(R["loss"][:, g], 0, 1)
+
+    _pairs(groups)
 
 
 def _second_kernel(names, *refs):
@@ -478,18 +601,10 @@
     _loop(NG, turn)
 
 
-def _prior_rows(R, g):
-    n = REACH[PRIOR_AT]
-    label = _getters(R, g)[0]
-
-    def row(r):
-        if r < 0:
-            return R["low1"][n + 2 + r, g]
-        if r >= AZ:
-            return R["high1"][n + r - AZ, g]
+def _prior_row(R, g, r):
+    if 0 <= r < AZ:
         return R["prior"][r, g]
-
-    return row, label
+    return R["prior_more"][r + 2 if r < 0 else r - AZ + 2, g]
 
 
 def _ready_kernel(names, *refs):
@@ -497,9 +612,9 @@
     lane, sub = _iotas()
 
     def fill(g):
-        prior, label = _prior_rows(R, g)
+        label = _label(R, g)
         for r in range(-2, AZ + 2):
-            t, lab = prior(r), label(r)
+            t, lab = _prior_row(R, g, r), label(r)
             R["t0"][r + 2, g] = t
             R["h0"][r + 2, g] = _half_cond(lab, t)
             R["cap"][r + 2, g] = _capacity(lab)
@@ -522,7 +637,7 @@
 
     _loop(AZ + 2, row)
     for end, (out, g, q) in enumerate(((R["part_lo"], ENDS[0], 0), (R["part_hi"], ENDS[1], G - 1))):
-        label = _prior_rows(R, g)[1]
+        label = _label(R, g)
         plane = slice(q, q + 1)
         for k in range(AZ + 2):
             at = slice(k, k + 1)
@@ -547,18 +662,9 @@
 
 _OWN = (AZ, NG, G, RAD)
 _MORE = (AZ + 2, NG, G, RAD)
-_BUFS = (2, AZ + 2 * HMAX, G, RAD)
-_STATE = ["a", "q", "before", "low", "high"]
-_LAST = _CONSTS + _STATE
-_PRIOR = ["lab", "f_low", "f_high", "nu", "oc", "os", "prior", "low1", "high1"]
-
-
-def _phase(index, V):
-    n = REACH[index + 1] + (2 if index + 1 == PRIOR_AT else 0)
-    names = _CONSTS + (_STATE if index else ["a"]) + (["prior"] if index + 1 == PRIOR_AT else [])
-    outs = {"a_out": _OWN, "q_out": _MORE, "before_out": (2, NG, G, RAD)}
-    outs.update(e_low=(n, NG, G, RAD), e_high=(n, NG, G, RAD))
-    return _call(_phase_kernel, f"field_{index}", V, names, outs, {"bufs": _BUFS}, index)
+_FILL = {"ends": (2, 2, 2, SPAN + DEPTH, G, RAD), "rows": (2, AZ, G, RAD)}
+_LAST = _CONSTS + _STATE + ["gone", "low", "high"]
+_PRIOR = ["lab", "f_low", "f_high", "prior", "prior_more"]
 
 
 def _ring(axis, x, step, closed):
@@ -575,21 +681,20 @@
     V = {}
     V["f_low"], V["f_high"] = _around(*_edges(labels, exc, a0))
     got = lax.all_to_all(_prior_send(prior), "sec", 0, 0)
-    V["prior"] = _prior_take(got)
-    V.update(zip(("a", "lab", "nu", "oc", "os"), _prepare(labels, exc, a0)))
-    last = len(WIDTHS) - 1
-    for index in range(last):
-        out = _phase(index, V)
-        V["a"], V["q"], V["before"] = out["a_out"], out["q_out"], out["before_out"]
-        V["low"], V["high"] = _around(out["e_low"], out["e_high"])
-        if index + 1 == PRIOR_AT:
-            V["low1"], V["high1"] = V["low"], V["high"]
-        if index + 1 == last:
-            scratch = {name: (AZ + 4, NG, G, RAD) for name in ("t0", "h0", "cap")}
-            scratch.update(jac=(2, AZ + 2, G, RAD), flux=(2, AZ + 2, G, RAD))
-            outs = {"base": _MORE, "gain": _MORE, "part_lo": _END, "part_hi": _END}
-            V.update(_call(_ready_kernel, "first_ready", V, _PRIOR, outs, scratch))
-    scratch = {"bufs": _BUFS, "q_out": (AZ + 2, G, RAD)}
+    V.update(zip(_STATE + _CONSTS[:4], _prepare(labels, exc, a0)))
+    edge = (NLATEST + DEPTH, NG, G, RAD)
+    outs = {"latest_out": _OWN, "earlier_out": _OWN, "q_out": _MORE, "gone": (2, NG, G, RAD), "e_low": edge, "e_high": edge}
+    out = _call(_middle_kernel, "field_middle", V, _CONSTS + _STATE, outs, {"bufs": (2, 2, AZ, G, RAD), **_FILL})
+    V["low"], V["high"] = _around(out["e_low"], out["e_high"])
+    for name in _STATE:
+        V[name] = out[name + "_out"]
+    V["gone"] = out["gone"]
+    V["prior"], V["prior_more"] = _prior_take(got)
+    scratch = {name: (AZ + 4, NG, G, RAD) for name in ("t0", "h0", "cap")}
+    scratch.update(jac=(2, AZ + 2, G, RAD), flux=(2, AZ + 2, G, RAD))
+    outs = {"base": _MORE, "gain": _MORE, "part_lo": _END, "part_hi": _END}
+    V.update(_call(_ready_kernel, "first_ready", V, _PRIOR, outs, scratch))
+    scratch = {"q_out": (2, AZ + 2, G, RAD), **_FILL}
     outs = {"down": _END, "up": _END}
     V.update(_call(_ends_kernel, "last_ends", V, _LAST + ["part_lo", "part_hi"], outs, scratch))
     V["t_lo"], V["t_hi"] = _ring("ax", V["up"], 1, False), _ring("ax", V["down"], -1, False)

time: 140 us -> 131 us (0.936)
  starting transfers between devices: 36.3 us -> 26.1 us
  Pallas kernels: 37.6 us -> 44.1 us
  local copies, waits for them, and re-layouts: 9.8 us -> 7.07 us
  blocking collectives: 26.4 us -> 24 us
    ppermute x10 -> x6, starting transfers between devices: 29.6 us -> 19.3 us  [_ring(): lax.ppermute(x, axis, pairs if step > 0 else [(b, a) for a, b in pairs])]
    pallas_call x7 -> x5, Pallas kernels: 24.7 us -> 27.9 us  [_call(): pl.pallas_call(functools.partial(kernel, *bound, names + list(outs) + lis...]
    unnamed x28, local copies, waits for them, and re-layouts: 9.8 us -> 7.07 us
    pallas_call x3, Pallas kernels: 5.94 us -> 8.41 us  [the longest x1 3.79 us: _prior_take(): pl.pallas_call(_prior_take_kernel, out_shape=[_sds(AZ, NG, G, RAD), _sds(...]
    all_to_all x1, blocking collectives: 26.4 us -> 24 us  [shards(): temperature = _temperature_take(lax.all_to_all(out['blocks'], 'sec', 0, 0))]
    all_to_all x1, waiting for transfers between devices: 1.6 us -> 0.01 us  [shards(): got = lax.all_to_all(_prior_send(prior), 'sec', 0, 0)]
    ppermute x10 -> x6, waiting for transfers between devices: 24.8 us -> 26.3 us  [_ring(): lax.ppermute(x, axis, pairs if step > 0 else [(b, a) for a, b in pairs])]
  transfers between devices with their start and end apart: 11 -> 7, of which waited for: 4 -> 2; matrix products, arithmetic and copies ran while one was open for 0% -> 0% of each run, Pallas kernels for 14% -> 23%
where the time goes in v4:
time: 131 us; the launch traced here: 128 us
  Pallas kernels  44.1 us (34%)
  waiting for transfers between devices  26.3 us (20%)
  starting transfers between devices  26.1 us (20%)
  blocking collectives  24 us (18%)
  local copies, waits for them, and re-layouts  7.07 us (5%)
    pallas_call x5, Pallas kernels, _call(): pl.pallas_call(functools.partial(kernel, *bound, names + list(outs) + lis...  27.9 us
    ppermute x6, waiting for transfers between devices, _ring(): lax.ppermute(x, axis, pairs if step > 0 else [(b, a) for a, b in pairs])  26.3 us
    all_to_all x1, blocking collectives, shards(): temperature = _temperature_take(lax.all_to_all(out['blocks'], 'sec', 0, 0))  24 us
    ppermute x6, starting transfers between devices, _ring(): lax.ppermute(x, axis, pairs if step > 0 else [(b, a) for a, b in pairs])  19.3 us
    unnamed x28, local copies, waits for them, and re-layouts  7.07 us
    all_to_all x1, starting transfers between devices, shards(): got = lax.all_to_all(_prior_send(prior), 'sec', 0, 0)  6.79 us
    pallas_call x1, Pallas kernels, _edges(): pl.pallas_call(_edges_kernel, in_specs=[pl.BlockSpec(memory_space=pl.ANY)...  4.82 us
    pallas_call x1, Pallas kernels, _prior_take(): pl.pallas_call(_prior_take_kernel, out_shape=[_sds(AZ, NG, G, RAD), _sds(...  3.79 us
  transfers between devices with their start and end apart: 7, of which 2 were waited for; matrix products, arithmetic and copies ran while one was open for 0% of the time, Pallas kernels for 23%

profile of v4, /device:TPU:3, one launch (start us, length us, event | category | flops | bytes accessed | tf_op | source)
XLA Modules:
  0.0 128.3 jit_solution(8221166942169907121)
XLA Ops:
  0.6 4.8 %edge_layers.1 = (f32[20,8,8,256]{3,2,1,0:T(8,128)}, f32[20,8,8,256]{3,2,1,0:T(8,128)}) custom-call(s32[64,16,256]{2,1,0:T(8,128)} %lab_hbm.1, f32[2,64,16,256]{3,2,1,0:T(8,128)} %exc_hbm.1, f32[64,16,256]{2,1,0:T(8,128)} %a_hbm.1), custom_call_target="tpu_custom_call" | custom-call | flops 1048576 | bytes 6291456 | tf_op jit(solution)/shard_map/edge_layers/pallas_call | solution.py:140
  5.5 1.7 %collective-permute-start = (f32[20,8,8,256]{3,2,1,0:T(8,128)}, f32[20,8,8,256]{3,2,1,0:T(8,128)S(1)}, u32[]{:S(2)}, u32[]{:S(2)}) collective-permute-start(f32[20,8,8,256]{3,2,1,0:T(8,128)} %get-tuple-element.35), channel_id=1, source_target_pairs={{0,4},{4,8},{8,12},{12,16},{16,20},{20,24},{24,28},{28,32},{32,36}... | collective-permute-start | bytes 3932168 | tf_op jit(solution)/shard_map/ppermute | solution.py:673
  7.2 3.2 %collective-permute-start.1 = (f32[20,8,8,256]{3,2,1,0:T(8,128)}, f32[20,8,8,256]{3,2,1,0:T(8,128)}, u32[]{:S(2)}, u32[]{:S(2)}) collective-permute-start(f32[20,8,8,256]{3,2,1,0:T(8,128)} %get-tuple-element.36), channel_id=1, source_target_pairs={{4,0},{8,4},{12,8},{16,12},{20,16},{24,20},{28,24},{32,28},{36,32}... | collective-permute-start | bytes 3932168 | tf_op jit(solution)/shard_map/ppermute | solution.py:673
  10.4 1.4 %prior_send.1 = f32[32,5,16,128]{3,2,1,0:T(8,128)} custom-call(f32[64,8,512]{2,1,0:T(8,128)S(1)} %copy-done.13), custom_call_target="tpu_custom_call" | custom-call | flops 1048576 | bytes 3145728 | tf_op jit(solution)/shard_map/prior_send/pallas_call | solution.py:212
  11.8 6.8 %all-to-all-start = ((f32[32,5,16,128]{3,2,1,0:T(8,128)}), f32[32,5,16,128]{3,2,1,0:T(8,128)}, u32[]{:S(2)}, u32[]{:S(2)}) async-start(f32[32,5,16,128]{3,2,1,0:T(8,128)} %prior_send.1), calls=%async_computation | async-start | bytes 2621440 | tf_op jit(solution)/shard_map/all_to_all | solution.py:683
  18.6 0.0 copy-start.4
  18.6 1.6 %copy-done.4 = f32[2,64,16,256]{3,2,1,0:T(8,128)S(1)} copy-done((f32[2,64,16,256]{3,2,1,0:T(8,128)S(1)}, f32[2,64,16,256]{3,2,1,0:T(8,128)}, u32[]{:S(2)}) %copy-start.4) | copy-done | bytes 2097176
  20.2 1.2 copy-done.7
  21.4 1.2 copy-done.8
  22.6 3.2 %prepare.1 = (f32[16,8,8,256]{3,2,1,0:T(8,128)S(1)}, f32[16,8,8,256]{3,2,1,0:T(8,128)S(1)}, f32[18,8,8,256]{3,2,1,0:T(8,128)S(1)}, f32[16,8,8,256]{3,2,1,0:T(8,1...) custom-call(s32[64,16,256]{2,1,0:T(8,128)S(1)} %copy-done.7, ...), custom_call_target="tpu_custom_call" | custom-call | flops 4194304 | bytes 8388608 | tf_op jit(solution)/shard_map/prepare/pallas_call | solution.py:181
  25.8 0.0 copy-start
  25.8 0.0 copy-start.2
  25.9 23.6 %collective-permute-done.refs_4_.refs_1_ = f32[20,8,8,256]{3,2,1,0:T(8,128)S(1)} collective-permute-done((f32[20,8,8,256]{3,2,1,0:T(8,128)}, f32[20,8,8,256]{3,2,1,0:T(8,128)S(1)}, u32[]{:S(2)}, u32[]{:S(2)}) %collective-permute-start) | collective-permute-done | bytes 1310752 | tf_op jit(solution)/shard_map/ppermute | solution.py:673
  49.5 0.0 collective-permute-done.1.refs_5_.refs_2_
  49.5 8.6 %field_middle.1 = (f32[16,8,8,256]{3,2,1,0:T(8,128)S(1)}, f32[16,8,8,256]{3,2,1,0:T(8,128)S(1)}, f32[18,8,8,256]{3,2,1,0:T(8,128)S(1)}, f32[2,8,8,256]{3,2,1,0:T...) custom-call(f32[16,8,8,256]{3,2,1,0:T(8,128)S(1)} %get-tuple-element.31.refs_0_.refs_6_, ...), custom_call_target="tpu_custom_call" | custom-call | flops 16777216 | bytes 8388608 | tf_op jit(solution)/shard_map/field_middle/pallas_call | solution.py:652
  58.2 1.0 copy-done.5
  59.2 1.0 copy-done.9
  60.1 1.0 copy-done.11
  61.2 5.0 %collective-permute-start.3 = (f32[9,8,8,256]{3,2,1,0:T(8,128)}, f32[9,8,8,256]{3,2,1,0:T(8,128)}, u32[]{:S(2)}, u32[]{:S(2)}) collective-permute-start(f32[9,8,8,256]{3,2,1,0:T(8,128)} %get-tuple-element.45), channel_id=1, source_target_pairs={{4,0},{8,4},{12,8},{16,12},{20,16},{24,20},{28,24},{32,28},{36,32}... | collective-permute-start | bytes 1769480 | tf_op jit(solution)/shard_map/ppermute | solution.py:673
  66.1 3.8 %prior_take.1 = (f32[16,8,8,256]{3,2,1,0:T(8,128)S(1)}, f32[4,8,8,256]{3,2,1,0:T(8,128)S(1)}) custom-call(f32[32,5,16,128]{3,2,1,0:T(8,128)} %all-to-all-done.x_ref), custom_call_target="tpu_custom_call" | custom-call | flops 4194304 | bytes 3145728 | tf_op jit(solution)/shard_map/prior_take/pallas_call | solution.py:260
  69.9 0.0 copy-start.1
  70.0 0.0 copy-start.3
  70.0 0.0 copy-start.10
  70.0 4.7 %first_ready.1 = (f32[18,8,8,256]{3,2,1,0:T(8,128)S(1)}, f32[18,8,8,256]{3,2,1,0:T(8,128)S(1)}, f32[5,18,256]{2,1,0:T(8,128)S(1)}, f32[5,18,256]{2,1,0:T(8,128)S(1)}) custom-call(f32[16,8,8,256]{3,2,1,0:T(8,128)S(1)} %get-tuple-element.31.refs_0_.refs_6_, f32[20,8,8,256]{3,2,1,0:T(8,128)S(1)} %collective-permute-done.refs_4_.refs_1_, ...), custom_call_target="tpu_custom_call" | custom-call | flops 16777216 | bytes 8388608 | tf_op jit(solution)/shard_map/first_ready/pallas_call | solution.py:652
  74.7 2.7 %collective-permute-done.2.refs_10_ = f32[9,8,8,256]{3,2,1,0:T(8,128)} collective-permute-done((f32[9,8,8,256]{3,2,1,0:T(8,128)}, f32[9,8,8,256]{3,2,1,0:T(8,128)}, u32[]{:S(2)}, u32[]{:S(2)}) %collective-permute-start.2) | collective-permute-done | bytes 589856 | tf_op jit(solution)/shard_map/ppermute | solution.py:673
  77.4 2.8 %last_ends.1 = (f32[5,18,256]{2,1,0:T(8,128)S(1)}, f32[5,18,256]{2,1,0:T(8,128)S(1)}) custom-call(f32[16,8,8,256]{3,2,1,0:T(8,128)S(1)} %get-tuple-element.31.refs_0_.refs_6_, f32[16,8,8,256]{3,2,1,0:T(8,128)S(1)} %get-tuple-element.32.refs_1_, f32[16,8,8,256]{3,2,1,0:T(8,128)S(1)} %copy-done.1, f32[16,8,8,256]{3,2,1,0:T(8,128)S(1)} %copy-done.3, ...), custom_call_target="tpu_custom_call" | custom-call | flops 16777216 | bytes 8388608 | tf_op jit(solution)/shard_map/last_ends/pallas_call | solution.py:652
  80.3 5.2 %collective-permute-start.5 = (f32[5,18,256]{2,1,0:T(8,128)S(1)}, f32[5,18,256]{2,1,0:T(8,128)S(1)}, u32[]{:S(2)}, u32[]{:S(2)}) collective-permute-start(f32[5,18,256]{2,1,0:T(8,128)S(1)} %get-tuple-element.56.refs_2_), channel_id=1, source_target_pairs={{1,0},{2,1},{3,2},{5,4},{6,5},{7,6},{9,8},{10,9},{11,10},{13,12},{... | collective-permute-start | bytes 276488 | tf_op jit(solution)/shard_map/ppermute | solution.py:673
  85.5 4.2 %collective-permute-start.4 = (f32[5,18,256]{2,1,0:T(8,128)S(1)}, f32[5,18,256]{2,1,0:T(8,128)S(1)}, u32[]{:S(2)}, u32[]{:S(2)}) collective-permute-start(f32[5,18,256]{2,1,0:T(8,128)S(1)} %get-tuple-element.57.refs_3_), channel_id=1, source_target_pairs={{0,1},{1,2},{2,3},{4,5},{5,6},{6,7},{8,9},{9,10},{10,11},{12,13},{... | collective-permute-start | bytes 276488 | tf_op jit(solution)/shard_map/ppermute | solution.py:673
  89.7 8.3 %field_last.1 = (f32[64,16,256]{2,1,0:T(8,128)}, f32[64,16,256]{2,1,0:T(8,128)}, f32[18,8,8,256]{3,2,1,0:T(8,128)S(1)}, f32[18,8,8,256]{3,2,1,0:T(8,128)S(1)}, f32[16,8,8,256]{3,2,1,0:T(8,128)S(1)}) custom-call(f32[16,8,8,256]{3,2,1,0:T(8,128)S(1)} %get-tuple-element.31.refs_0_.refs_6_, f32[16,8,8,256]{3,2,1,0:T(8,128)S(1)} %get-tuple-element.32.refs_1_, ...), custom_call_target="tpu_custom_call" | custom-call | flops 16777216 | bytes 8388608 | tf_op jit(solution)/shard_map/field_last/pallas_call | solution.py:652
  98.0 3.4 %second_sweep.1 = f32[32,8,8,128]{3,2,1,0:T(8,128)S(1)} custom-call(f32[18,8,8,256]{3,2,1,0:T(8,128)S(1)} %get-tuple-element.52.refs_0_, f32[18,8,8,256]{3,2,1,0:T(8,128)S(1)} %get-tuple-element.53.refs_1_, f32[5,18,256]{2,1,0:T(8,128)S(1)} %get-tuple-element.56.refs_2_, f32[5,18,256]{2,1,0:T(8,128)S(1)} %get-tuple-element.57.refs_3_, ...), custom_call_target="tpu_custom_call" | custom-call | flops 16777216 | bytes 8388608 | tf_op jit(solution)/shard_map/second_sweep/pallas_call | solution.py:652
  101.4 24.0 %all_to_all.10.x_ref = f32[32,8,8,128]{3,2,1,0:T(8,128)S(1)} all-to-all(f32[32,8,8,128]{3,2,1,0:T(8,128)S(1)} %second_sweep.1), channel_id=1, replica_groups=mesh['sec'=32,'ax'=4] {'sec'}, dimensions={0} | all-to-all | bytes 2097152 | tf_op jit(solution)/shard_map/all_to_all | solution.py:707
  125.4 2.9 %temperature_take.1 = f32[64,8,512]{2,1,0:T(8,128)} custom-call(f32[32,8,8,128]{3,2,1,0:T(8,128)S(1)} %all_to_all.10.x_ref), custom_call_target="tpu_custom_call" | custom-call | flops 4194304 | bytes 2097152 | tf_op jit(solution)/shard_map/temperature_take/pallas_call | solution.py:280
  (21 shorter events, 0.0 us)
Async XLA Ops:
  0.6 9.7 %copy-start.13 = (f32[64,8,512]{2,1,0:T(8,128)S(1)}, f32[64,8,512]{2,1,0:T(8,128)}, u32[]{:S(2)}) copy-start(f32[64,8,512]{2,1,0:T(8,128)} %prior_ref.1) | copy-start | bytes 3145732
  5.5 44.0 %collective-permute-start = (f32[20,8,8,256]{3,2,1,0:T(8,128)}, f32[20,8,8,256]{3,2,1,0:T(8,128)S(1)}, u32[]{:S(2)}, u32[]{:S(2)}) collective-permute-start(f32[20,8,8,256]{3,2,1,0:T(8,128)} %get-tuple-element.35), channel_id=1, source_target_pairs={{0,4},{4,8},{8,12},{12,16},{16,20},{20,24},{24,28},{28,32},{32,36}... | collective-permute-start | bytes 3932168 | tf_op jit(solution)/shard_map/ppermute | solution.py:673
  7.2 42.3 %collective-permute-start.1 = (f32[20,8,8,256]{3,2,1,0:T(8,128)}, f32[20,8,8,256]{3,2,1,0:T(8,128)}, u32[]{:S(2)}, u32[]{:S(2)}) collective-permute-start(f32[20,8,8,256]{3,2,1,0:T(8,128)} %get-tuple-element.36), channel_id=1, source_target_pairs={{4,0},{8,4},{12,8},{16,12},{20,16},{24,20},{28,24},{32,28},{36,32}... | collective-permute-start | bytes 3932168 | tf_op jit(solution)/shard_map/ppermute | solution.py:673
  11.8 54.4 %all-to-all-start = ((f32[32,5,16,128]{3,2,1,0:T(8,128)}), f32[32,5,16,128]{3,2,1,0:T(8,128)}, u32[]{:S(2)}, u32[]{:S(2)}) async-start(f32[32,5,16,128]{3,2,1,0:T(8,128)} %prior_send.1), calls=%async_computation | async-start | bytes 2621440 | tf_op jit(solution)/shard_map/all_to_all | solution.py:683
  18.6 1.6 %copy-start.4 = (f32[2,64,16,256]{3,2,1,0:T(8,128)S(1)}, f32[2,64,16,256]{3,2,1,0:T(8,128)}, u32[]{:S(2)}) copy-start(f32[2,64,16,256]{3,2,1,0:T(8,128)} %exc_hbm.1) | copy-start | bytes 6291460
  20.2 1.2 copy-start.7
  21.4 1.2 copy-start.8
  25.8 32.3 %copy-start = (f32[16,8,8,256]{3,2,1,0:T(8,128)}, f32[16,8,8,256]{3,2,1,0:T(8,128)S(1)}, u32[]{:S(2)}) copy-start(f32[16,8,8,256]{3,2,1,0:T(8,128)S(1)} %get-tuple-element.33.refs_2_) | copy-start | bytes 3145732
  25.8 32.3 %copy-start.2 = (f32[16,8,8,256]{3,2,1,0:T(8,128)}, f32[16,8,8,256]{3,2,1,0:T(8,128)S(1)}, u32[]{:S(2)}) copy-start(f32[16,8,8,256]{3,2,1,0:T(8,128)S(1)} %get-tuple-element.34.refs_3_) | copy-start | bytes 3145732
  58.2 1.0 copy-start.5
  59.2 1.0 copy-start.9
  60.1 1.0 copy-start.11
  61.1 16.3 %collective-permute-start.2 = (f32[9,8,8,256]{3,2,1,0:T(8,128)}, f32[9,8,8,256]{3,2,1,0:T(8,128)}, u32[]{:S(2)}, u32[]{:S(2)}) collective-permute-start(f32[9,8,8,256]{3,2,1,0:T(8,128)} %get-tuple-element.44), channel_id=1, source_target_pairs={{0,4},{4,8},{8,12},{12,16},{16,20},{20,24},{24,28},{28,32},{32,36}... | collective-permute-start | bytes 1769480 | tf_op jit(solution)/shard_map/ppermute | solution.py:673
  61.2 16.3 %collective-permute-start.3 = (f32[9,8,8,256]{3,2,1,0:T(8,128)}, f32[9,8,8,256]{3,2,1,0:T(8,128)}, u32[]{:S(2)}, u32[]{:S(2)}) collective-permute-start(f32[9,8,8,256]{3,2,1,0:T(8,128)} %get-tuple-element.45), channel_id=1, source_target_pairs={{4,0},{8,4},{12,8},{16,12},{20,16},{24,20},{28,24},{32,28},{36,32}... | collective-permute-start | bytes 1769480 | tf_op jit(solution)/shard_map/ppermute | solution.py:673
  66.1 11.3 %copy-start.12 = (f32[16,8,8,256]{3,2,1,0:T(8,128)S(1)}, f32[16,8,8,256]{3,2,1,0:T(8,128)}, u32[]{:S(2)}) copy-start(f32[16,8,8,256]{3,2,1,0:T(8,128)} %copy-done.11) | copy-start | bytes 3145732
  69.9 7.5 %copy-start.1 = (f32[16,8,8,256]{3,2,1,0:T(8,128)S(1)}, f32[16,8,8,256]{3,2,1,0:T(8,128)}, u32[]{:S(2)}) copy-start(f32[16,8,8,256]{3,2,1,0:T(8,128)} %copy-done) | copy-start | bytes 3145732
  70.0 7.5 %copy-start.3 = (f32[16,8,8,256]{3,2,1,0:T(8,128)S(1)}, f32[16,8,8,256]{3,2,1,0:T(8,128)}, u32[]{:S(2)}) copy-start(f32[16,8,8,256]{3,2,1,0:T(8,128)} %copy-done.2) | copy-start | bytes 3145732
  70.0 7.5 %copy-start.6 = (f32[18,8,8,256]{3,2,1,0:T(8,128)S(1)}, f32[18,8,8,256]{3,2,1,0:T(8,128)}, u32[]{:S(2)}) copy-start(f32[18,8,8,256]{3,2,1,0:T(8,128)} %copy-done.5) | copy-start | bytes 3538948
  70.0 7.5 %copy-start.10 = (f32[16,8,8,256]{3,2,1,0:T(8,128)S(1)}, f32[16,8,8,256]{3,2,1,0:T(8,128)}, u32[]{:S(2)}) copy-start(f32[16,8,8,256]{3,2,1,0:T(8,128)} %copy-done.9) | copy-start | bytes 3145732
  80.3 17.7 %collective-permute-start.5 = (f32[5,18,256]{2,1,0:T(8,128)S(1)}, f32[5,18,256]{2,1,0:T(8,128)S(1)}, u32[]{:S(2)}, u32[]{:S(2)}) collective-permute-start(f32[5,18,256]{2,1,0:T(8,128)S(1)} %get-tuple-element.56.refs_2_), channel_id=1, source_target_pairs={{1,0},{2,1},{3,2},{5,4},{6,5},{7,6},{9,8},{10,9},{11,10},{13,12},{... | collective-permute-start | bytes 276488 | tf_op jit(solution)/shard_map/ppermute | solution.py:673
  85.5 12.5 %collective-permute-start.4 = (f32[5,18,256]{2,1,0:T(8,128)S(1)}, f32[5,18,256]{2,1,0:T(8,128)S(1)}, u32[]{:S(2)}, u32[]{:S(2)}) collective-permute-start(f32[5,18,256]{2,1,0:T(8,128)S(1)} %get-tuple-element.57.refs_3_), channel_id=1, source_target_pairs={{0,1},{1,2},{2,3},{4,5},{5,6},{6,7},{8,9},{9,10},{10,11},{12,13},{... | collective-permute-start | bytes 276488 | tf_op jit(solution)/shard_map/ppermute | solution.py:673

commit v5 on v4

--- a/solution.py
+++ b/solution.py
@@ -86,6 +86,20 @@
 
 def _capacity(lab):
     return jnp.where(lab == 1, 3.5, jnp.where(lab == 2, 0.5, 3.0)).astype(F32)
+
+
+def _corner(first, latest_count, rows, consts, store, lane):
+    top = 2 * DEPTH - 1 + latest_count - DEPTH
+    level = {j: rows(j) for j in range(top + 1)}
+    for t in range(latest_count):
+        yield
+        store(t, level[t])
+        if t < DEPTH:
+            store(latest_count + t, level[t + 1])
+        level = {
+            j: _step(first + t, level[j - 1], level[j], level[j + 1], *consts(j), lane)[0]
+            for j in range(t + 1, top - t)
+        }
 
 
 def _edges_kernel(lab_hbm, exc_hbm, a_hbm, low_ref, high_ref, lab_v, exc_v, a_v, sems):
@@ -106,23 +120,19 @@
     lane, _ = _iotas()
 
     def corner(g, out, row, a, c, s, lab):
-        nu, oc, os = {}, {}, {}
+        kept = {}
         for j in range(2 * DEPTH - 1):
             r = row(j)
-            nu[j], oc[j], os[j] = _reluct(lab[r]), _driven(lab[r], c[r]), _driven(lab[r], s[r])
+            kept[j] = _reluct(lab[r]), _driven(lab[r], c[r]), _driven(lab[r], s[r])
             if j < DEPTH:
                 out[FIRST_AT[2] + j, g] = lab[r].astype(F32)
-                out[FIRST_AT[3] + j, g] = oc[j]
-                out[FIRST_AT[4] + j, g] = os[j]
-        level = {j: a[row(j)] for j in range(2 * DEPTH)}
-        for t in range(DEPTH):
-            yield
-            out[FIRST_AT[0] + t, g] = level[t]
-            out[FIRST_AT[1] + t, g] = level[t + 1]
-            level = {
-                j: _step(t, level[j - 1], level[j], level[j + 1], nu[j], oc[j], os[j], lane)[0]
-                for j in range(t + 1, 2 * DEPTH - 1 - t)
-            }
+                out[FIRST_AT[3] + j, g] = kept[j][1]
+                out[FIRST_AT[4] + j, g] = kept[j][2]
+
+        def store(k, x):
+            out[k, g] = x
+
+        return _corner(0, DEPTH, lambda j: a[row(j)], lambda j: kept[j], store, lane)
 
     for pair in range(NG // 2):
         chains = []
@@ -267,19 +277,28 @@
     )(x)
 
 
-def _temperature_take_kernel(x_ref, out):
+def _temperature_take_kernel(x_ref, out, planes, sems):
+    def copy(g):
+        at = _planes(g)
+        return pltpu.make_async_copy(planes.at[at], out.at[at], sems.at[g])
+
     def group(g):
         tiles = [_swap_blocks([x_ref[s * 8 + j, g] for j in range(8)], AZ) for s in range(SEC // 8)]
         for q in range(G):
-            out[g * G + q] = jnp.concatenate([t[q] for t in tiles], axis=1)
+            planes[g * G + q] = jnp.concatenate([t[q] for t in tiles], axis=1)
+        copy(g).start()
 
     _loop(NG, group)
+    for g in range(NG):
+        copy(g).wait()
 
 
 def _temperature_take(x):
     return pl.pallas_call(
         _temperature_take_kernel,
         out_shape=_sds(AX, RL, ANG),
+        out_specs=pl.BlockSpec(memory_space=pl.ANY),
+        scratch_shapes=[pltpu.VMEM((AX, RL, ANG), F32), pltpu.SemaphoreType.DMA((NG,))],
         compiler_params=_params(),
         cost_estimate=_cost(2**22, 2**21),
         name="temperature_take",
@@ -471,32 +490,49 @@
         chains = []
         for k, g in enumerate(gs):
 
-            def final(r, v, k=k):
-                R["rows"][k, r] = v
+            def final(r, v, g=g):
+                R["rows8"][r, g] = v
 
             chains += _fill(False, R, g, lambda r, g=g: (r + 1, g), final, R["ends"].at[k], lane)
         gone = _lockstep(chains)
         chains = []
         for k, g in enumerate(gs):
-            for end in range(2):
+            for end, (name, row) in enumerate((("e_low", lambda j: j), ("e_high", lambda j: AZ - 1 - j))):
                 R["gone"][end, g] = gone[2 * k + end]
-            consts = [lambda r, name=name, g=g: R[name][r, g] for name in ("nu", "oc", "os")]
-
-            def add_square(t, r, sq, g=g):
-                R["q_out"][r + 1, g] = R["q_out"][r + 1, g] + sq
-
-            latest, earlier = R["latest_out"], R["earlier_out"]
-            start = lambda r, k=k: R["rows"][k, r]
-            chains.append(_triangle(SPAN, start, consts, add_square, latest, earlier, g, R["bufs"].at[k], lane))
+
+                def rows(j, g=g, row=row):
+                    return R["rows8"][row(j), g]
+
+                def consts(j, g=g, row=row):
+                    return [R[c][row(j), g] for c in ("nu", "oc", "os")]
+
+                def store(at, x, g=g, name=name):
+                    R[name][at, g] = x
+
+                chains.append(_corner(SPAN, NLATEST, rows, consts, store, lane))
         _lockstep(chains)
-        for g in gs:
-            for name, row in (("e_low", lambda j: j), ("e_high", lambda j: AZ - 1 - j)):
-                for j in range(NLATEST):
-                    R[name][j, g] = latest[row(j), g]
-                for j in range(1, DEPTH + 1):
-                    R[name][NLATEST + j - 1, g] = earlier[row(j), g]
 
     _pairs(groups)
+
+
+def _triangle_kernel(names, *refs):
+    R = dict(zip(names, refs))
+    lane, _ = _iotas()
+
+    def group(g, k):
+        q, q_out = R["q"], R["q_out"]
+        for r in (-1, 0, AZ - 1, AZ):
+            q_out[r + 1, g] = q[r + 1, g]
+
+        def add_square(t, r, sq):
+            q_out[r + 1, g] = (q if t == 0 else q_out)[r + 1, g] + sq
+
+        consts = [lambda r, name=name: R[name][r, g] for name in ("nu", "oc", "os")]
+        latest, earlier = R["latest_out"], R["earlier_out"]
+        start = lambda r: R["rows8"][r, g]
+        return _triangle(SPAN, start, consts, add_square, latest, earlier, g, R["bufs"].at[k], lane)
+
+    _pairs(lambda gs: _lockstep([group(g, k) for k, g in enumerate(gs)]))
 
 
 def _losses(R, gs, lane, store, final):
@@ -517,42 +553,68 @@
 _END = (5, AZ + 2, RAD)
 
 
-def _ends_kernel(names, *refs):
+def _last(R, gs, lane, rows, send=None):
+    def final(k, r, v):
+        rows[k, r] = v
+
+    def store(k, r, d, lab):
+        g = gs[k]
+        t = R["base"][r + 1, g] + d * R["gain"][r + 1, g]
+        R["t1_out"][r + 1, g] = t
+        R["h1_out"][r + 1, g] = _half_cond(lab, t)
+        if 0 <= r < AZ:
+            R["loss_out"][r, g] = d
+        if send is not None:
+            send(k, r, d)
+
+    _losses(R, gs, lane, store, final)
+
+
+def _last_ends_kernel(names, *refs):
     R = dict(zip(names, refs))
     lane, _ = _iotas()
     outs, parts = (R["down"], R["up"]), (R["part_lo"], R["part_hi"])
     for out, part in zip(outs, parts):
         out[...] = part[...]
 
-    def store(k, r, d, lab):
+    def send(k, r, d):
         at, q = slice(r + 1, r + 2), (0, G - 1)[k]
         outs[k][_N, at, :] = parts[k][_N, at, :] + d[q : q + 1]
 
-    _losses(R, ENDS, lane, store, lambda k, r, v: None)
+    _last(R, ENDS, lane, R["end_rows"], send)
 
 
 def _last_kernel(names, *refs):
     R = dict(zip(names, refs))
     lane, _ = _iotas()
-
-    def groups(gs):
-        def final(k, r, v):
-            R["rows"][k, r] = v
-
-        def store(k, r, d, lab):
-            g = gs[k]
-            t = R["base"][r + 1, g] + d * R["gain"][r + 1, g]
-            R["t1"][r + 1, g] = t
-            R["h1"][r + 1, g] = _half_cond(lab, t)
-            if 0 <= r < AZ:
-                R["loss"][r, g] = d
-
-        _losses(R, gs, lane, store, final)
+    closing, dissipation = R["closing_v"], R["dissipation_v"]
+
+    def copies(g):
+        at = _planes(g)
+        return [
+            pltpu.make_async_copy(closing.at[at], R["closing"].at[at], R["sems"].at[0, g]),
+            pltpu.make_async_copy(dissipation.at[at], R["dissipation"].at[at], R["sems"].at[1, g]),
+        ]
+
+    def natural(g, rows):
+        closing[_planes(g)] = jnp.swapaxes(rows, 0, 1)
+        dissipation[_planes(g)] = jnp.swapaxes(R["loss_out"][:, g], 0, 1)
+        for copy in copies(g):
+            copy.start()
+
+    for k, g in enumerate(ENDS):
+        natural(g, R["end_rows"][k])
+
+    def groups(i):
+        gs = [2 * i + 1, 2 * i + 2]
+        _last(R, gs, lane, R["rows"])
         for k, g in enumerate(gs):
-            R["closing"][_planes(g)] = jnp.swapaxes(R["rows"][k], 0, 1)
-            R["dissipation"][_planes(g)] = jnp.swapaxes(R["loss"][:, g], 0, 1)
-
-    _pairs(groups)
+            natural(g, R["rows"][k])
+
+    _loop(NG // 2 - 1, groups)
+    for g in range(NG):
+        for copy in copies(g):
+            copy.wait()
 
 
 def _second_kernel(names, *refs):
@@ -648,11 +710,17 @@
             out[_L, at, :] = label(k - 1)[plane]
 
 
-def _call(kernel, name, given, names, outs, scratch, *bound):
+def _call(kernel, name, given, names, outs, scratch, alias=(), apart=()):
+    shapes = {key: pltpu.VMEM(shape, F32) for key, shape in scratch.items()}
+    if apart:
+        shapes["sems"] = pltpu.SemaphoreType.DMA((len(apart), NG))
+    space = {True: pl.ANY, False: pltpu.VMEM}
     results = pl.pallas_call(
-        functools.partial(kernel, *bound, names + list(outs) + list(scratch)),
+        functools.partial(kernel, names + list(outs) + list(shapes)),
         out_shape=[_sds(*shape) for shape in outs.values()],
-        scratch_shapes=[pltpu.VMEM(shape, F32) for shape in scratch.values()],
+        out_specs=[pl.BlockSpec(memory_space=space[key in apart]) for key in outs],
+        scratch_shapes=list(shapes.values()),
+        input_output_aliases={names.index(key): list(outs).index(key + "_out") for key in alias},
         compiler_params=_params(),
         cost_estimate=_cost(2**24, 2**23),
         name=name,
@@ -662,8 +730,8 @@
 
 _OWN = (AZ, NG, G, RAD)
 _MORE = (AZ + 2, NG, G, RAD)
-_FILL = {"ends": (2, 2, 2, SPAN + DEPTH, G, RAD), "rows": (2, AZ, G, RAD)}
-_LAST = _CONSTS + _STATE + ["gone", "low", "high"]
+_ENDS = (2, 2, 2, SPAN + DEPTH, G, RAD)
+_LAST = _CONSTS + _STATE + ["gone", "low", "high", "base", "gain"]
 _PRIOR = ["lab", "f_low", "f_high", "prior", "prior_more"]
 
 
@@ -683,23 +751,34 @@
     got = lax.all_to_all(_prior_send(prior), "sec", 0, 0)
     V.update(zip(_STATE + _CONSTS[:4], _prepare(labels, exc, a0)))
     edge = (NLATEST + DEPTH, NG, G, RAD)
-    outs = {"latest_out": _OWN, "earlier_out": _OWN, "q_out": _MORE, "gone": (2, NG, G, RAD), "e_low": edge, "e_high": edge}
-    out = _call(_middle_kernel, "field_middle", V, _CONSTS + _STATE, outs, {"bufs": (2, 2, AZ, G, RAD), **_FILL})
+    outs = {"rows8": _OWN, "q_out": _MORE, "gone": (2, NG, G, RAD), "e_low": edge, "e_high": edge}
+    out = _call(_middle_kernel, "field_middle", V, _CONSTS + _STATE, outs, {"ends": _ENDS})
     V["low"], V["high"] = _around(out["e_low"], out["e_high"])
+    V.update(rows8=out["rows8"], q=out["q_out"], gone=out["gone"])
+    outs = {"latest_out": _OWN, "earlier_out": _OWN, "q_out": _MORE}
+    names = ["rows8", "q", "nu", "oc", "os"]
+    out = _call(_triangle_kernel, "field_triangle", V, names, outs, {"bufs": (2, 2, AZ, G, RAD)})
     for name in _STATE:
         V[name] = out[name + "_out"]
-    V["gone"] = out["gone"]
+    got, V["latest"] = lax.optimization_barrier((got, V["latest"]))
     V["prior"], V["prior_more"] = _prior_take(got)
     scratch = {name: (AZ + 4, NG, G, RAD) for name in ("t0", "h0", "cap")}
     scratch.update(jac=(2, AZ + 2, G, RAD), flux=(2, AZ + 2, G, RAD))
     outs = {"base": _MORE, "gain": _MORE, "part_lo": _END, "part_hi": _END}
     V.update(_call(_ready_kernel, "first_ready", V, _PRIOR, outs, scratch))
-    scratch = {"q_out": (2, AZ + 2, G, RAD), **_FILL}
-    outs = {"down": _END, "up": _END}
-    V.update(_call(_ends_kernel, "last_ends", V, _LAST + ["part_lo", "part_hi"], outs, scratch))
+    scratch = {"q_out": (2, AZ + 2, G, RAD), "ends": _ENDS}
+    state = {"t1_out": _MORE, "h1_out": _MORE, "loss_out": _OWN}
+    outs = {**state, "down": _END, "up": _END, "end_rows": (2, AZ, G, RAD)}
+    V.update(_call(_last_ends_kernel, "last_ends", V, _LAST + ["part_lo", "part_hi"], outs, scratch))
     V["t_lo"], V["t_hi"] = _ring("ax", V["up"], 1, False), _ring("ax", V["down"], -1, False)
-    outs = {"closing": (AX, AZ, RAD), "dissipation": (AX, AZ, RAD), "t1": _MORE, "h1": _MORE, "loss": _OWN}
-    V.update(_call(_last_kernel, "field_last", V, _LAST + ["base", "gain"], outs, scratch))
+    V.update(t1=V["t1_out"], h1=V["h1_out"], loss=V["loss_out"])
+    results = {"closing": (AX, AZ, RAD), "dissipation": (AX, AZ, RAD)}
+    scratch.update(rows=(2, AZ, G, RAD), closing_v=(AX, AZ, RAD), dissipation_v=(AX, AZ, RAD))
+    names = _LAST + ["end_rows", "t1", "h1", "loss"]
+    V.update(
+        _call(_last_kernel, "field_last", V, names, {**results, **state}, scratch, ["t1", "h1", "loss"], list(results))
+    )
+    V.update(t1=V["t1_out"], h1=V["h1_out"], loss=V["loss_out"])
     names = ["t1", "h1", "down", "up", "t_lo", "t_hi", "lab", "prior", "loss"]
     shape = (2, 2, AZ + 2, RAD)
     scratch = {"t2": _OWN, "own1": shape, "beside1": shape}

time: 131 us -> 126 us (0.962)
  waiting for transfers between devices: 26.3 us -> 23.7 us
  blocking collectives: 24 us -> 21.6 us
    ppermute x6, waiting for transfers between devices: 26.3 us -> 23.7 us  [_ring(): lax.ppermute(x, axis, pairs if step > 0 else [(b, a) for a, b in pairs])]
    all_to_all x1, blocking collectives: 24 us -> 21.6 us  [shards(): temperature = _temperature_take(lax.all_to_all(out['blocks'], 'sec', 0, 0))]
    pallas_call x6 -> x7, Pallas kernels: 30.8 us -> 30.8 us  [the longest x6 28.2 us: _call(): pl.pallas_call(functools.partial(kernel, names + list(outs) + list(shapes...]
  transfers between devices with their start and end apart: 7 -> 7, of which waited for: 2 -> 1; matrix products, arithmetic and copies ran while one was open for 0% -> 0% of each run, Pallas kernels for 23% -> 24%
where the time goes in v5:
time: 126 us; the launch traced here: 123 us
  Pallas kernels  44.1 us (35%)
  starting transfers between devices  26.1 us (21%)
  waiting for transfers between devices  23.7 us (19%)
  blocking collectives  21.6 us (17%)
  local copies, waits for them, and re-layouts  7.04 us (6%)
    pallas_call x6, Pallas kernels, _call(): pl.pallas_call(functools.partial(kernel, names + list(outs) + list(shapes...  28.2 us
    ppermute x6, waiting for transfers between devices, _ring(): lax.ppermute(x, axis, pairs if step > 0 else [(b, a) for a, b in pairs])  23.7 us
    all_to_all x1, blocking collectives, shards(): temperature = _temperature_take(lax.all_to_all(out['blocks'], 'sec', 0, 0))  21.6 us
    ppermute x6, starting transfers between devices, _ring(): lax.ppermute(x, axis, pairs if step > 0 else [(b, a) for a, b in pairs])  19.3 us
    unnamed x28, local copies, waits for them, and re-layouts  7.04 us
    all_to_all x1, starting transfers between devices, shards(): got = lax.all_to_all(_prior_send(prior), 'sec', 0, 0)  6.79 us
    pallas_call x1, Pallas kernels, _edges(): pl.pallas_call(_edges_kernel, in_specs=[pl.BlockSpec(memory_space=pl.ANY)...  4.84 us
    pallas_call x1, Pallas kernels, _prior_take(): pl.pallas_call(_prior_take_kernel, out_shape=[_sds(AZ, NG, G, RAD), _sds(...  3.79 us
  transfers between devices with their start and end apart: 7, of which 1 were waited for; matrix products, arithmetic and copies ran while one was open for 0% of the time, Pallas kernels for 24%

profile of v5, /device:TPU:3, one launch (start us, length us, event | category | flops | bytes accessed | tf_op | source)
XLA Modules:
  0.0 123.4 jit_solution(16695785839808051205)
XLA Ops:
  0.6 4.8 %edge_layers.1 = (f32[20,8,8,256]{3,2,1,0:T(8,128)}, f32[20,8,8,256]{3,2,1,0:T(8,128)}) custom-call(s32[64,16,256]{2,1,0:T(8,128)} %lab_hbm.1, f32[2,64,16,256]{3,2,1,0:T(8,128)} %exc_hbm.1, f32[64,16,256]{2,1,0:T(8,128)} %a_hbm.1), custom_call_target="tpu_custom_call" | custom-call | flops 1048576 | bytes 6291456 | tf_op jit(solution)/shard_map/edge_layers/pallas_call | solution.py:150
  5.5 1.7 %collective-permute-start = (f32[20,8,8,256]{3,2,1,0:T(8,128)}, f32[20,8,8,256]{3,2,1,0:T(8,128)S(1)}, u32[]{:S(2)}, u32[]{:S(2)}) collective-permute-start(f32[20,8,8,256]{3,2,1,0:T(8,128)} %get-tuple-element.43), channel_id=1, source_target_pairs={{0,4},{4,8},{8,12},{12,16},{16,20},{20,24},{24,28},{28,32},{32,36}... | collective-permute-start | bytes 3932168 | tf_op jit(solution)/shard_map/ppermute | solution.py:741
  7.2 3.2 %collective-permute-start.1 = (f32[20,8,8,256]{3,2,1,0:T(8,128)}, f32[20,8,8,256]{3,2,1,0:T(8,128)}, u32[]{:S(2)}, u32[]{:S(2)}) collective-permute-start(f32[20,8,8,256]{3,2,1,0:T(8,128)} %get-tuple-element.44), channel_id=1, source_target_pairs={{4,0},{8,4},{12,8},{16,12},{20,16},{24,20},{28,24},{32,28},{36,32}... | collective-permute-start | bytes 3932168 | tf_op jit(solution)/shard_map/ppermute | solution.py:741
  10.4 1.4 %prior_send.1 = f32[32,5,16,128]{3,2,1,0:T(8,128)} custom-call(f32[64,8,512]{2,1,0:T(8,128)S(1)} %copy-done.13), custom_call_target="tpu_custom_call" | custom-call | flops 1048576 | bytes 3145728 | tf_op jit(solution)/shard_map/prior_send/pallas_call | solution.py:222
  11.8 6.8 %all-to-all-start = ((f32[32,5,16,128]{3,2,1,0:T(8,128)}), f32[32,5,16,128]{3,2,1,0:T(8,128)}, u32[]{:S(2)}, u32[]{:S(2)}) async-start(f32[32,5,16,128]{3,2,1,0:T(8,128)} %prior_send.1), calls=%async_computation | async-start | bytes 2621440 | tf_op jit(solution)/shard_map/all_to_all | solution.py:751
  18.6 0.0 copy-start.4
  18.6 1.6 %copy-done.4 = f32[2,64,16,256]{3,2,1,0:T(8,128)S(1)} copy-done((f32[2,64,16,256]{3,2,1,0:T(8,128)S(1)}, f32[2,64,16,256]{3,2,1,0:T(8,128)}, u32[]{:S(2)}) %copy-start.4) | copy-done | bytes 2097176
  20.2 1.2 copy-done.7
  21.4 1.2 copy-done.8
  22.6 3.2 %prepare.1 = (f32[16,8,8,256]{3,2,1,0:T(8,128)S(1)}, f32[16,8,8,256]{3,2,1,0:T(8,128)S(1)}, f32[18,8,8,256]{3,2,1,0:T(8,128)S(1)}, f32[16,8,8,256]{3,2,1,0:T(8,1...) custom-call(s32[64,16,256]{2,1,0:T(8,128)S(1)} %copy-done.7, ...), custom_call_target="tpu_custom_call" | custom-call | flops 4194304 | bytes 8388608 | tf_op jit(solution)/shard_map/prepare/pallas_call | solution.py:191
  25.8 0.0 copy-start
  25.8 0.0 copy-start.2
  25.9 23.7 %collective-permute-done.refs_4_.refs_1_ = f32[20,8,8,256]{3,2,1,0:T(8,128)S(1)} collective-permute-done((f32[20,8,8,256]{3,2,1,0:T(8,128)}, f32[20,8,8,256]{3,2,1,0:T(8,128)S(1)}, u32[]{:S(2)}, u32[]{:S(2)}) %collective-permute-start) | collective-permute-done | bytes 1310752 | tf_op jit(solution)/shard_map/ppermute | solution.py:741
  49.5 0.0 collective-permute-done.1.refs_5_.refs_2_
  49.5 7.8 %field_middle.1 = (f32[16,8,8,256]{3,2,1,0:T(8,128)S(1)}, f32[18,8,8,256]{3,2,1,0:T(8,128)S(1)}, f32[2,8,8,256]{3,2,1,0:T(8,128)S(1)}, f32[9,8,8,256]{3,2,1,0:T(8,128)}, f32[9,8,8,256]{3,2,1,0:T(8,128)}) custom-call(f32[16,8,8,256]{3,2,1,0:T(8,128)S(1)} %get-tuple-element.39.refs_0_.refs_6_, f32[16,8,8,256]{3,2,1,0:T(8,128)S(1)} %get-tuple-element.40.refs_1_.refs_2_, ...), custom_call_target="tpu_custom_call" | custom-call | flops 16777216 | bytes 8388608 | tf_op jit(solution)/shard_map/field_middle/pallas_call | solution.py:718
  57.3 5.0 %collective-permute-start.3 = (f32[9,8,8,256]{3,2,1,0:T(8,128)}, f32[9,8,8,256]{3,2,1,0:T(8,128)}, u32[]{:S(2)}, u32[]{:S(2)}) collective-permute-start(f32[9,8,8,256]{3,2,1,0:T(8,128)} %get-tuple-element.56), channel_id=1, source_target_pairs={{4,0},{8,4},{12,8},{16,12},{20,16},{24,20},{28,24},{32,28},{36,32}... | collective-permute-start | bytes 1769480 | tf_op jit(solution)/shard_map/ppermute | solution.py:741
  62.3 2.6 %field_triangle.1 = (f32[16,8,8,256]{3,2,1,0:T(8,128)S(1)}, f32[16,8,8,256]{3,2,1,0:T(8,128)S(1)}, f32[18,8,8,256]{3,2,1,0:T(8,128)S(1)}) custom-call(f32[16,8,8,256]{3,2,1,0:T(8,128)S(1)} %get-tuple-element.48.refs_0_, f32[18,8,8,256]{3,2,1,0:T(8,128)S(1)} %get-tuple-element.49.refs_1_, f32[16,8,8,256]{3,2,1,0:T(8,128)S(1)} %get-tuple-element.40.refs_1_.refs_2_, ...), custom_call_target="tpu_custom_call" | custom-call | flops 16777216 | bytes 8388608 | tf_op jit(solution)/shard_map/field_triangle/pallas_call | solution.py:718
  64.9 1.0 copy-done.5
  65.9 1.0 copy-done.9
  66.9 1.0 copy-done.11
  67.9 3.8 %prior_take.1 = (f32[16,8,8,256]{3,2,1,0:T(8,128)S(1)}, f32[4,8,8,256]{3,2,1,0:T(8,128)S(1)}) custom-call(f32[32,5,16,128]{3,2,1,0:T(8,128)} %all-to-all-done.x_ref), custom_call_target="tpu_custom_call" | custom-call | flops 4194304 | bytes 3145728 | tf_op jit(solution)/shard_map/prior_take/pallas_call | solution.py:270
  71.7 0.0 copy-start.1
  71.7 0.0 copy-start.3
  71.7 0.0 copy-start.10
  71.7 4.8 %first_ready.1 = (f32[18,8,8,256]{3,2,1,0:T(8,128)S(1)}, f32[18,8,8,256]{3,2,1,0:T(8,128)S(1)}, f32[5,18,256]{2,1,0:T(8,128)S(1)}, f32[5,18,256]{2,1,0:T(8,128)S(1)}) custom-call(f32[16,8,8,256]{3,2,1,0:T(8,128)S(1)} %get-tuple-element.39.refs_0_.refs_6_, f32[20,8,8,256]{3,2,1,0:T(8,128)S(1)} %collective-permute-done.refs_4_.refs_1_, ...), custom_call_target="tpu_custom_call" | custom-call | flops 16777216 | bytes 8388608 | tf_op jit(solution)/shard_map/first_ready/pallas_call | solution.py:718
  76.6 3.0 %last_ends.1 = (f32[18,8,8,256]{3,2,1,0:T(8,128)S(1)}, f32[18,8,8,256]{3,2,1,0:T(8,128)S(1)}, f32[16,8,8,256]{3,2,1,0:T(8,128)S(1)}, f32[5,18,256]{2,1,0:T(8,128...) custom-call(f32[16,8,8,256]{3,2,1,0:T(8,128)S(1)} %get-tuple-element.39.refs_0_.refs_6_, ...), custom_call_target="tpu_custom_call" | custom-call | flops 16777216 | bytes 8388608 | tf_op jit(solution)/shard_map/last_ends/pallas_call | solution.py:718
  79.6 4.9 %collective-permute-start.5 = (f32[5,18,256]{2,1,0:T(8,128)S(1)}, f32[5,18,256]{2,1,0:T(8,128)S(1)}, u32[]{:S(2)}, u32[]{:S(2)}) collective-permute-start(f32[5,18,256]{2,1,0:T(8,128)S(1)} %get-tuple-element.72.refs_2_), channel_id=1, source_target_pairs={{1,0},{2,1},{3,2},{5,4},{6,5},{7,6},{9,8},{10,9},{11,10},{13,12},{... | collective-permute-start | bytes 276488 | tf_op jit(solution)/shard_map/ppermute | solution.py:741
  84.4 4.6 %collective-permute-start.4 = (f32[5,18,256]{2,1,0:T(8,128)S(1)}, f32[5,18,256]{2,1,0:T(8,128)S(1)}, u32[]{:S(2)}, u32[]{:S(2)}) collective-permute-start(f32[5,18,256]{2,1,0:T(8,128)S(1)} %get-tuple-element.73.refs_3_), channel_id=1, source_target_pairs={{0,1},{1,2},{2,3},{4,5},{5,6},{6,7},{8,9},{9,10},{10,11},{12,13},{... | collective-permute-start | bytes 276488 | tf_op jit(solution)/shard_map/ppermute | solution.py:741
  89.0 6.6 %field_last.1 = (f32[64,16,256]{2,1,0:T(8,128)}, f32[64,16,256]{2,1,0:T(8,128)}, f32[18,8,8,256]{3,2,1,0:T(8,128)S(1)}, f32[18,8,8,256]{3,2,1,0:T(8,128)S(1)}, f32[16,8,8,256]{3,2,1,0:T(8,128)S(1)}) custom-call(f32[16,8,8,256]{3,2,1,0:T(8,128)S(1)} %get-tuple-element.39.refs_0_.refs_6_, ...), custom_call_target="tpu_custom_call", output_to_operand_aliasing={{2}: (15, {}), {3}: (16, {}), {4}: (17, {})} | custom-call | flops 16777216 | bytes 8388608 | tf_op jit(solution)/shard_map/field_last/pallas_call | solution.py:718
  95.7 3.4 %second_sweep.1 = f32[32,8,8,128]{3,2,1,0:T(8,128)S(1)} custom-call(f32[18,8,8,256]{3,2,1,0:T(8,128)S(1)} %get-tuple-element.70.refs_0_, f32[18,8,8,256]{3,2,1,0:T(8,128)S(1)} %get-tuple-element.71.refs_1_, f32[5,18,256]{2,1,0:T(8,128)S(1)} %get-tuple-element.72.refs_2_, f32[5,18,256]{2,1,0:T(8,128)S(1)} %get-tuple-element.73.refs_3_, ...), custom_call_target="tpu_custom_call" | custom-call | flops 16777216 | bytes 8388608 | tf_op jit(solution)/shard_map/second_sweep/pallas_call | solution.py:718
  99.1 21.6 %all_to_all.10.x_ref = f32[32,8,8,128]{3,2,1,0:T(8,128)S(1)} all-to-all(f32[32,8,8,128]{3,2,1,0:T(8,128)S(1)} %second_sweep.1), channel_id=1, replica_groups=mesh['sec'=32,'ax'=4] {'sec'}, dimensions={0} | all-to-all | bytes 2097152 | tf_op jit(solution)/shard_map/all_to_all | solution.py:786
  120.7 2.7 %temperature_take.1 = f32[64,8,512]{2,1,0:T(8,128)} custom-call(f32[32,8,8,128]{3,2,1,0:T(8,128)S(1)} %all_to_all.10.x_ref), custom_call_target="tpu_custom_call" | custom-call | flops 4194304 | bytes 2097152 | tf_op jit(solution)/shard_map/temperature_take/pallas_call | solution.py:297
  (22 shorter events, 0.0 us)
Async XLA Ops:
  0.6 9.8 %copy-start.13 = (f32[64,8,512]{2,1,0:T(8,128)S(1)}, f32[64,8,512]{2,1,0:T(8,128)}, u32[]{:S(2)}) copy-start(f32[64,8,512]{2,1,0:T(8,128)} %prior_ref.1) | copy-start | bytes 3145732
  5.5 44.0 %collective-permute-start = (f32[20,8,8,256]{3,2,1,0:T(8,128)}, f32[20,8,8,256]{3,2,1,0:T(8,128)S(1)}, u32[]{:S(2)}, u32[]{:S(2)}) collective-permute-start(f32[20,8,8,256]{3,2,1,0:T(8,128)} %get-tuple-element.43), channel_id=1, source_target_pairs={{0,4},{4,8},{8,12},{12,16},{16,20},{20,24},{24,28},{28,32},{32,36}... | collective-permute-start | bytes 3932168 | tf_op jit(solution)/shard_map/ppermute | solution.py:741
  7.2 42.3 %collective-permute-start.1 = (f32[20,8,8,256]{3,2,1,0:T(8,128)}, f32[20,8,8,256]{3,2,1,0:T(8,128)}, u32[]{:S(2)}, u32[]{:S(2)}) collective-permute-start(f32[20,8,8,256]{3,2,1,0:T(8,128)} %get-tuple-element.44), channel_id=1, source_target_pairs={{4,0},{8,4},{12,8},{16,12},{20,16},{24,20},{28,24},{32,28},{36,32}... | collective-permute-start | bytes 3932168 | tf_op jit(solution)/shard_map/ppermute | solution.py:741
  11.8 56.1 %all-to-all-start = ((f32[32,5,16,128]{3,2,1,0:T(8,128)}), f32[32,5,16,128]{3,2,1,0:T(8,128)}, u32[]{:S(2)}, u32[]{:S(2)}) async-start(f32[32,5,16,128]{3,2,1,0:T(8,128)} %prior_send.1), calls=%async_computation | async-start | bytes 2621440 | tf_op jit(solution)/shard_map/all_to_all | solution.py:751
  18.6 1.6 %copy-start.4 = (f32[2,64,16,256]{3,2,1,0:T(8,128)S(1)}, f32[2,64,16,256]{3,2,1,0:T(8,128)}, u32[]{:S(2)}) copy-start(f32[2,64,16,256]{3,2,1,0:T(8,128)} %exc_hbm.1) | copy-start | bytes 6291460
  20.2 1.2 copy-start.7
  21.4 1.2 copy-start.8
  25.8 36.4 %copy-start = (f32[16,8,8,256]{3,2,1,0:T(8,128)}, f32[16,8,8,256]{3,2,1,0:T(8,128)S(1)}, u32[]{:S(2)}) copy-start(f32[16,8,8,256]{3,2,1,0:T(8,128)S(1)} %get-tuple-element.41.refs_2_.refs_3_) | copy-start | bytes 3145732
  25.8 36.4 %copy-start.2 = (f32[16,8,8,256]{3,2,1,0:T(8,128)}, f32[16,8,8,256]{3,2,1,0:T(8,128)S(1)}, u32[]{:S(2)}) copy-start(f32[16,8,8,256]{3,2,1,0:T(8,128)S(1)} %get-tuple-element.42.refs_3_.refs_4_) | copy-start | bytes 3145732
  57.3 19.2 %collective-permute-start.2 = (f32[9,8,8,256]{3,2,1,0:T(8,128)}, f32[9,8,8,256]{3,2,1,0:T(8,128)}, u32[]{:S(2)}, u32[]{:S(2)}) collective-permute-start(f32[9,8,8,256]{3,2,1,0:T(8,128)} %get-tuple-element.55), channel_id=1, source_target_pairs={{0,4},{4,8},{8,12},{12,16},{16,20},{20,24},{24,28},{28,32},{32,36}... | collective-permute-start | bytes 1769480 | tf_op jit(solution)/shard_map/ppermute | solution.py:741
  57.3 19.2 %collective-permute-start.3 = (f32[9,8,8,256]{3,2,1,0:T(8,128)}, f32[9,8,8,256]{3,2,1,0:T(8,128)}, u32[]{:S(2)}, u32[]{:S(2)}) collective-permute-start(f32[9,8,8,256]{3,2,1,0:T(8,128)} %get-tuple-element.56), channel_id=1, source_target_pairs={{4,0},{8,4},{12,8},{16,12},{20,16},{24,20},{28,24},{32,28},{36,32}... | collective-permute-start | bytes 1769480 | tf_op jit(solution)/shard_map/ppermute | solution.py:741
  64.9 1.0 copy-start.5
  65.9 1.0 copy-start.9
  66.9 1.0 copy-start.11
  67.9 8.7 %copy-start.12 = (f32[16,8,8,256]{3,2,1,0:T(8,128)S(1)}, f32[16,8,8,256]{3,2,1,0:T(8,128)}, u32[]{:S(2)}) copy-start(f32[16,8,8,256]{3,2,1,0:T(8,128)} %copy-done.11) | copy-start | bytes 3145732
  71.7 4.9 %copy-start.1 = (f32[16,8,8,256]{3,2,1,0:T(8,128)S(1)}, f32[16,8,8,256]{3,2,1,0:T(8,128)}, u32[]{:S(2)}) copy-start(f32[16,8,8,256]{3,2,1,0:T(8,128)} %copy-done) | copy-start | bytes 3145732
  71.7 4.9 %copy-start.3 = (f32[16,8,8,256]{3,2,1,0:T(8,128)S(1)}, f32[16,8,8,256]{3,2,1,0:T(8,128)}, u32[]{:S(2)}) copy-start(f32[16,8,8,256]{3,2,1,0:T(8,128)} %copy-done.2) | copy-start | bytes 3145732
  71.7 4.9 %copy-start.6 = (f32[18,8,8,256]{3,2,1,0:T(8,128)S(1)}, f32[18,8,8,256]{3,2,1,0:T(8,128)}, u32[]{:S(2)}) copy-start(f32[18,8,8,256]{3,2,1,0:T(8,128)} %copy-done.5) | copy-start | bytes 3538948
  71.7 4.9 %copy-start.10 = (f32[16,8,8,256]{3,2,1,0:T(8,128)S(1)}, f32[16,8,8,256]{3,2,1,0:T(8,128)}, u32[]{:S(2)}) copy-start(f32[16,8,8,256]{3,2,1,0:T(8,128)} %copy-done.9) | copy-start | bytes 3145732
  79.6 16.1 %collective-permute-start.5 = (f32[5,18,256]{2,1,0:T(8,128)S(1)}, f32[5,18,256]{2,1,0:T(8,128)S(1)}, u32[]{:S(2)}, u32[]{:S(2)}) collective-permute-start(f32[5,18,256]{2,1,0:T(8,128)S(1)} %get-tuple-element.72.refs_2_), channel_id=1, source_target_pairs={{1,0},{2,1},{3,2},{5,4},{6,5},{7,6},{9,8},{10,9},{11,10},{13,12},{... | collective-permute-start | bytes 276488 | tf_op jit(solution)/shard_map/ppermute | solution.py:741
  84.4 11.2 %collective-permute-start.4 = (f32[5,18,256]{2,1,0:T(8,128)S(1)}, f32[5,18,256]{2,1,0:T(8,128)S(1)}, u32[]{:S(2)}, u32[]{:S(2)}) collective-permute-start(f32[5,18,256]{2,1,0:T(8,128)S(1)} %get-tuple-element.73.refs_3_), channel_id=1, source_target_pairs={{0,1},{1,2},{2,3},{4,5},{5,6},{6,7},{8,9},{9,10},{10,11},{12,13},{... | collective-permute-start | bytes 276488 | tf_op jit(solution)/shard_map/ppermute | solution.py:741

commit v6 on v5

--- a/solution.py
+++ b/solution.py
@@ -102,7 +102,7 @@
         }
 
 
-def _edges_kernel(lab_hbm, exc_hbm, a_hbm, low_ref, high_ref, lab_v, exc_v, a_v, sems):
+def _edges_kernel(lab_hbm, exc_hbm, a_hbm, low_out, high_out, lab_v, exc_v, a_v, low_ref, high_ref, sems, out_sems):
     copies = []
     for g in range(NG):
         at = pl.ds(g * G, G)
@@ -119,6 +119,12 @@
 
     lane, _ = _iotas()
 
+    def sent(g):
+        return [
+            pltpu.make_async_copy(low_ref.at[:, g], low_out.at[:, g], out_sems.at[0, g]),
+            pltpu.make_async_copy(high_ref.at[:, g], high_out.at[:, g], out_sems.at[1, g]),
+        ]
+
     def corner(g, out, row, a, c, s, lab):
         kept = {}
         for j in range(2 * DEPTH - 1):
@@ -144,18 +150,28 @@
             chains.append(corner(g, low_ref, lambda j: j, *given))
             chains.append(corner(g, high_ref, lambda j: AZ - 1 - j, *given))
         _lockstep(chains)
+        for g in (2 * pair, 2 * pair + 1):
+            for copy in sent(g):
+                copy.start()
+    for g in range(NG):
+        for copy in sent(g):
+            copy.wait()
 
 
 def _edges(labels, exc, a):
     return pl.pallas_call(
         _edges_kernel,
         in_specs=[pl.BlockSpec(memory_space=pl.ANY)] * 3,
+        out_specs=[pl.BlockSpec(memory_space=pl.ANY)] * 2,
         out_shape=[_sds(NSEND, NG, G, RAD)] * 2,
         scratch_shapes=[
             pltpu.VMEM((AX, AZ, RAD), jnp.int32),
             pltpu.VMEM((2, AX, AZ, RAD), F32),
             pltpu.VMEM((AX, AZ, RAD), F32),
+            pltpu.VMEM((NSEND, NG, G, RAD), F32),
+            pltpu.VMEM((NSEND, NG, G, RAD), F32),
             pltpu.SemaphoreType.DMA((NG, 4)),
+            pltpu.SemaphoreType.DMA((2, NG)),
         ],
         compiler_params=_params(56),
         cost_estimate=_cost(2**20, 6 * 2**20),
@@ -244,7 +260,11 @@
     return x
 
 
-def _prior_take_kernel(x_ref, out, more, nat):
+def _prior_take_kernel(x_hbm, out, more, x_ref, nat, sems):
+    copies = [pltpu.make_async_copy(x_hbm.at[:, p], x_ref.at[:, p], sems.at[p]) for p in range(NP + 1)]
+    for copy in copies:
+        copy.start()
+
     def fill(p):
         for tile in range(AZ // 8):
             rows = slice(tile * 8, tile * 8 + 8)
@@ -254,11 +274,13 @@
                     nat[k, rows, half * 128 : half * 128 + 128] = got[k]
 
     def block(p):
+        pltpu.make_async_copy(x_hbm.at[:, p], x_ref.at[:, p], sems.at[p]).wait()
         fill(p)
         for k in range(PG // G):
             out[:, p * (PG // G) + k] = jnp.swapaxes(nat[k * G : k * G + G], 0, 1)
 
     _loop(NP, block)
+    copies[NP].wait()
     fill(NP)
     for k in range(PG // G):
         x = jnp.swapaxes(nat[k * G : k * G + G], 0, 1)
@@ -269,10 +291,15 @@
 def _prior_take(x):
     return pl.pallas_call(
         _prior_take_kernel,
+        in_specs=[pl.BlockSpec(memory_space=pl.ANY)],
         out_shape=[_sds(AZ, NG, G, RAD), _sds(4, NG, G, RAD)],
-        scratch_shapes=[pltpu.VMEM((PG, AZ, RAD), F32)],
+        scratch_shapes=[
+            pltpu.VMEM((SEC, NP + 1, AZ, PG * RL), F32),
+            pltpu.VMEM((PG, AZ, RAD), F32),
+            pltpu.SemaphoreType.DMA((NP + 1,)),
+        ],
         compiler_params=_params(),
-        cost_estimate=_cost(2**22, 3 * 2**20),
+        cost_estimate=_cost(2**24, 2**25),
         name="prior_take",
     )(x)
 
@@ -283,9 +310,10 @@
         return pltpu.make_async_copy(planes.at[at], out.at[at], sems.at[g])
 
     def group(g):
-        tiles = [_swap_blocks([x_ref[s * 8 + j, g] for j in range(8)], AZ) for s in range(SEC // 8)]
-        for q in range(G):
-            planes[g * G + q] = jnp.concatenate([t[q] for t in tiles], axis=1)
+        for s in range(SEC // 8):
+            got = _swap_blocks([x_ref[s * 8 + j, g] for j in range(8)], AZ)
+            for q in range(G):
+                planes[g * G + q, :, s * 128 : s * 128 + 128] = got[q]
         copy(g).start()
 
     _loop(NG, group)
@@ -409,17 +437,15 @@
     return bufs[SPAN % 2, DEPTH - 1]
 
 
-_CONSTS = ["lab", "nu", "oc", "os", "f_low", "f_high"]
+_CONSTS = ["nu", "oc", "os"]
 _STATE = ["latest", "earlier", "q"]
 
 
 def _label(R, g):
     def get(r):
-        if r < 0:
-            return R["f_low"][FIRST_AT[2] - 1 - r, g]
-        if r >= AZ:
-            return R["f_high"][FIRST_AT[2] + r - AZ, g]
-        return R["lab"][r, g]
+        if 0 <= r < AZ:
+            return R["lab"][r, g]
+        return R["lab_more"][r + 2 if r < 0 else r - AZ + 2, g]
 
     return get
 
@@ -485,8 +511,20 @@
 def _middle_kernel(names, *refs):
     R = dict(zip(names, refs))
     lane, _ = _iotas()
+    for g in range(NG):
+        for copy in _fetch(R, g):
+            copy.start()
+
+    def sent(g):
+        return [
+            pltpu.make_async_copy(R[name + "_v"].at[:, g], R[name].at[:, g], R["sems"].at[k, g])
+            for k, name in enumerate(("e_low", "e_high"))
+        ]
 
     def groups(gs):
+        for g in gs:
+            for copy in _fetch(R, g):
+                copy.wait()
         chains = []
         for k, g in enumerate(gs):
 
@@ -497,6 +535,9 @@
         gone = _lockstep(chains)
         chains = []
         for k, g in enumerate(gs):
+            at = FIRST_AT[2]
+            R["lab_more"][0, g], R["lab_more"][1, g] = R["f_low"][at + 1, g], R["f_low"][at, g]
+            R["lab_more"][2, g], R["lab_more"][3, g] = R["f_high"][at, g], R["f_high"][at + 1, g]
             for end, (name, row) in enumerate((("e_low", lambda j: j), ("e_high", lambda j: AZ - 1 - j))):
                 R["gone"][end, g] = gone[2 * k + end]
 
@@ -507,12 +548,18 @@
                     return [R[c][row(j), g] for c in ("nu", "oc", "os")]
 
                 def store(at, x, g=g, name=name):
-                    R[name][at, g] = x
+                    R[name + "_v"][at, g] = x
 
                 chains.append(_corner(SPAN, NLATEST, rows, consts, store, lane))
         _lockstep(chains)
+        for g in gs:
+            for copy in sent(g):
+                copy.start()
 
     _pairs(groups)
+    for g in range(NG):
+        for copy in sent(g):
+            copy.wait()
 
 
 def _triangle_kernel(names, *refs):
@@ -574,8 +621,13 @@
     R = dict(zip(names, refs))
     lane, _ = _iotas()
     outs, parts = (R["down"], R["up"]), (R["part_lo"], R["part_hi"])
+    copies = [copy for g in ENDS for copy in _fetch(R, g, FIRST_AT[2])]
+    for copy in copies:
+        copy.start()
     for out, part in zip(outs, parts):
         out[...] = part[...]
+    for copy in copies:
+        copy.wait()
 
     def send(k, r, d):
         at, q = slice(r + 1, r + 2), (0, G - 1)[k]
@@ -602,11 +654,17 @@
         for copy in copies(g):
             copy.start()
 
+    for g in range(1, NG - 1):
+        for copy in _fetch(R, g, FIRST_AT[2]):
+            copy.start()
     for k, g in enumerate(ENDS):
         natural(g, R["end_rows"][k])
 
     def groups(i):
         gs = [2 * i + 1, 2 * i + 2]
+        for g in gs:
+            for copy in _fetch(R, g, FIRST_AT[2]):
+                copy.wait()
         _last(R, gs, lane, R["rows"])
         for k, g in enumerate(gs):
             natural(g, R["rows"][k])
@@ -656,11 +714,12 @@
 
     _loop(AZ, row)
 
-    def turn(g):
-        nat = jnp.swapaxes(R["t2"][:, g], 0, 1).reshape(G * AZ, RAD)
-        R["blocks"][:, g] = jnp.transpose(nat).reshape(SEC, RL, G * AZ)
-
-    _loop(NG, turn)
+    def turn(i):
+        for g in [4 * i + k for k in range(4)]:
+            nat = jnp.swapaxes(R["t2"][:, g], 0, 1).reshape(G * AZ, RAD)
+            R["blocks"][:, g] = jnp.transpose(nat).reshape(SEC, RL, G * AZ)
+
+    _loop(NG // 4, turn)
 
 
 def _prior_row(R, g, r):
@@ -669,9 +728,8 @@
     return R["prior_more"][r + 2 if r < 0 else r - AZ + 2, g]
 
 
-def _ready_kernel(names, *refs):
+def _warmth_kernel(names, *refs):
     R = dict(zip(names, refs))
-    lane, sub = _iotas()
 
     def fill(g):
         label = _label(R, g)
@@ -682,6 +740,11 @@
             R["cap"][r + 2, g] = _capacity(lab)
 
     _loop(NG, fill)
+
+
+def _ready_kernel(names, *refs):
+    R = dict(zip(names, refs))
+    lane, sub = _iotas()
 
     def row(k):
         for g in range(NG):
@@ -710,19 +773,34 @@
             out[_L, at, :] = label(k - 1)[plane]
 
 
-def _call(kernel, name, given, names, outs, scratch, alias=(), apart=()):
+def _fetch(R, g, skip=0):
+    copies = []
+    for k, name in enumerate(sorted(key for key in R if "apart " + key in R)):
+        lo = skip if name.startswith("f_") else 0
+        at = pl.ds(lo, R[name].shape[0] - lo)
+        copies.append(pltpu.make_async_copy(R["apart " + name].at[at, g], R[name].at[at, g], R["in_sems"].at[k, g]))
+    return copies
+
+
+def _call(kernel, name, given, names, outs, scratch, alias=(), apart=(), fetch=()):
+    given = {**given, **{"apart " + key: given[key] for key in fetch}}
+    names = names + ["apart " + key for key in fetch]
     shapes = {key: pltpu.VMEM(shape, F32) for key, shape in scratch.items()}
+    shapes.update({key: pltpu.VMEM(given[key].shape, F32) for key in fetch})
+    if fetch:
+        shapes["in_sems"] = pltpu.SemaphoreType.DMA((len(fetch), NG))
     if apart:
         shapes["sems"] = pltpu.SemaphoreType.DMA((len(apart), NG))
     space = {True: pl.ANY, False: pltpu.VMEM}
     results = pl.pallas_call(
         functools.partial(kernel, names + list(outs) + list(shapes)),
         out_shape=[_sds(*shape) for shape in outs.values()],
+        in_specs=[pl.BlockSpec(memory_space=space[key.startswith("apart ")]) for key in names],
         out_specs=[pl.BlockSpec(memory_space=space[key in apart]) for key in outs],
         scratch_shapes=list(shapes.values()),
         input_output_aliases={names.index(key): list(outs).index(key + "_out") for key in alias},
         compiler_params=_params(),
-        cost_estimate=_cost(2**24, 2**23),
+        cost_estimate=_cost(2**24, 2**25),
         name=name,
     )(*[given[key] for key in names])
     return dict(zip(outs, results))
@@ -731,8 +809,9 @@
 _OWN = (AZ, NG, G, RAD)
 _MORE = (AZ + 2, NG, G, RAD)
 _ENDS = (2, 2, 2, SPAN + DEPTH, G, RAD)
-_LAST = _CONSTS + _STATE + ["gone", "low", "high", "base", "gain"]
-_PRIOR = ["lab", "f_low", "f_high", "prior", "prior_more"]
+_LAST = _CONSTS + _STATE + ["lab", "lab_more", "gone", "base", "gain"]
+_FETCH = ["f_low", "f_high", "low", "high"]
+_PRIOR = ["lab", "lab_more", "prior", "prior_more"]
 
 
 def _ring(axis, x, step, closed):
@@ -749,12 +828,14 @@
     V = {}
     V["f_low"], V["f_high"] = _around(*_edges(labels, exc, a0))
     got = lax.all_to_all(_prior_send(prior), "sec", 0, 0)
-    V.update(zip(_STATE + _CONSTS[:4], _prepare(labels, exc, a0)))
+    V.update(zip(_STATE + ["lab"] + _CONSTS, _prepare(labels, exc, a0)))
     edge = (NLATEST + DEPTH, NG, G, RAD)
-    outs = {"rows8": _OWN, "q_out": _MORE, "gone": (2, NG, G, RAD), "e_low": edge, "e_high": edge}
-    out = _call(_middle_kernel, "field_middle", V, _CONSTS + _STATE, outs, {"ends": _ENDS})
+    outs = {"rows8": _OWN, "q_out": _MORE, "gone": (2, NG, G, RAD), "lab_more": (4, NG, G, RAD)}
+    outs.update(e_low=edge, e_high=edge)
+    scratch = {"ends": _ENDS, "e_low_v": edge, "e_high_v": edge}
+    out = _call(_middle_kernel, "field_middle", V, _CONSTS + _STATE, outs, scratch, (), ["e_low", "e_high"], ["f_low", "f_high"])
     V["low"], V["high"] = _around(out["e_low"], out["e_high"])
-    V.update(rows8=out["rows8"], q=out["q_out"], gone=out["gone"])
+    V.update(rows8=out["rows8"], q=out["q_out"], gone=out["gone"], lab_more=out["lab_more"])
     outs = {"latest_out": _OWN, "earlier_out": _OWN, "q_out": _MORE}
     names = ["rows8", "q", "nu", "oc", "os"]
     out = _call(_triangle_kernel, "field_triangle", V, names, outs, {"bufs": (2, 2, AZ, G, RAD)})
@@ -762,21 +843,24 @@
         V[name] = out[name + "_out"]
     got, V["latest"] = lax.optimization_barrier((got, V["latest"]))
     V["prior"], V["prior_more"] = _prior_take(got)
-    scratch = {name: (AZ + 4, NG, G, RAD) for name in ("t0", "h0", "cap")}
-    scratch.update(jac=(2, AZ + 2, G, RAD), flux=(2, AZ + 2, G, RAD))
+    warmth = {name: (AZ + 4, NG, G, RAD) for name in ("t0", "h0", "cap")}
+    V.update(_call(_warmth_kernel, "prior_warmth", V, _PRIOR, warmth, {}))
+    scratch = {"jac": (2, AZ + 2, G, RAD), "flux": (2, AZ + 2, G, RAD)}
     outs = {"base": _MORE, "gain": _MORE, "part_lo": _END, "part_hi": _END}
-    V.update(_call(_ready_kernel, "first_ready", V, _PRIOR, outs, scratch))
+    V.update(_call(_ready_kernel, "first_ready", V, ["lab", "lab_more", *warmth], outs, scratch))
     scratch = {"q_out": (2, AZ + 2, G, RAD), "ends": _ENDS}
     state = {"t1_out": _MORE, "h1_out": _MORE, "loss_out": _OWN}
+    names = _LAST + ["part_lo", "part_hi"]
     outs = {**state, "down": _END, "up": _END, "end_rows": (2, AZ, G, RAD)}
-    V.update(_call(_last_ends_kernel, "last_ends", V, _LAST + ["part_lo", "part_hi"], outs, scratch))
+    V.update(_call(_last_ends_kernel, "last_ends", V, names, outs, scratch, fetch=_FETCH))
     V["t_lo"], V["t_hi"] = _ring("ax", V["up"], 1, False), _ring("ax", V["down"], -1, False)
     V.update(t1=V["t1_out"], h1=V["h1_out"], loss=V["loss_out"])
     results = {"closing": (AX, AZ, RAD), "dissipation": (AX, AZ, RAD)}
     scratch.update(rows=(2, AZ, G, RAD), closing_v=(AX, AZ, RAD), dissipation_v=(AX, AZ, RAD))
     names = _LAST + ["end_rows", "t1", "h1", "loss"]
+    outs = {**results, **state}
     V.update(
-        _call(_last_kernel, "field_last", V, names, {**results, **state}, scratch, ["t1", "h1", "loss"], list(results))
+        _call(_last_kernel, "field_last", V, names, outs, scratch, ["t1", "h1", "loss"], list(results), _FETCH)
     )
     V.update(t1=V["t1_out"], h1=V["h1_out"], loss=V["loss_out"])
     names = ["t1", "h1", "down", "up", "t_lo", "t_hi", "lab", "prior", "loss"]

time: 126 us -> 125 us (level)
  Pallas kernels: 44.1 us -> 40.7 us
  blocking collectives: 21.6 us -> 23.5 us
    pallas_call x6 -> x7, Pallas kernels: 28.2 us -> 25.6 us  [_call(): pl.pallas_call(functools.partial(kernel, names + list(outs) + list(shapes...]
    all_to_all x1, blocking collectives: 21.6 us -> 23.5 us  [shards(): temperature = _temperature_take(lax.all_to_all(out['blocks'], 'sec', 0, 0))]
    unnamed x28 -> x24, local copies, waits for them, and re-layouts: 7.04 us -> 7.04 us
  transfers between devices with their start and end apart: 7 -> 7, of which waited for: 1 -> 3; matrix products, arithmetic and copies ran while one was open for 0% -> 0% of each run, Pallas kernels for 24% -> 23%
where the time goes in v6:
time: 125 us; the launch traced here: 122 us
  Pallas kernels  40.7 us (33%)
  starting transfers between devices  25.5 us (20%)
  waiting for transfers between devices  24.4 us (20%)
  blocking collectives  23.5 us (19%)
  local copies, waits for them, and re-layouts  7.04 us (6%)
    pallas_call x7, Pallas kernels, _call(): pl.pallas_call(functools.partial(kernel, names + list(outs) + list(shapes...  25.6 us
    ppermute x6, waiting for transfers between devices, _ring(): lax.ppermute(x, axis, pairs if step > 0 else [(b, a) for a, b in pairs])  24.4 us
    all_to_all x1, blocking collectives, shards(): temperature = _temperature_take(lax.all_to_all(out['blocks'], 'sec', 0, 0))  23.5 us
    ppermute x6, starting transfers between devices, _ring(): lax.ppermute(x, axis, pairs if step > 0 else [(b, a) for a, b in pairs])  18.7 us
    unnamed x24, local copies, waits for them, and re-layouts  7.04 us
    all_to_all x1, starting transfers between devices, shards(): got = lax.all_to_all(_prior_send(prior), 'sec', 0, 0)  6.79 us
    pallas_call x1, Pallas kernels, _edges(): pl.pallas_call(_edges_kernel, in_specs=[pl.BlockSpec(memory_space=pl.ANY)...  4.42 us
    pallas_call x1, Pallas kernels, _prior_take(): pl.pallas_call(_prior_take_kernel, in_specs=[pl.BlockSpec(memory_space=pl...  3.39 us
  transfers between devices with their start and end apart: 7, of which 3 were waited for; matrix products, arithmetic and copies ran while one was open for 0% of the time, Pallas kernels for 23%

profile of v6, /device:TPU:3, one launch (start us, length us, event | category | flops | bytes accessed | tf_op | source)
XLA Modules:
  0.0 122.1 jit_solution(12594615267411261431)
XLA Ops:
  0.6 4.4 %edge_layers.1 = (f32[20,8,8,256]{3,2,1,0:T(8,128)}, f32[20,8,8,256]{3,2,1,0:T(8,128)}) custom-call(s32[64,16,256]{2,1,0:T(8,128)} %lab_hbm.1, f32[2,64,16,256]{3,2,1,0:T(8,128)} %exc_hbm.1, f32[64,16,256]{2,1,0:T(8,128)} %a_hbm.1), custom_call_target="tpu_custom_call" | custom-call | flops 1048576 | bytes 6291456 | tf_op jit(solution)/shard_map/edge_layers/pallas_call | solution.py:162
  5.1 1.7 %collective-permute-start = (f32[20,8,8,256]{3,2,1,0:T(8,128)}, f32[20,8,8,256]{3,2,1,0:T(8,128)}, u32[]{:S(2)}, u32[]{:S(2)}) collective-permute-start(f32[20,8,8,256]{3,2,1,0:T(8,128)} %get-tuple-element.49), channel_id=1, source_target_pairs={{0,4},{4,8},{8,12},{12,16},{16,20},{20,24},{24,28},{28,32},{32,36}... | collective-permute-start | bytes 3932168 | tf_op jit(solution)/shard_map/ppermute | solution.py:820
  6.8 3.2 %collective-permute-start.1 = (f32[20,8,8,256]{3,2,1,0:T(8,128)}, f32[20,8,8,256]{3,2,1,0:T(8,128)}, u32[]{:S(2)}, u32[]{:S(2)}) collective-permute-start(f32[20,8,8,256]{3,2,1,0:T(8,128)} %get-tuple-element.50), channel_id=1, source_target_pairs={{4,0},{8,4},{12,8},{16,12},{20,16},{24,20},{28,24},{32,28},{36,32}... | collective-permute-start | bytes 3932168 | tf_op jit(solution)/shard_map/ppermute | solution.py:820
  10.0 1.4 %prior_send.1 = f32[32,5,16,128]{3,2,1,0:T(8,128)} custom-call(f32[64,8,512]{2,1,0:T(8,128)S(1)} %copy-done.11), custom_call_target="tpu_custom_call" | custom-call | flops 1048576 | bytes 3145728 | tf_op jit(solution)/shard_map/prior_send/pallas_call | solution.py:238
  11.4 6.8 %all-to-all-start = ((f32[32,5,16,128]{3,2,1,0:T(8,128)}), f32[32,5,16,128]{3,2,1,0:T(8,128)}, u32[]{:S(2)}, u32[]{:S(2)}) async-start(f32[32,5,16,128]{3,2,1,0:T(8,128)} %prior_send.1), calls=%async_computation | async-start | bytes 2621440 | tf_op jit(solution)/shard_map/all_to_all | solution.py:830
  18.2 0.0 copy-start.2
  18.2 1.6 %copy-done.2 = f32[2,64,16,256]{3,2,1,0:T(8,128)S(1)} copy-done((f32[2,64,16,256]{3,2,1,0:T(8,128)S(1)}, f32[2,64,16,256]{3,2,1,0:T(8,128)}, u32[]{:S(2)}) %copy-start.2) | copy-done | bytes 2097176
  19.8 1.2 %copy-done.5 = s32[64,16,256]{2,1,0:T(8,128)S(1)} copy-done((s32[64,16,256]{2,1,0:T(8,128)S(1)}, s32[64,16,256]{2,1,0:T(8,128)}, u32[]{:S(2)}) %copy-start.5) | copy-done | bytes 1048600
  21.0 1.2 %copy-done.6 = f32[64,16,256]{2,1,0:T(8,128)S(1)} copy-done((f32[64,16,256]{2,1,0:T(8,128)S(1)}, f32[64,16,256]{2,1,0:T(8,128)}, u32[]{:S(2)}) %copy-start.6) | copy-done | bytes 1048600
  22.2 3.2 %prepare.1 = (f32[16,8,8,256]{3,2,1,0:T(8,128)S(1)}, f32[16,8,8,256]{3,2,1,0:T(8,128)S(1)}, f32[18,8,8,256]{3,2,1,0:T(8,128)S(1)}, f32[16,8,8,256]{3,2,1,0:T(8,1...) custom-call(s32[64,16,256]{2,1,0:T(8,128)S(1)} %copy-done.5, ...), custom_call_target="tpu_custom_call" | custom-call | flops 4194304 | bytes 8388608 | tf_op jit(solution)/shard_map/prepare/pallas_call | solution.py:207
  25.4 0.0 copy-start
  25.5 23.8 %collective-permute-done.refs_6_.refs_13_.refs_15_ = f32[20,8,8,256]{3,2,1,0:T(8,128)} collective-permute-done((f32[20,8,8,256]{3,2,1,0:T(8,128)}, f32[20,8,8,256]{3,2,1,0:T(8,128)}, u32[]{:S(2)}, u32[]{:S(2)}) %collective-permute-start) | collective-permute-done | bytes 1310752 | tf_op jit(solution)/shard_map/ppermute | solution.py:820
  49.2 7.6 %field_middle.1 = (f32[16,8,8,256]{3,2,1,0:T(8,128)S(1)}, f32[18,8,8,256]{3,2,1,0:T(8,128)S(1)}, f32[2,8,8,256]{3,2,1,0:T(8,128)S(1)}, f32[4,8,8,256]{3,2,1,0:T(...) custom-call(f32[16,8,8,256]{3,2,1,0:T(8,128)S(1)} %get-tuple-element.43.refs_0_.refs_2_, ...), custom_call_target="tpu_custom_call" | custom-call | flops 16777216 | bytes 33554432 | tf_op jit(solution)/shard_map/field_middle/pallas_call | solution.py:795
  56.8 0.1 collective-permute-start.2
  56.9 4.9 %collective-permute-start.3 = (f32[9,8,8,256]{3,2,1,0:T(8,128)}, f32[9,8,8,256]{3,2,1,0:T(8,128)}, u32[]{:S(2)}, u32[]{:S(2)}) collective-permute-start(f32[9,8,8,256]{3,2,1,0:T(8,128)} %get-tuple-element.71), channel_id=1, source_target_pairs={{4,0},{8,4},{12,8},{16,12},{20,16},{24,20},{28,24},{32,28},{36,32}... | collective-permute-start | bytes 1769480 | tf_op jit(solution)/shard_map/ppermute | solution.py:820
  61.8 2.6 %field_triangle.1 = (f32[16,8,8,256]{3,2,1,0:T(8,128)S(1)}, f32[16,8,8,256]{3,2,1,0:T(8,128)S(1)}, f32[18,8,8,256]{3,2,1,0:T(8,128)S(1)}) custom-call(f32[16,8,8,256]{3,2,1,0:T(8,128)S(1)} %get-tuple-element.51.refs_0_, f32[18,8,8,256]{3,2,1,0:T(8,128)S(1)} %get-tuple-element.52.refs_1_, f32[16,8,8,256]{3,2,1,0:T(8,128)S(1)} %get-tuple-element.43.refs_0_.refs_2_, ...), custom_call_target="tpu_custom_call" | custom-call | flops 16777216 | bytes 33554432 | tf_op jit(solution)/shard_map/field_triangle/pallas_call | solution.py:795
  64.4 1.0 copy-done.3
  65.5 1.0 copy-done.7
  66.5 1.0 copy-done.9
  67.4 3.4 %prior_take.1 = (f32[16,8,8,256]{3,2,1,0:T(8,128)S(1)}, f32[4,8,8,256]{3,2,1,0:T(8,128)S(1)}) custom-call(f32[32,5,16,128]{3,2,1,0:T(8,128)} %all-to-all-done.x_hbm), custom_call_target="tpu_custom_call" | custom-call | flops 16777216 | bytes 33554432 | tf_op jit(solution)/shard_map/prior_take/pallas_call | solution.py:292
  70.8 0.6 prior_warmth.1
  71.4 0.0 copy-start.10
  71.4 2.7 %first_ready.1 = (f32[18,8,8,256]{3,2,1,0:T(8,128)S(1)}, f32[18,8,8,256]{3,2,1,0:T(8,128)S(1)}, f32[5,18,256]{2,1,0:T(8,128)S(1)}, f32[5,18,256]{2,1,0:T(8,128)S(1)}) custom-call(f32[16,8,8,256]{3,2,1,0:T(8,128)S(1)} %get-tuple-element.57.refs_0_.refs_6_, f32[4,8,8,256]{3,2,1,0:T(8,128)S(1)} %get-tuple-element.58.refs_1_.refs_7_, ...), custom_call_target="tpu_custom_call" | custom-call | flops 16777216 | bytes 33554432 | tf_op jit(solution)/shard_map/first_ready/pallas_call | solution.py:795
  74.2 0.5 collective-permute-done.2.refs_15_.refs_17_
  74.6 0.2 collective-permute-done.3.refs_16_.refs_18_
  74.8 2.7 %last_ends.1 = (f32[18,8,8,256]{3,2,1,0:T(8,128)S(1)}, f32[18,8,8,256]{3,2,1,0:T(8,128)S(1)}, f32[16,8,8,256]{3,2,1,0:T(8,128)S(1)}, f32[5,18,256]{2,1,0:T(8,128...) custom-call(f32[16,8,8,256]{3,2,1,0:T(8,128)S(1)} %get-tuple-element.43.refs_0_.refs_2_, ...), custom_call_target="tpu_custom_call" | custom-call | flops 16777216 | bytes 33554432 | tf_op jit(solution)/shard_map/last_ends/pallas_call | solution.py:795
  77.6 4.2 %collective-permute-start.5 = (f32[5,18,256]{2,1,0:T(8,128)S(1)}, f32[5,18,256]{2,1,0:T(8,128)S(1)}, u32[]{:S(2)}, u32[]{:S(2)}) collective-permute-start(f32[5,18,256]{2,1,0:T(8,128)S(1)} %get-tuple-element.80.refs_2_), channel_id=1, source_target_pairs={{1,0},{2,1},{3,2},{5,4},{6,5},{7,6},{9,8},{10,9},{11,10},{13,12},{... | collective-permute-start | bytes 276488 | tf_op jit(solution)/shard_map/ppermute | solution.py:820
  81.8 4.6 %collective-permute-start.4 = (f32[5,18,256]{2,1,0:T(8,128)S(1)}, f32[5,18,256]{2,1,0:T(8,128)S(1)}, u32[]{:S(2)}, u32[]{:S(2)}) collective-permute-start(f32[5,18,256]{2,1,0:T(8,128)S(1)} %get-tuple-element.81.refs_3_), channel_id=1, source_target_pairs={{0,1},{1,2},{2,3},{4,5},{5,6},{6,7},{8,9},{9,10},{10,11},{12,13},{... | collective-permute-start | bytes 276488 | tf_op jit(solution)/shard_map/ppermute | solution.py:820
  86.4 6.5 %field_last.1 = (f32[64,16,256]{2,1,0:T(8,128)}, f32[64,16,256]{2,1,0:T(8,128)}, f32[18,8,8,256]{3,2,1,0:T(8,128)S(1)}, f32[18,8,8,256]{3,2,1,0:T(8,128)S(1)}, f32[16,8,8,256]{3,2,1,0:T(8,128)S(1)}) custom-call(f32[16,8,8,256]{3,2,1,0:T(8,128)S(1)} %get-tuple-element.43.refs_0_.refs_2_, ...), custom_call_target="tpu_custom_call", output_to_operand_aliasing={{2}: (12, {}), {3}: (13, {}), {4}: (14, {})} | custom-call | flops 16777216 | bytes 33554432 | tf_op jit(solution)/shard_map/field_last/pallas_call | solution.py:795
  92.9 2.9 %second_sweep.1 = f32[32,8,8,128]{3,2,1,0:T(8,128)S(1)} custom-call(f32[18,8,8,256]{3,2,1,0:T(8,128)S(1)} %get-tuple-element.78.refs_0_, f32[18,8,8,256]{3,2,1,0:T(8,128)S(1)} %get-tuple-element.79.refs_1_, f32[5,18,256]{2,1,0:T(8,128)S(1)} %get-tuple-element.80.refs_2_, f32[5,18,256]{2,1,0:T(8,128)S(1)} %get-tuple-element.81.refs_3_, ...), custom_call_target="tpu_custom_call" | custom-call | flops 16777216 | bytes 33554432 | tf_op jit(solution)/shard_map/second_sweep/pallas_call | solution.py:795
  95.9 23.5 %all_to_all.10.x_ref = f32[32,8,8,128]{3,2,1,0:T(8,128)S(1)} all-to-all(f32[32,8,8,128]{3,2,1,0:T(8,128)S(1)} %second_sweep.1), channel_id=1, replica_groups=mesh['sec'=32,'ax'=4] {'sec'}, dimensions={0} | all-to-all | bytes 2097152 | tf_op jit(solution)/shard_map/all_to_all | solution.py:870
  119.4 2.7 %temperature_take.1 = f32[64,8,512]{2,1,0:T(8,128)} custom-call(f32[32,8,8,128]{3,2,1,0:T(8,128)S(1)} %all_to_all.10.x_ref), custom_call_target="tpu_custom_call" | custom-call | flops 4194304 | bytes 2097152 | tf_op jit(solution)/shard_map/temperature_take/pallas_call | solution.py:325
  (19 shorter events, 0.0 us)
Async XLA Ops:
  0.6 9.3 %copy-start.11 = (f32[64,8,512]{2,1,0:T(8,128)S(1)}, f32[64,8,512]{2,1,0:T(8,128)}, u32[]{:S(2)}) copy-start(f32[64,8,512]{2,1,0:T(8,128)} %prior_ref.1) | copy-start | bytes 3145732
  5.1 44.1 %collective-permute-start = (f32[20,8,8,256]{3,2,1,0:T(8,128)}, f32[20,8,8,256]{3,2,1,0:T(8,128)}, u32[]{:S(2)}, u32[]{:S(2)}) collective-permute-start(f32[20,8,8,256]{3,2,1,0:T(8,128)} %get-tuple-element.49), channel_id=1, source_target_pairs={{0,4},{4,8},{8,12},{12,16},{16,20},{20,24},{24,28},{28,32},{32,36}... | collective-permute-start | bytes 3932168 | tf_op jit(solution)/shard_map/ppermute | solution.py:820
  6.8 42.4 %collective-permute-start.1 = (f32[20,8,8,256]{3,2,1,0:T(8,128)}, f32[20,8,8,256]{3,2,1,0:T(8,128)}, u32[]{:S(2)}, u32[]{:S(2)}) collective-permute-start(f32[20,8,8,256]{3,2,1,0:T(8,128)} %get-tuple-element.50), channel_id=1, source_target_pairs={{4,0},{8,4},{12,8},{16,12},{20,16},{24,20},{28,24},{32,28},{36,32}... | collective-permute-start | bytes 3932168 | tf_op jit(solution)/shard_map/ppermute | solution.py:820
  11.4 56.0 %all-to-all-start = ((f32[32,5,16,128]{3,2,1,0:T(8,128)}), f32[32,5,16,128]{3,2,1,0:T(8,128)}, u32[]{:S(2)}, u32[]{:S(2)}) async-start(f32[32,5,16,128]{3,2,1,0:T(8,128)} %prior_send.1), calls=%async_computation | async-start | bytes 2621440 | tf_op jit(solution)/shard_map/all_to_all | solution.py:830
  18.2 1.6 %copy-start.2 = (f32[2,64,16,256]{3,2,1,0:T(8,128)S(1)}, f32[2,64,16,256]{3,2,1,0:T(8,128)}, u32[]{:S(2)}) copy-start(f32[2,64,16,256]{3,2,1,0:T(8,128)} %exc_hbm.1) | copy-start | bytes 6291460
  19.8 1.2 %copy-start.5 = (s32[64,16,256]{2,1,0:T(8,128)S(1)}, s32[64,16,256]{2,1,0:T(8,128)}, u32[]{:S(2)}) copy-start(s32[64,16,256]{2,1,0:T(8,128)} %lab_hbm.1) | copy-start | bytes 3145732
  21.0 1.2 %copy-start.6 = (f32[64,16,256]{2,1,0:T(8,128)S(1)}, f32[64,16,256]{2,1,0:T(8,128)}, u32[]{:S(2)}) copy-start(f32[64,16,256]{2,1,0:T(8,128)} %a_hbm.1) | copy-start | bytes 3145732
  25.4 36.4 %copy-start = (f32[16,8,8,256]{3,2,1,0:T(8,128)}, f32[16,8,8,256]{3,2,1,0:T(8,128)S(1)}, u32[]{:S(2)}) copy-start(f32[16,8,8,256]{3,2,1,0:T(8,128)S(1)} %get-tuple-element.45.refs_2_.refs_4_) | copy-start | bytes 3145732
  56.8 17.8 %collective-permute-start.2 = (f32[9,8,8,256]{3,2,1,0:T(8,128)}, f32[9,8,8,256]{3,2,1,0:T(8,128)}, u32[]{:S(2)}, u32[]{:S(2)}) collective-permute-start(f32[9,8,8,256]{3,2,1,0:T(8,128)} %get-tuple-element.70), channel_id=1, source_target_pairs={{0,4},{4,8},{8,12},{12,16},{16,20},{20,24},{24,28},{28,32},{32,36}... | collective-permute-start | bytes 1769480 | tf_op jit(solution)/shard_map/ppermute | solution.py:820
  56.9 18.0 %collective-permute-start.3 = (f32[9,8,8,256]{3,2,1,0:T(8,128)}, f32[9,8,8,256]{3,2,1,0:T(8,128)}, u32[]{:S(2)}, u32[]{:S(2)}) collective-permute-start(f32[9,8,8,256]{3,2,1,0:T(8,128)} %get-tuple-element.71), channel_id=1, source_target_pairs={{4,0},{8,4},{12,8},{16,12},{20,16},{24,20},{28,24},{32,28},{36,32}... | collective-permute-start | bytes 1769480 | tf_op jit(solution)/shard_map/ppermute | solution.py:820
  64.4 1.0 copy-start.3
  65.5 1.0 copy-start.7
  66.5 1.0 copy-start.9
  71.4 3.4 %copy-start.1 = (f32[16,8,8,256]{3,2,1,0:T(8,128)S(1)}, f32[16,8,8,256]{3,2,1,0:T(8,128)}, u32[]{:S(2)}) copy-start(f32[16,8,8,256]{3,2,1,0:T(8,128)} %copy-done) | copy-start | bytes 3145732
  71.4 3.4 %copy-start.4 = (f32[18,8,8,256]{3,2,1,0:T(8,128)S(1)}, f32[18,8,8,256]{3,2,1,0:T(8,128)}, u32[]{:S(2)}) copy-start(f32[18,8,8,256]{3,2,1,0:T(8,128)} %copy-done.3) | copy-start | bytes 3538948
  71.4 3.4 %copy-start.8 = (f32[16,8,8,256]{3,2,1,0:T(8,128)S(1)}, f32[16,8,8,256]{3,2,1,0:T(8,128)}, u32[]{:S(2)}) copy-start(f32[16,8,8,256]{3,2,1,0:T(8,128)} %copy-done.7) | copy-start | bytes 3145732
  71.4 3.4 %copy-start.10 = (f32[16,8,8,256]{3,2,1,0:T(8,128)S(1)}, f32[16,8,8,256]{3,2,1,0:T(8,128)}, u32[]{:S(2)}) copy-start(f32[16,8,8,256]{3,2,1,0:T(8,128)} %copy-done.9) | copy-start | bytes 3145732
  77.6 15.3 %collective-permute-start.5 = (f32[5,18,256]{2,1,0:T(8,128)S(1)}, f32[5,18,256]{2,1,0:T(8,128)S(1)}, u32[]{:S(2)}, u32[]{:S(2)}) collective-permute-start(f32[5,18,256]{2,1,0:T(8,128)S(1)} %get-tuple-element.80.refs_2_), channel_id=1, source_target_pairs={{1,0},{2,1},{3,2},{5,4},{6,5},{7,6},{9,8},{10,9},{11,10},{13,12},{... | collective-permute-start | bytes 276488 | tf_op jit(solution)/shard_map/ppermute | solution.py:820
  81.8 11.1 %collective-permute-start.4 = (f32[5,18,256]{2,1,0:T(8,128)S(1)}, f32[5,18,256]{2,1,0:T(8,128)S(1)}, u32[]{:S(2)}, u32[]{:S(2)}) collective-permute-start(f32[5,18,256]{2,1,0:T(8,128)S(1)} %get-tuple-element.81.refs_3_), channel_id=1, source_target_pairs={{0,1},{1,2},{2,3},{4,5},{5,6},{6,7},{8,9},{9,10},{10,11},{12,13},{... | collective-permute-start | bytes 276488 | tf_op jit(solution)/shard_map/ppermute | solution.py:820

commit v7 on v6

--- a/solution.py
+++ b/solution.py
@@ -309,14 +309,16 @@
         at = _planes(g)
         return pltpu.make_async_copy(planes.at[at], out.at[at], sems.at[g])
 
-    def group(g):
-        for s in range(SEC // 8):
-            got = _swap_blocks([x_ref[s * 8 + j, g] for j in range(8)], AZ)
-            for q in range(G):
-                planes[g * G + q, :, s * 128 : s * 128 + 128] = got[q]
-        copy(g).start()
-
-    _loop(NG, group)
+    def groups(gs):
+        for g in gs:
+            for s in range(SEC // 8):
+                got = _swap_blocks([x_ref[s * 8 + j, g] for j in range(8)], AZ)
+                for q in range(G):
+                    planes[g * G + q, :, s * 128 : s * 128 + 128] = got[q]
+        for g in gs:
+            copy(g).start()
+
+    _pairs(groups)
     for g in range(NG):
         copy(g).wait()
 
@@ -617,6 +619,10 @@
     _losses(R, gs, lane, store, final)
 
 
+def _even():
+    return lax.rem(lax.axis_index("ax"), 2) == 0
+
+
 def _last_ends_kernel(names, *refs):
     R = dict(zip(names, refs))
     lane, _ = _iotas()
@@ -634,6 +640,9 @@
         outs[k][_N, at, :] = parts[k][_N, at, :] + d[q : q + 1]
 
     _last(R, ENDS, lane, R["end_rows"], send)
+    even = _even()
+    R["swap_a"][...] = jnp.where(even, R["up"][...], R["down"][...])
+    R["swap_b"][...] = jnp.where(even, R["down"][...], R["up"][...])
 
 
 def _last_kernel(names, *refs):
@@ -680,6 +689,11 @@
     lane, sub = _iotas()
     ax = lax.axis_index("ax")
     exists = (ax > 0, ax < lax.axis_size("ax") - 1)
+    even = _even()
+    for k in range(5):
+        a, b = R["got_a"][k], R["got_b"][k]
+        R["t_lo"][k] = jnp.where(even, b, a)
+        R["t_hi"][k] = jnp.where(even, a, b)
     for side, (own, other) in enumerate(((R["down"], R["t_lo"]), (R["up"], R["t_hi"]))):
         kf = own[_H] + other[_H]
         jump = kf * (other[_T] - own[_T])
@@ -818,6 +832,11 @@
     count = lax.axis_size(axis)
     pairs = [(i, (i + 1) % count) for i in range(count if closed else count - 1)]
     return lax.ppermute(x, axis, pairs if step > 0 else [(b, a) for a, b in pairs])
+
+
+def _swap(axis, x, start):
+    pairs = [(i, i + 1) for i in range(start, lax.axis_size(axis) - 1, 2)]
+    return lax.ppermute(x, axis, pairs + [(b, a) for a, b in pairs])
 
 
 def _around(low_edge, high_edge):
@@ -851,9 +870,9 @@
     scratch = {"q_out": (2, AZ + 2, G, RAD), "ends": _ENDS}
     state = {"t1_out": _MORE, "h1_out": _MORE, "loss_out": _OWN}
     names = _LAST + ["part_lo", "part_hi"]
-    outs = {**state, "down": _END, "up": _END, "end_rows": (2, AZ, G, RAD)}
+    outs = {**state, "down": _END, "up": _END, "swap_a": _END, "swap_b": _END, "end_rows": (2, AZ, G, RAD)}
     V.update(_call(_last_ends_kernel, "last_ends", V, names, outs, scratch, fetch=_FETCH))
-    V["t_lo"], V["t_hi"] = _ring("ax", V["up"], 1, False), _ring("ax", V["down"], -1, False)
+    V["got_a"], V["got_b"] = _swap("ax", V["swap_a"], 0), _swap("ax", V["swap_b"], 1)
     V.update(t1=V["t1_out"], h1=V["h1_out"], loss=V["loss_out"])
     results = {"closing": (AX, AZ, RAD), "dissipation": (AX, AZ, RAD)}
     scratch.update(rows=(2, AZ, G, RAD), closing_v=(AX, AZ, RAD), dissipation_v=(AX, AZ, RAD))
@@ -863,9 +882,9 @@
         _call(_last_kernel, "field_last", V, names, outs, scratch, ["t1", "h1", "loss"], list(results), _FETCH)
     )
     V.update(t1=V["t1_out"], h1=V["h1_out"], loss=V["loss_out"])
-    names = ["t1", "h1", "down", "up", "t_lo", "t_hi", "lab", "prior", "loss"]
+    names = ["t1", "h1", "down", "up", "got_a", "got_b", "lab", "prior", "loss"]
     shape = (2, 2, AZ + 2, RAD)
-    scratch = {"t2": _OWN, "own1": shape, "beside1": shape}
+    scratch = {"t2": _OWN, "own1": shape, "beside1": shape, "t_lo": _END, "t_hi": _END}
     out = _call(_second_kernel, "second_sweep", V, names, {"blocks": (SEC, NG, RL, G * AZ)}, scratch)
     temperature = _temperature_take(lax.all_to_all(out["blocks"], "sec", 0, 0))
     return V["closing"], V["dissipation"], temperature

time: 125 us -> 121 us (0.968)
  the two profiles are of different devices: /device:TPU:3 before, /device:TPU:1 now
where the time goes in v7:
time: 121 us
  Pallas kernels  40.4 us (33%)
  starting transfers between devices  26.3 us (22%)
  waiting for transfers between devices  25.1 us (21%)
  blocking collectives  20.8 us (17%)
  local copies, waits for them, and re-layouts  7.04 us (6%)
    pallas_call x7, Pallas kernels, _call(): pl.pallas_call(functools.partial(kernel, names + list(outs) + list(shapes...  25.7 us
    ppermute x4, waiting for transfers between devices, _ring(): lax.ppermute(x, axis, pairs if step > 0 else [(b, a) for a, b in pairs])  25.1 us
    all_to_all x1, blocking collectives, shards(): temperature = _temperature_take(lax.all_to_all(out['blocks'], 'sec', 0, 0))  20.8 us
    ppermute x4, starting transfers between devices, _ring(): lax.ppermute(x, axis, pairs if step > 0 else [(b, a) for a, b in pairs])  13.7 us
    ppermute x2, starting transfers between devices, _swap(): return lax.ppermute(x, axis, pairs + [(b, a) for a, b in pairs])  7.9 us
    unnamed x24, local copies, waits for them, and re-layouts  7.04 us
    all_to_all x1, starting transfers between devices, shards(): got = lax.all_to_all(_prior_send(prior), 'sec', 0, 0)  4.68 us
    pallas_call x1, Pallas kernels, _edges(): pl.pallas_call(_edges_kernel, in_specs=[pl.BlockSpec(memory_space=pl.ANY)...  4.42 us
  transfers between devices with their start and end apart: 7, of which 1 were waited for; matrix products, arithmetic and copies ran while one was open for 0% of the time, Pallas kernels for 23%

profile of v7, /device:TPU:1, one launch (start us, length us, event | category | flops | bytes accessed | tf_op | source)
XLA Modules:
  0.0 120.7 jit_solution(8438924711266975144)
XLA Ops:
  0.6 4.4 %edge_layers.1 = (f32[20,8,8,256]{3,2,1,0:T(8,128)}, f32[20,8,8,256]{3,2,1,0:T(8,128)}) custom-call(s32[64,16,256]{2,1,0:T(8,128)} %lab_hbm.1, f32[2,64,16,256]{3,2,1,0:T(8,128)} %exc_hbm.1, f32[64,16,256]{2,1,0:T(8,128)} %a_hbm.1), custom_call_target="tpu_custom_call" | custom-call | flops 1048576 | bytes 6291456 | tf_op jit(solution)/shard_map/edge_layers/pallas_call | solution.py:162
  5.1 2.5 %collective-permute-start = (f32[20,8,8,256]{3,2,1,0:T(8,128)}, f32[20,8,8,256]{3,2,1,0:T(8,128)}, u32[]{:S(2)}, u32[]{:S(2)}) collective-permute-start(f32[20,8,8,256]{3,2,1,0:T(8,128)} %get-tuple-element.51), channel_id=1, source_target_pairs={{0,4},{4,8},{8,12},{12,16},{16,20},{20,24},{24,28},{28,32},{32,36}... | collective-permute-start | bytes 3932168 | tf_op jit(solution)/shard_map/ppermute | solution.py:834
  7.6 5.4 %collective-permute-start.1 = (f32[20,8,8,256]{3,2,1,0:T(8,128)}, f32[20,8,8,256]{3,2,1,0:T(8,128)}, u32[]{:S(2)}, u32[]{:S(2)}) collective-permute-start(f32[20,8,8,256]{3,2,1,0:T(8,128)} %get-tuple-element.52), channel_id=1, source_target_pairs={{4,0},{8,4},{12,8},{16,12},{20,16},{24,20},{28,24},{32,28},{36,32}... | collective-permute-start | bytes 3932168 | tf_op jit(solution)/shard_map/ppermute | solution.py:834
  13.0 1.4 %prior_send.1 = f32[32,5,16,128]{3,2,1,0:T(8,128)} custom-call(f32[64,8,512]{2,1,0:T(8,128)S(1)} %copy-done.11), custom_call_target="tpu_custom_call" | custom-call | flops 1048576 | bytes 3145728 | tf_op jit(solution)/shard_map/prior_send/pallas_call | solution.py:238
  14.5 4.7 %all-to-all-start = ((f32[32,5,16,128]{3,2,1,0:T(8,128)}), f32[32,5,16,128]{3,2,1,0:T(8,128)}, u32[]{:S(2)}, u32[]{:S(2)}) async-start(f32[32,5,16,128]{3,2,1,0:T(8,128)} %prior_send.1), calls=%async_computation | async-start | bytes 2621440 | tf_op jit(solution)/shard_map/all_to_all | solution.py:849
  19.1 0.0 copy-start.2
  19.2 1.6 %copy-done.2 = f32[2,64,16,256]{3,2,1,0:T(8,128)S(1)} copy-done((f32[2,64,16,256]{3,2,1,0:T(8,128)S(1)}, f32[2,64,16,256]{3,2,1,0:T(8,128)}, u32[]{:S(2)}) %copy-start.2) | copy-done | bytes 2097176
  20.7 1.2 %copy-done.5 = s32[64,16,256]{2,1,0:T(8,128)S(1)} copy-done((s32[64,16,256]{2,1,0:T(8,128)S(1)}, s32[64,16,256]{2,1,0:T(8,128)}, u32[]{:S(2)}) %copy-start.5) | copy-done | bytes 1048600
  22.0 1.2 %copy-done.6 = f32[64,16,256]{2,1,0:T(8,128)S(1)} copy-done((f32[64,16,256]{2,1,0:T(8,128)S(1)}, f32[64,16,256]{2,1,0:T(8,128)}, u32[]{:S(2)}) %copy-start.6) | copy-done | bytes 1048600
  23.2 3.2 %prepare.1 = (f32[16,8,8,256]{3,2,1,0:T(8,128)S(1)}, f32[16,8,8,256]{3,2,1,0:T(8,128)S(1)}, f32[18,8,8,256]{3,2,1,0:T(8,128)S(1)}, f32[16,8,8,256]{3,2,1,0:T(8,1...) custom-call(s32[64,16,256]{2,1,0:T(8,128)S(1)} %copy-done.5, ...), custom_call_target="tpu_custom_call" | custom-call | flops 4194304 | bytes 8388608 | tf_op jit(solution)/shard_map/prepare/pallas_call | solution.py:207
  26.4 0.0 copy-start
  26.4 25.1 %collective-permute-done.refs_6_.refs_13_.refs_15_ = f32[20,8,8,256]{3,2,1,0:T(8,128)} collective-permute-done((f32[20,8,8,256]{3,2,1,0:T(8,128)}, f32[20,8,8,256]{3,2,1,0:T(8,128)}, u32[]{:S(2)}, u32[]{:S(2)}) %collective-permute-start) | collective-permute-done | bytes 1310752 | tf_op jit(solution)/shard_map/ppermute | solution.py:834
  51.5 7.6 %field_middle.1 = (f32[16,8,8,256]{3,2,1,0:T(8,128)S(1)}, f32[18,8,8,256]{3,2,1,0:T(8,128)S(1)}, f32[2,8,8,256]{3,2,1,0:T(8,128)S(1)}, f32[4,8,8,256]{3,2,1,0:T(...) custom-call(f32[16,8,8,256]{3,2,1,0:T(8,128)S(1)} %get-tuple-element.45.refs_0_.refs_2_, ...), custom_call_target="tpu_custom_call" | custom-call | flops 16777216 | bytes 33554432 | tf_op jit(solution)/shard_map/field_middle/pallas_call | solution.py:809
  59.0 0.1 collective-permute-start.2
  59.1 5.7 %collective-permute-start.3 = (f32[9,8,8,256]{3,2,1,0:T(8,128)}, f32[9,8,8,256]{3,2,1,0:T(8,128)}, u32[]{:S(2)}, u32[]{:S(2)}) collective-permute-start(f32[9,8,8,256]{3,2,1,0:T(8,128)} %get-tuple-element.73), channel_id=1, source_target_pairs={{4,0},{8,4},{12,8},{16,12},{20,16},{24,20},{28,24},{32,28},{36,32}... | collective-permute-start | bytes 1769480 | tf_op jit(solution)/shard_map/ppermute | solution.py:834
  64.8 2.6 %field_triangle.1 = (f32[16,8,8,256]{3,2,1,0:T(8,128)S(1)}, f32[16,8,8,256]{3,2,1,0:T(8,128)S(1)}, f32[18,8,8,256]{3,2,1,0:T(8,128)S(1)}) custom-call(f32[16,8,8,256]{3,2,1,0:T(8,128)S(1)} %get-tuple-element.53.refs_0_, f32[18,8,8,256]{3,2,1,0:T(8,128)S(1)} %get-tuple-element.54.refs_1_, f32[16,8,8,256]{3,2,1,0:T(8,128)S(1)} %get-tuple-element.45.refs_0_.refs_2_, ...), custom_call_target="tpu_custom_call" | custom-call | flops 16777216 | bytes 33554432 | tf_op jit(solution)/shard_map/field_triangle/pallas_call | solution.py:809
  67.5 1.0 copy-done.3
  68.5 1.0 copy-done.7
  69.5 1.0 copy-done.9
  70.4 3.4 %prior_take.1 = (f32[16,8,8,256]{3,2,1,0:T(8,128)S(1)}, f32[4,8,8,256]{3,2,1,0:T(8,128)S(1)}) custom-call(f32[32,5,16,128]{3,2,1,0:T(8,128)} %all-to-all-done.x_hbm), custom_call_target="tpu_custom_call" | custom-call | flops 16777216 | bytes 33554432 | tf_op jit(solution)/shard_map/prior_take/pallas_call | solution.py:292
  73.8 0.6 prior_warmth.1
  74.4 0.0 copy-start.1
  74.4 0.0 copy-start.8
  74.5 0.0 copy-start.10
  74.5 2.7 %first_ready.1 = (f32[18,8,8,256]{3,2,1,0:T(8,128)S(1)}, f32[18,8,8,256]{3,2,1,0:T(8,128)S(1)}, f32[5,18,256]{2,1,0:T(8,128)S(1)}, f32[5,18,256]{2,1,0:T(8,128)S(1)}) custom-call(f32[16,8,8,256]{3,2,1,0:T(8,128)S(1)} %get-tuple-element.59.refs_0_.refs_6_, f32[4,8,8,256]{3,2,1,0:T(8,128)S(1)} %get-tuple-element.60.refs_1_.refs_7_, ...), custom_call_target="tpu_custom_call" | custom-call | flops 16777216 | bytes 33554432 | tf_op jit(solution)/shard_map/first_ready/pallas_call | solution.py:809
  77.2 2.8 %last_ends.1 = (f32[18,8,8,256]{3,2,1,0:T(8,128)S(1)}, f32[18,8,8,256]{3,2,1,0:T(8,128)S(1)}, f32[16,8,8,256]{3,2,1,0:T(8,128)S(1)}, f32[5,18,256]{2,1,0:T(8,128...) custom-call(f32[16,8,8,256]{3,2,1,0:T(8,128)S(1)} %get-tuple-element, ...), custom_call_target="tpu_custom_call" | custom-call | flops 16777216 | bytes 33554432 | tf_op jit(solution)/shard_map/last_ends/pallas_call | solution.py:809
  80.0 3.2 %collective-permute-start.4 = (f32[5,18,256]{2,1,0:T(8,128)S(1)}, f32[5,18,256]{2,1,0:T(8,128)S(1)}, u32[]{:S(2)}, u32[]{:S(2)}) collective-permute-start(f32[5,18,256]{2,1,0:T(8,128)S(1)} %get-tuple-element.84), channel_id=1, source_target_pairs={{0,1},{2,3},{1,0},{3,2},{4,5},{6,7},{5,4},{7,6},{8,9},{10,11},{9,8... | collective-permute-start | bytes 276488 | tf_op jit(solution)/shard_map/ppermute | solution.py:839
  83.2 4.7 %collective-permute-start.5 = (f32[5,18,256]{2,1,0:T(8,128)S(1)}, f32[5,18,256]{2,1,0:T(8,128)S(1)}, u32[]{:S(2)}, u32[]{:S(2)}) collective-permute-start(f32[5,18,256]{2,1,0:T(8,128)S(1)} %get-tuple-element.85), channel_id=1, source_target_pairs={{1,2},{2,1},{5,6},{6,5},{9,10},{10,9},{13,14},{14,13},{17,18},{18,... | collective-permute-start | bytes 276488 | tf_op jit(solution)/shard_map/ppermute | solution.py:839
  87.9 6.5 %field_last.1 = (f32[64,16,256]{2,1,0:T(8,128)}, f32[64,16,256]{2,1,0:T(8,128)}, f32[18,8,8,256]{3,2,1,0:T(8,128)S(1)}, f32[18,8,8,256]{3,2,1,0:T(8,128)S(1)}, f32[16,8,8,256]{3,2,1,0:T(8,128)S(1)}) custom-call(f32[16,8,8,256]{3,2,1,0:T(8,128)S(1)} %get-tuple-element.45.refs_0_.refs_2_, ...), custom_call_target="tpu_custom_call", output_to_operand_aliasing={{2}: (12, {}), {3}: (13, {}), {4}: (14, {})} | custom-call | flops 16777216 | bytes 33554432 | tf_op jit(solution)/shard_map/field_last/pallas_call | solution.py:809
  94.4 2.9 %second_sweep.1 = f32[32,8,8,128]{3,2,1,0:T(8,128)S(1)} custom-call(f32[18,8,8,256]{3,2,1,0:T(8,128)S(1)} %get-tuple-element.80.refs_0_, f32[18,8,8,256]{3,2,1,0:T(8,128)S(1)} %get-tuple-element.81.refs_1_, f32[5,18,256]{2,1,0:T(8,128)S(1)} %get-tuple-element.82.refs_2_, f32[5,18,256]{2,1,0:T(8,128)S(1)} %get-tuple-element.83.refs_3_, ...), custom_call_target="tpu_custom_call" | custom-call | flops 16777216 | bytes 33554432 | tf_op jit(solution)/shard_map/second_sweep/pallas_call | solution.py:809
  97.4 20.8 %all_to_all.10.x_ref = f32[32,8,8,128]{3,2,1,0:T(8,128)S(1)} all-to-all(f32[32,8,8,128]{3,2,1,0:T(8,128)S(1)} %second_sweep.1), channel_id=1, replica_groups=mesh['sec'=32,'ax'=4] {'sec'}, dimensions={0} | all-to-all | bytes 2097152 | tf_op jit(solution)/shard_map/all_to_all | solution.py:889
  118.2 2.3 %temperature_take.1 = f32[64,8,512]{2,1,0:T(8,128)} custom-call(f32[32,8,8,128]{3,2,1,0:T(8,128)S(1)} %all_to_all.10.x_ref), custom_call_target="tpu_custom_call" | custom-call | flops 4194304 | bytes 2097152 | tf_op jit(solution)/shard_map/temperature_take/pallas_call | solution.py:327
  (19 shorter events, 0.0 us)
Async XLA Ops:
  0.6 12.4 %copy-start.11 = (f32[64,8,512]{2,1,0:T(8,128)S(1)}, f32[64,8,512]{2,1,0:T(8,128)}, u32[]{:S(2)}) copy-start(f32[64,8,512]{2,1,0:T(8,128)} %prior_ref.1) | copy-start | bytes 3145732
  5.1 46.4 %collective-permute-start = (f32[20,8,8,256]{3,2,1,0:T(8,128)}, f32[20,8,8,256]{3,2,1,0:T(8,128)}, u32[]{:S(2)}, u32[]{:S(2)}) collective-permute-start(f32[20,8,8,256]{3,2,1,0:T(8,128)} %get-tuple-element.51), channel_id=1, source_target_pairs={{0,4},{4,8},{8,12},{12,16},{16,20},{20,24},{24,28},{28,32},{32,36}... | collective-permute-start | bytes 3932168 | tf_op jit(solution)/shard_map/ppermute | solution.py:834
  7.6 43.8 %collective-permute-start.1 = (f32[20,8,8,256]{3,2,1,0:T(8,128)}, f32[20,8,8,256]{3,2,1,0:T(8,128)}, u32[]{:S(2)}, u32[]{:S(2)}) collective-permute-start(f32[20,8,8,256]{3,2,1,0:T(8,128)} %get-tuple-element.52), channel_id=1, source_target_pairs={{4,0},{8,4},{12,8},{16,12},{20,16},{24,20},{28,24},{32,28},{36,32}... | collective-permute-start | bytes 3932168 | tf_op jit(solution)/shard_map/ppermute | solution.py:834
  14.5 56.0 %all-to-all-start = ((f32[32,5,16,128]{3,2,1,0:T(8,128)}), f32[32,5,16,128]{3,2,1,0:T(8,128)}, u32[]{:S(2)}, u32[]{:S(2)}) async-start(f32[32,5,16,128]{3,2,1,0:T(8,128)} %prior_send.1), calls=%async_computation | async-start | bytes 2621440 | tf_op jit(solution)/shard_map/all_to_all | solution.py:849
  19.1 1.6 %copy-start.2 = (f32[2,64,16,256]{3,2,1,0:T(8,128)S(1)}, f32[2,64,16,256]{3,2,1,0:T(8,128)}, u32[]{:S(2)}) copy-start(f32[2,64,16,256]{3,2,1,0:T(8,128)} %exc_hbm.1) | copy-start | bytes 6291460
  20.7 1.2 %copy-start.5 = (s32[64,16,256]{2,1,0:T(8,128)S(1)}, s32[64,16,256]{2,1,0:T(8,128)}, u32[]{:S(2)}) copy-start(s32[64,16,256]{2,1,0:T(8,128)} %lab_hbm.1) | copy-start | bytes 3145732
  22.0 1.2 %copy-start.6 = (f32[64,16,256]{2,1,0:T(8,128)S(1)}, f32[64,16,256]{2,1,0:T(8,128)}, u32[]{:S(2)}) copy-start(f32[64,16,256]{2,1,0:T(8,128)} %a_hbm.1) | copy-start | bytes 3145732
  26.4 38.4 %copy-start = (f32[16,8,8,256]{3,2,1,0:T(8,128)}, f32[16,8,8,256]{3,2,1,0:T(8,128)S(1)}, u32[]{:S(2)}) copy-start(f32[16,8,8,256]{3,2,1,0:T(8,128)S(1)} %get-tuple-element.47.refs_2_.refs_4_) | copy-start | bytes 3145732
  59.0 18.2 %collective-permute-start.2 = (f32[9,8,8,256]{3,2,1,0:T(8,128)}, f32[9,8,8,256]{3,2,1,0:T(8,128)}, u32[]{:S(2)}, u32[]{:S(2)}) collective-permute-start(f32[9,8,8,256]{3,2,1,0:T(8,128)} %get-tuple-element.72), channel_id=1, source_target_pairs={{0,4},{4,8},{8,12},{12,16},{16,20},{20,24},{24,28},{28,32},{32,36}... | collective-permute-start | bytes 1769480 | tf_op jit(solution)/shard_map/ppermute | solution.py:834
  59.1 18.1 %collective-permute-start.3 = (f32[9,8,8,256]{3,2,1,0:T(8,128)}, f32[9,8,8,256]{3,2,1,0:T(8,128)}, u32[]{:S(2)}, u32[]{:S(2)}) collective-permute-start(f32[9,8,8,256]{3,2,1,0:T(8,128)} %get-tuple-element.73), channel_id=1, source_target_pairs={{4,0},{8,4},{12,8},{16,12},{20,16},{24,20},{28,24},{32,28},{36,32}... | collective-permute-start | bytes 1769480 | tf_op jit(solution)/shard_map/ppermute | solution.py:834
  67.5 1.0 copy-start.3
  68.5 1.0 copy-start.7
  69.5 1.0 copy-start.9
  74.4 2.8 %copy-start.1 = (f32[16,8,8,256]{3,2,1,0:T(8,128)S(1)}, f32[16,8,8,256]{3,2,1,0:T(8,128)}, u32[]{:S(2)}) copy-start(f32[16,8,8,256]{3,2,1,0:T(8,128)} %copy-done) | copy-start | bytes 3145732
  74.4 2.8 %copy-start.4 = (f32[18,8,8,256]{3,2,1,0:T(8,128)S(1)}, f32[18,8,8,256]{3,2,1,0:T(8,128)}, u32[]{:S(2)}) copy-start(f32[18,8,8,256]{3,2,1,0:T(8,128)} %copy-done.3) | copy-start | bytes 3538948
  74.4 2.8 %copy-start.8 = (f32[16,8,8,256]{3,2,1,0:T(8,128)S(1)}, f32[16,8,8,256]{3,2,1,0:T(8,128)}, u32[]{:S(2)}) copy-start(f32[16,8,8,256]{3,2,1,0:T(8,128)} %copy-done.7) | copy-start | bytes 3145732
  74.5 2.8 %copy-start.10 = (f32[16,8,8,256]{3,2,1,0:T(8,128)S(1)}, f32[16,8,8,256]{3,2,1,0:T(8,128)}, u32[]{:S(2)}) copy-start(f32[16,8,8,256]{3,2,1,0:T(8,128)} %copy-done.9) | copy-start | bytes 3145732
  80.0 14.4 %collective-permute-start.4 = (f32[5,18,256]{2,1,0:T(8,128)S(1)}, f32[5,18,256]{2,1,0:T(8,128)S(1)}, u32[]{:S(2)}, u32[]{:S(2)}) collective-permute-start(f32[5,18,256]{2,1,0:T(8,128)S(1)} %get-tuple-element.84), channel_id=1, source_target_pairs={{0,1},{2,3},{1,0},{3,2},{4,5},{6,7},{5,4},{7,6},{8,9},{10,11},{9,8... | collective-permute-start | bytes 276488 | tf_op jit(solution)/shard_map/ppermute | solution.py:839
  83.2 11.2 %collective-permute-start.5 = (f32[5,18,256]{2,1,0:T(8,128)S(1)}, f32[5,18,256]{2,1,0:T(8,128)S(1)}, u32[]{:S(2)}, u32[]{:S(2)}) collective-permute-start(f32[5,18,256]{2,1,0:T(8,128)S(1)} %get-tuple-element.85), channel_id=1, source_target_pairs={{1,2},{2,1},{5,6},{6,5},{9,10},{10,9},{13,14},{14,13},{17,18},{18,... | collective-permute-start | bytes 276488 | tf_op jit(solution)/shard_map/ppermute | solution.py:839

commit v8 on v7

--- a/solution.py
+++ b/solution.py
@@ -59,8 +59,8 @@
     return results
 
 
-def _pairs(body):
-    _loop(NG // 2, lambda i: body([2 * i, 2 * i + 1]))
+def _pairs(body, count=2):
+    _loop(NG // count, lambda i: body([count * i + k for k in range(count)]))
 
 
 def _planes(g):
@@ -558,7 +558,7 @@
             for copy in sent(g):
                 copy.start()
 
-    _pairs(groups)
+    _pairs(groups, 4)
     for g in range(NG):
         for copy in sent(g):
             copy.wait()
@@ -670,7 +670,7 @@
         natural(g, R["end_rows"][k])
 
     def groups(i):
-        gs = [2 * i + 1, 2 * i + 2]
+        gs = [3 * i + k for k in (1, 2, 3)]
         for g in gs:
             for copy in _fetch(R, g, FIRST_AT[2]):
                 copy.wait()
@@ -678,7 +678,7 @@
         for k, g in enumerate(gs):
             natural(g, R["rows"][k])
 
-    _loop(NG // 2 - 1, groups)
+    _loop((NG - 2) // 3, groups)
     for g in range(NG):
         for copy in copies(g):
             copy.wait()
@@ -851,7 +851,7 @@
     edge = (NLATEST + DEPTH, NG, G, RAD)
     outs = {"rows8": _OWN, "q_out": _MORE, "gone": (2, NG, G, RAD), "lab_more": (4, NG, G, RAD)}
     outs.update(e_low=edge, e_high=edge)
-    scratch = {"ends": _ENDS, "e_low_v": edge, "e_high_v": edge}
+    scratch = {"ends": (4, *_ENDS[1:]), "e_low_v": edge, "e_high_v": edge}
     out = _call(_middle_kernel, "field_middle", V, _CONSTS + _STATE, outs, scratch, (), ["e_low", "e_high"], ["f_low", "f_high"])
     V["low"], V["high"] = _around(out["e_low"], out["e_high"])
     V.update(rows8=out["rows8"], q=out["q_out"], gone=out["gone"], lab_more=out["lab_more"])
@@ -867,7 +867,7 @@
     scratch = {"jac": (2, AZ + 2, G, RAD), "flux": (2, AZ + 2, G, RAD)}
     outs = {"base": _MORE, "gain": _MORE, "part_lo": _END, "part_hi": _END}
     V.update(_call(_ready_kernel, "first_ready", V, ["lab", "lab_more", *warmth], outs, scratch))
-    scratch = {"q_out": (2, AZ + 2, G, RAD), "ends": _ENDS}
+    scratch = {"q_out": (3, AZ + 2, G, RAD), "ends": (3, *_ENDS[1:])}
     state = {"t1_out": _MORE, "h1_out": _MORE, "loss_out": _OWN}
     names = _LAST + ["part_lo", "part_hi"]
     outs = {**state, "down": _END, "up": _END, "swap_a": _END, "swap_b": _END, "end_rows": (2, AZ, G, RAD)}
@@ -875,7 +875,7 @@
     V["got_a"], V["got_b"] = _swap("ax", V["swap_a"], 0), _swap("ax", V["swap_b"], 1)
     V.update(t1=V["t1_out"], h1=V["h1_out"], loss=V["loss_out"])
     results = {"closing": (AX, AZ, RAD), "dissipation": (AX, AZ, RAD)}
-    scratch.update(rows=(2, AZ, G, RAD), closing_v=(AX, AZ, RAD), dissipation_v=(AX, AZ, RAD))
+    scratch.update(rows=(3, AZ, G, RAD), closing_v=(AX, AZ, RAD), dissipation_v=(AX, AZ, RAD))
     names = _LAST + ["end_rows", "t1", "h1", "loss"]
     outs = {**results, **state}
     V.update(

time: 121 us -> 121 us (level)
  no operation moved by 1% of the time
where the time goes in v8:
time: 121 us
  Pallas kernels  40.7 us (34%)
  starting transfers between devices  26.3 us (22%)
  waiting for transfers between devices  25.1 us (21%)
  blocking collectives  20.8 us (17%)
  local copies, waits for them, and re-layouts  7.04 us (6%)
    pallas_call x7, Pallas kernels, _call(): pl.pallas_call(functools.partial(kernel, names + list(outs) + list(shapes...  26 us
    ppermute x4, waiting for transfers between devices, _ring(): lax.ppermute(x, axis, pairs if step > 0 else [(b, a) for a, b in pairs])  25.1 us
    all_to_all x1, blocking collectives, shards(): temperature = _temperature_take(lax.all_to_all(out['blocks'], 'sec', 0, 0))  20.8 us
    ppermute x4, starting transfers between devices, _ring(): lax.ppermute(x, axis, pairs if step > 0 else [(b, a) for a, b in pairs])  13.7 us
    ppermute x2, starting transfers between devices, _swap(): return lax.ppermute(x, axis, pairs + [(b, a) for a, b in pairs])  7.9 us
    unnamed x24, local copies, waits for them, and re-layouts  7.04 us
    all_to_all x1, starting transfers between devices, shards(): got = lax.all_to_all(_prior_send(prior), 'sec', 0, 0)  4.68 us
    pallas_call x1, Pallas kernels, _edges(): pl.pallas_call(_edges_kernel, in_specs=[pl.BlockSpec(memory_space=pl.ANY)...  4.42 us
  transfers between devices with their start and end apart: 7, of which 1 were waited for; matrix products, arithmetic and copies ran while one was open for 0% of the time, Pallas kernels for 23%

profile of v8, /device:TPU:1, one launch (start us, length us, event | category | flops | bytes accessed | tf_op | source)
XLA Modules:
  0.0 121.0 jit_solution(9526753362646489809)
XLA Ops:
  0.6 4.4 %edge_layers.1 = (f32[20,8,8,256]{3,2,1,0:T(8,128)}, f32[20,8,8,256]{3,2,1,0:T(8,128)}) custom-call(s32[64,16,256]{2,1,0:T(8,128)} %lab_hbm.1, f32[2,64,16,256]{3,2,1,0:T(8,128)} %exc_hbm.1, f32[64,16,256]{2,1,0:T(8,128)} %a_hbm.1), custom_call_target="tpu_custom_call" | custom-call | flops 1048576 | bytes 6291456 | tf_op jit(solution)/shard_map/edge_layers/pallas_call | solution.py:162
  5.1 2.5 %collective-permute-start = (f32[20,8,8,256]{3,2,1,0:T(8,128)}, f32[20,8,8,256]{3,2,1,0:T(8,128)}, u32[]{:S(2)}, u32[]{:S(2)}) collective-permute-start(f32[20,8,8,256]{3,2,1,0:T(8,128)} %get-tuple-element.51), channel_id=1, source_target_pairs={{0,4},{4,8},{8,12},{12,16},{16,20},{20,24},{24,28},{28,32},{32,36}... | collective-permute-start | bytes 3932168 | tf_op jit(solution)/shard_map/ppermute | solution.py:834
  7.6 5.4 %collective-permute-start.1 = (f32[20,8,8,256]{3,2,1,0:T(8,128)}, f32[20,8,8,256]{3,2,1,0:T(8,128)}, u32[]{:S(2)}, u32[]{:S(2)}) collective-permute-start(f32[20,8,8,256]{3,2,1,0:T(8,128)} %get-tuple-element.52), channel_id=1, source_target_pairs={{4,0},{8,4},{12,8},{16,12},{20,16},{24,20},{28,24},{32,28},{36,32}... | collective-permute-start | bytes 3932168 | tf_op jit(solution)/shard_map/ppermute | solution.py:834
  13.0 1.4 %prior_send.1 = f32[32,5,16,128]{3,2,1,0:T(8,128)} custom-call(f32[64,8,512]{2,1,0:T(8,128)S(1)} %copy-done.11), custom_call_target="tpu_custom_call" | custom-call | flops 1048576 | bytes 3145728 | tf_op jit(solution)/shard_map/prior_send/pallas_call | solution.py:238
  14.5 4.7 %all-to-all-start = ((f32[32,5,16,128]{3,2,1,0:T(8,128)}), f32[32,5,16,128]{3,2,1,0:T(8,128)}, u32[]{:S(2)}, u32[]{:S(2)}) async-start(f32[32,5,16,128]{3,2,1,0:T(8,128)} %prior_send.1), calls=%async_computation | async-start | bytes 2621440 | tf_op jit(solution)/shard_map/all_to_all | solution.py:849
  19.1 0.0 copy-start.2
  19.2 1.6 %copy-done.2 = f32[2,64,16,256]{3,2,1,0:T(8,128)S(1)} copy-done((f32[2,64,16,256]{3,2,1,0:T(8,128)S(1)}, f32[2,64,16,256]{3,2,1,0:T(8,128)}, u32[]{:S(2)}) %copy-start.2) | copy-done | bytes 2097176
  20.7 1.2 %copy-done.5 = s32[64,16,256]{2,1,0:T(8,128)S(1)} copy-done((s32[64,16,256]{2,1,0:T(8,128)S(1)}, s32[64,16,256]{2,1,0:T(8,128)}, u32[]{:S(2)}) %copy-start.5) | copy-done | bytes 1048600
  22.0 1.2 %copy-done.6 = f32[64,16,256]{2,1,0:T(8,128)S(1)} copy-done((f32[64,16,256]{2,1,0:T(8,128)S(1)}, f32[64,16,256]{2,1,0:T(8,128)}, u32[]{:S(2)}) %copy-start.6) | copy-done | bytes 1048600
  23.2 3.2 %prepare.1 = (f32[16,8,8,256]{3,2,1,0:T(8,128)S(1)}, f32[16,8,8,256]{3,2,1,0:T(8,128)S(1)}, f32[18,8,8,256]{3,2,1,0:T(8,128)S(1)}, f32[16,8,8,256]{3,2,1,0:T(8,1...) custom-call(s32[64,16,256]{2,1,0:T(8,128)S(1)} %copy-done.5, ...), custom_call_target="tpu_custom_call" | custom-call | flops 4194304 | bytes 8388608 | tf_op jit(solution)/shard_map/prepare/pallas_call | solution.py:207
  26.4 0.0 copy-start
  26.4 25.1 %collective-permute-done.refs_6_.refs_13_.refs_15_ = f32[20,8,8,256]{3,2,1,0:T(8,128)} collective-permute-done((f32[20,8,8,256]{3,2,1,0:T(8,128)}, f32[20,8,8,256]{3,2,1,0:T(8,128)}, u32[]{:S(2)}, u32[]{:S(2)}) %collective-permute-start) | collective-permute-done | bytes 1310752 | tf_op jit(solution)/shard_map/ppermute | solution.py:834
  51.5 7.6 %field_middle.1 = (f32[16,8,8,256]{3,2,1,0:T(8,128)S(1)}, f32[18,8,8,256]{3,2,1,0:T(8,128)S(1)}, f32[2,8,8,256]{3,2,1,0:T(8,128)S(1)}, f32[4,8,8,256]{3,2,1,0:T(...) custom-call(f32[16,8,8,256]{3,2,1,0:T(8,128)S(1)} %get-tuple-element.45.refs_0_.refs_2_, ...), custom_call_target="tpu_custom_call" | custom-call | flops 16777216 | bytes 33554432 | tf_op jit(solution)/shard_map/field_middle/pallas_call | solution.py:809
  59.1 0.1 collective-permute-start.2
  59.2 5.7 %collective-permute-start.3 = (f32[9,8,8,256]{3,2,1,0:T(8,128)}, f32[9,8,8,256]{3,2,1,0:T(8,128)}, u32[]{:S(2)}, u32[]{:S(2)}) collective-permute-start(f32[9,8,8,256]{3,2,1,0:T(8,128)} %get-tuple-element.73), channel_id=1, source_target_pairs={{4,0},{8,4},{12,8},{16,12},{20,16},{24,20},{28,24},{32,28},{36,32}... | collective-permute-start | bytes 1769480 | tf_op jit(solution)/shard_map/ppermute | solution.py:834
  64.9 2.6 %field_triangle.1 = (f32[16,8,8,256]{3,2,1,0:T(8,128)S(1)}, f32[16,8,8,256]{3,2,1,0:T(8,128)S(1)}, f32[18,8,8,256]{3,2,1,0:T(8,128)S(1)}) custom-call(f32[16,8,8,256]{3,2,1,0:T(8,128)S(1)} %get-tuple-element.53.refs_0_, f32[18,8,8,256]{3,2,1,0:T(8,128)S(1)} %get-tuple-element.54.refs_1_, f32[16,8,8,256]{3,2,1,0:T(8,128)S(1)} %get-tuple-element.45.refs_0_.refs_2_, ...), custom_call_target="tpu_custom_call" | custom-call | flops 16777216 | bytes 33554432 | tf_op jit(solution)/shard_map/field_triangle/pallas_call | solution.py:809
  67.5 1.0 copy-done.3
  68.6 1.0 copy-done.7
  69.5 1.0 copy-done.9
  70.5 3.4 %prior_take.1 = (f32[16,8,8,256]{3,2,1,0:T(8,128)S(1)}, f32[4,8,8,256]{3,2,1,0:T(8,128)S(1)}) custom-call(f32[32,5,16,128]{3,2,1,0:T(8,128)} %all-to-all-done.x_hbm), custom_call_target="tpu_custom_call" | custom-call | flops 16777216 | bytes 33554432 | tf_op jit(solution)/shard_map/prior_take/pallas_call | solution.py:292
  73.9 0.6 prior_warmth.1
  74.5 0.0 copy-start.1
  74.5 0.0 copy-start.8
  74.5 0.0 copy-start.10
  74.5 2.7 %first_ready.1 = (f32[18,8,8,256]{3,2,1,0:T(8,128)S(1)}, f32[18,8,8,256]{3,2,1,0:T(8,128)S(1)}, f32[5,18,256]{2,1,0:T(8,128)S(1)}, f32[5,18,256]{2,1,0:T(8,128)S(1)}) custom-call(f32[16,8,8,256]{3,2,1,0:T(8,128)S(1)} %get-tuple-element.59.refs_0_.refs_6_, f32[4,8,8,256]{3,2,1,0:T(8,128)S(1)} %get-tuple-element.60.refs_1_.refs_7_, ...), custom_call_target="tpu_custom_call" | custom-call | flops 16777216 | bytes 33554432 | tf_op jit(solution)/shard_map/first_ready/pallas_call | solution.py:809
  77.3 2.8 %last_ends.1 = (f32[18,8,8,256]{3,2,1,0:T(8,128)S(1)}, f32[18,8,8,256]{3,2,1,0:T(8,128)S(1)}, f32[16,8,8,256]{3,2,1,0:T(8,128)S(1)}, f32[5,18,256]{2,1,0:T(8,128...) custom-call(f32[16,8,8,256]{3,2,1,0:T(8,128)S(1)} %get-tuple-element, ...), custom_call_target="tpu_custom_call" | custom-call | flops 16777216 | bytes 33554432 | tf_op jit(solution)/shard_map/last_ends/pallas_call | solution.py:809
  80.1 3.2 %collective-permute-start.4 = (f32[5,18,256]{2,1,0:T(8,128)S(1)}, f32[5,18,256]{2,1,0:T(8,128)S(1)}, u32[]{:S(2)}, u32[]{:S(2)}) collective-permute-start(f32[5,18,256]{2,1,0:T(8,128)S(1)} %get-tuple-element.84), channel_id=1, source_target_pairs={{0,1},{2,3},{1,0},{3,2},{4,5},{6,7},{5,4},{7,6},{8,9},{10,11},{9,8... | collective-permute-start | bytes 276488 | tf_op jit(solution)/shard_map/ppermute | solution.py:839
  83.3 4.7 %collective-permute-start.5 = (f32[5,18,256]{2,1,0:T(8,128)S(1)}, f32[5,18,256]{2,1,0:T(8,128)S(1)}, u32[]{:S(2)}, u32[]{:S(2)}) collective-permute-start(f32[5,18,256]{2,1,0:T(8,128)S(1)} %get-tuple-element.85), channel_id=1, source_target_pairs={{1,2},{2,1},{5,6},{6,5},{9,10},{10,9},{13,14},{14,13},{17,18},{18,... | collective-permute-start | bytes 276488 | tf_op jit(solution)/shard_map/ppermute | solution.py:839
  88.0 6.8 %field_last.1 = (f32[64,16,256]{2,1,0:T(8,128)}, f32[64,16,256]{2,1,0:T(8,128)}, f32[18,8,8,256]{3,2,1,0:T(8,128)S(1)}, f32[18,8,8,256]{3,2,1,0:T(8,128)S(1)}, f32[16,8,8,256]{3,2,1,0:T(8,128)S(1)}) custom-call(f32[16,8,8,256]{3,2,1,0:T(8,128)S(1)} %get-tuple-element.45.refs_0_.refs_2_, ...), custom_call_target="tpu_custom_call", output_to_operand_aliasing={{2}: (12, {}), {3}: (13, {}), {4}: (14, {})} | custom-call | flops 16777216 | bytes 33554432 | tf_op jit(solution)/shard_map/field_last/pallas_call | solution.py:809
  94.8 2.9 %second_sweep.1 = f32[32,8,8,128]{3,2,1,0:T(8,128)S(1)} custom-call(f32[18,8,8,256]{3,2,1,0:T(8,128)S(1)} %get-tuple-element.80.refs_0_, f32[18,8,8,256]{3,2,1,0:T(8,128)S(1)} %get-tuple-element.81.refs_1_, f32[5,18,256]{2,1,0:T(8,128)S(1)} %get-tuple-element.82.refs_2_, f32[5,18,256]{2,1,0:T(8,128)S(1)} %get-tuple-element.83.refs_3_, ...), custom_call_target="tpu_custom_call" | custom-call | flops 16777216 | bytes 33554432 | tf_op jit(solution)/shard_map/second_sweep/pallas_call | solution.py:809
  97.7 20.8 %all_to_all.10.x_ref = f32[32,8,8,128]{3,2,1,0:T(8,128)S(1)} all-to-all(f32[32,8,8,128]{3,2,1,0:T(8,128)S(1)} %second_sweep.1), channel_id=1, replica_groups=mesh['sec'=32,'ax'=4] {'sec'}, dimensions={0} | all-to-all | bytes 2097152 | tf_op jit(solution)/shard_map/all_to_all | solution.py:889
  118.5 2.3 %temperature_take.1 = f32[64,8,512]{2,1,0:T(8,128)} custom-call(f32[32,8,8,128]{3,2,1,0:T(8,128)S(1)} %all_to_all.10.x_ref), custom_call_target="tpu_custom_call" | custom-call | flops 4194304 | bytes 2097152 | tf_op jit(solution)/shard_map/temperature_take/pallas_call | solution.py:327
  (19 shorter events, 0.0 us)
Async XLA Ops:
  0.6 12.4 %copy-start.11 = (f32[64,8,512]{2,1,0:T(8,128)S(1)}, f32[64,8,512]{2,1,0:T(8,128)}, u32[]{:S(2)}) copy-start(f32[64,8,512]{2,1,0:T(8,128)} %prior_ref.1) | copy-start | bytes 3145732
  5.1 46.4 %collective-permute-start = (f32[20,8,8,256]{3,2,1,0:T(8,128)}, f32[20,8,8,256]{3,2,1,0:T(8,128)}, u32[]{:S(2)}, u32[]{:S(2)}) collective-permute-start(f32[20,8,8,256]{3,2,1,0:T(8,128)} %get-tuple-element.51), channel_id=1, source_target_pairs={{0,4},{4,8},{8,12},{12,16},{16,20},{20,24},{24,28},{28,32},{32,36}... | collective-permute-start | bytes 3932168 | tf_op jit(solution)/shard_map/ppermute | solution.py:834
  7.6 43.8 %collective-permute-start.1 = (f32[20,8,8,256]{3,2,1,0:T(8,128)}, f32[20,8,8,256]{3,2,1,0:T(8,128)}, u32[]{:S(2)}, u32[]{:S(2)}) collective-permute-start(f32[20,8,8,256]{3,2,1,0:T(8,128)} %get-tuple-element.52), channel_id=1, source_target_pairs={{4,0},{8,4},{12,8},{16,12},{20,16},{24,20},{28,24},{32,28},{36,32}... | collective-permute-start | bytes 3932168 | tf_op jit(solution)/shard_map/ppermute | solution.py:834
  14.5 56.1 %all-to-all-start = ((f32[32,5,16,128]{3,2,1,0:T(8,128)}), f32[32,5,16,128]{3,2,1,0:T(8,128)}, u32[]{:S(2)}, u32[]{:S(2)}) async-start(f32[32,5,16,128]{3,2,1,0:T(8,128)} %prior_send.1), calls=%async_computation | async-start | bytes 2621440 | tf_op jit(solution)/shard_map/all_to_all | solution.py:849
  19.1 1.6 %copy-start.2 = (f32[2,64,16,256]{3,2,1,0:T(8,128)S(1)}, f32[2,64,16,256]{3,2,1,0:T(8,128)}, u32[]{:S(2)}) copy-start(f32[2,64,16,256]{3,2,1,0:T(8,128)} %exc_hbm.1) | copy-start | bytes 6291460
  20.7 1.2 %copy-start.5 = (s32[64,16,256]{2,1,0:T(8,128)S(1)}, s32[64,16,256]{2,1,0:T(8,128)}, u32[]{:S(2)}) copy-start(s32[64,16,256]{2,1,0:T(8,128)} %lab_hbm.1) | copy-start | bytes 3145732
  22.0 1.2 %copy-start.6 = (f32[64,16,256]{2,1,0:T(8,128)S(1)}, f32[64,16,256]{2,1,0:T(8,128)}, u32[]{:S(2)}) copy-start(f32[64,16,256]{2,1,0:T(8,128)} %a_hbm.1) | copy-start | bytes 3145732
  26.4 38.5 %copy-start = (f32[16,8,8,256]{3,2,1,0:T(8,128)}, f32[16,8,8,256]{3,2,1,0:T(8,128)S(1)}, u32[]{:S(2)}) copy-start(f32[16,8,8,256]{3,2,1,0:T(8,128)S(1)} %get-tuple-element.47.refs_2_.refs_4_) | copy-start | bytes 3145732
  59.1 18.2 %collective-permute-start.2 = (f32[9,8,8,256]{3,2,1,0:T(8,128)}, f32[9,8,8,256]{3,2,1,0:T(8,128)}, u32[]{:S(2)}, u32[]{:S(2)}) collective-permute-start(f32[9,8,8,256]{3,2,1,0:T(8,128)} %get-tuple-element.72), channel_id=1, source_target_pairs={{0,4},{4,8},{8,12},{12,16},{16,20},{20,24},{24,28},{28,32},{32,36}... | collective-permute-start | bytes 1769480 | tf_op jit(solution)/shard_map/ppermute | solution.py:834
  59.2 18.1 %collective-permute-start.3 = (f32[9,8,8,256]{3,2,1,0:T(8,128)}, f32[9,8,8,256]{3,2,1,0:T(8,128)}, u32[]{:S(2)}, u32[]{:S(2)}) collective-permute-start(f32[9,8,8,256]{3,2,1,0:T(8,128)} %get-tuple-element.73), channel_id=1, source_target_pairs={{4,0},{8,4},{12,8},{16,12},{20,16},{24,20},{28,24},{32,28},{36,32}... | collective-permute-start | bytes 1769480 | tf_op jit(solution)/shard_map/ppermute | solution.py:834
  67.5 1.0 copy-start.3
  68.6 1.0 copy-start.7
  69.5 1.0 copy-start.9
  74.5 2.8 %copy-start.1 = (f32[16,8,8,256]{3,2,1,0:T(8,128)S(1)}, f32[16,8,8,256]{3,2,1,0:T(8,128)}, u32[]{:S(2)}) copy-start(f32[16,8,8,256]{3,2,1,0:T(8,128)} %copy-done) | copy-start | bytes 3145732
  74.5 2.8 %copy-start.4 = (f32[18,8,8,256]{3,2,1,0:T(8,128)S(1)}, f32[18,8,8,256]{3,2,1,0:T(8,128)}, u32[]{:S(2)}) copy-start(f32[18,8,8,256]{3,2,1,0:T(8,128)} %copy-done.3) | copy-start | bytes 3538948
  74.5 2.8 %copy-start.8 = (f32[16,8,8,256]{3,2,1,0:T(8,128)S(1)}, f32[16,8,8,256]{3,2,1,0:T(8,128)}, u32[]{:S(2)}) copy-start(f32[16,8,8,256]{3,2,1,0:T(8,128)} %copy-done.7) | copy-start | bytes 3145732
  74.5 2.8 %copy-start.10 = (f32[16,8,8,256]{3,2,1,0:T(8,128)S(1)}, f32[16,8,8,256]{3,2,1,0:T(8,128)}, u32[]{:S(2)}) copy-start(f32[16,8,8,256]{3,2,1,0:T(8,128)} %copy-done.9) | copy-start | bytes 3145732
  80.1 14.7 %collective-permute-start.4 = (f32[5,18,256]{2,1,0:T(8,128)S(1)}, f32[5,18,256]{2,1,0:T(8,128)S(1)}, u32[]{:S(2)}, u32[]{:S(2)}) collective-permute-start(f32[5,18,256]{2,1,0:T(8,128)S(1)} %get-tuple-element.84), channel_id=1, source_target_pairs={{0,1},{2,3},{1,0},{3,2},{4,5},{6,7},{5,4},{7,6},{8,9},{10,11},{9,8... | collective-permute-start | bytes 276488 | tf_op jit(solution)/shard_map/ppermute | solution.py:839
  83.3 11.5 %collective-permute-start.5 = (f32[5,18,256]{2,1,0:T(8,128)S(1)}, f32[5,18,256]{2,1,0:T(8,128)S(1)}, u32[]{:S(2)}, u32[]{:S(2)}) collective-permute-start(f32[5,18,256]{2,1,0:T(8,128)S(1)} %get-tuple-element.85), channel_id=1, source_target_pairs={{1,2},{2,1},{5,6},{6,5},{9,10},{10,9},{13,14},{14,13},{17,18},{18,... | collective-permute-start | bytes 276488 | tf_op jit(solution)/shard_map/ppermute | solution.py:839
